TPU v7x, 32 devices: a whole 2x2x4 slice. The times are simulated.
32 devices in a mesh: dp: 8 (over z, y), factor: 4 (over x, core).
Axes of the slice: x: 2, y: 2, z: 4, core: 2. Of those that a mesh axis runs over, the one named last changes fastest.
Arguments:
- train_inputs: bfloat16 [64, 8, 64, 320], P('dp'), may hold values from -6 to 6
- train_cotangents: bfloat16 [64, 8, 64, 320], P('dp'), may hold values from -0.26367188 to 0.26367188
- query_inputs: bfloat16 [8, 8, 64, 320], P('dp'), may hold values from -6 to 6
- query_cotangents: bfloat16 [8, 8, 64, 320], P('dp'), may hold values from -0.26367188 to 0.26367188
- timesteps: int32 [64], P('dp'), may hold values from 0 to 999
- input_basis: bfloat16 [2880, 2880], P('dp', 'factor'), may hold values from -0.109375 to 0.109375
- output_basis: bfloat16 [320, 320], replicated, may hold values from -0.3125 to 0.3125
- eigenvalues: float32 [320, 2880], P(None, 'factor'), may hold values from 0.1 to 10
Outputs:
- scores: float32 [64], P('dp')
- query_proj: float32 [320, 2880], P(None, 'factor')
All inputs are finite; a program needn't handle non-finite values.
Results may differ from a plain program's by a relative error of at most 0.0037.
Values may be sent and summed in bfloat16 or wider, within the bound.
No kernel may reach another device: no remote copies, remote signals or barrier semaphores. Data moves between devices by JAX's collectives and lax.ppermute only.
A program may use at most 192 MiB of HBM per device.

v0:
```python
import math

import jax
import jax.numpy as jnp
from jax import lax
from jax.sharding import PartitionSpec as P

damping = 0.01


def patch_matrix(activations):
    batch, rows_count, cols_count, channels = activations.shape
    padded = jnp.pad(activations, ((0, 0), (1, 1), (1, 1), (0, 0)))
    taps = [
        padded[:, row_off : row_off + rows_count, col_off : col_off + cols_count, :]
        for row_off in range(3)
        for col_off in range(3)
    ]
    return jnp.concatenate(taps, axis=-1).reshape(batch * rows_count * cols_count, 9 * channels)


def on_device(
    train_inputs,
    train_cotangents,
    query_inputs,
    query_cotangents,
    timesteps,
    input_basis,
    output_basis,
    eigenvalues,
):
    high = lax.Precision.HIGHEST
    channels = output_basis.shape[0]
    width = input_basis.shape[0] * lax.axis_size("dp")
    batch = train_inputs.shape[0]
    positions = train_inputs.shape[1] * train_inputs.shape[2]
    panel_width = input_basis.shape[1]
    train_patches = patch_matrix(train_inputs)
    query_patches = patch_matrix(query_inputs)
    query_flat = query_cotangents.reshape(-1, channels)
    partial_query = jnp.dot(query_flat.T, query_patches, preferred_element_type=jnp.float32)
    count = query_inputs.shape[0] * lax.axis_size("dp")
    query_grad = lax.psum(partial_query, "dp") / count
    piece = lax.all_gather(input_basis, "dp", axis=0, tiled=True)
    query_part = jnp.dot(query_grad, piece.astype(jnp.float32), precision=high)
    projected = jnp.dot(train_patches, piece, preferred_element_type=jnp.float32)
    basis_out = output_basis.astype(jnp.float32)
    query_proj = jnp.dot(basis_out.T, query_part, precision=high) / (eigenvalues + damping)
    rotated = jnp.dot(
        train_cotangents.reshape(-1, channels), output_basis, preferred_element_type=jnp.float32
    )
    rotated = rotated.astype(jnp.bfloat16).reshape(batch, positions, channels)
    projected = projected.astype(jnp.bfloat16).reshape(batch, positions, panel_width)
    train_proj = jnp.einsum("bpc,bpk->bck", rotated, projected, preferred_element_type=jnp.float32)
    partial_scores = jnp.einsum("bck,ck->b", train_proj, query_proj, precision=high)
    raw_scores = lax.psum(partial_scores, "factor")
    phase = (timesteps.astype(jnp.float32) / 1000.0 + 0.008) / 1.008 * (math.pi / 2)
    weight = jnp.sin(phase)
    scores = raw_scores * weight / math.sqrt(channels * width)
    return (scores, query_proj)


def solution(mesh):
    in_specs = (
        P("dp", None, None, None),
        P("dp", None, None, None),
        P("dp", None, None, None),
        P("dp", None, None, None),
        P("dp"),
        P("dp", "factor"),
        P(),
        P(None, "factor"),
    )
    out_specs = (P("dp"), P(None, "factor"))
    return jax.shard_map(
        on_device, mesh=mesh, in_specs=in_specs, out_specs=out_specs, check_vma=False
    )
```

profile of v0, /device:TPU:0, one launch (start us, length us, event | category | flops | bytes accessed | tf_op | source)
XLA Modules:
  0.0 306.1 jit_solution(6350234049092365632)
XLA Ops:
  7.2 0.0 copy-start
  7.2 0.0 all-gather.2.cloned.1.call-start
  7.2 0.7 all-gather.2.cloned.1.call-update
  7.9 0.0 all-reduce.4.cloned.1.call-start
  8.0 4.4 %pad_slice_fusion.8 = (bf16[1,8,64,320]{3,2,1,0:T(8,128)(2,1)S(1)}, bf16[1,8,64,320]{3,2,1,0:T(8,128)(2,1)}, bf16[1,8,64,320]{3,2,1,0:T(8,128)(2,1)}, bf16[1,8,6...) fusion(bf16[1,8,64,320]{3,2,1,0:T(8,128)(2,1)} %param.10), kind=kLoop, calls=%fused_computation.26 | loop fusion | bytes 2949120 | tf_op jit(solution)/shard_map/slice | solution.py:15
  12.4 6.1 %concatenate.7 = bf16[1,8,64,2880]{3,2,1,0:T(8,128)(2,1)} concatenate(bf16[1,8,64,320]{3,2,1,0:T(8,128)(2,1)} %get-tuple-element.17, bf16[1,8,64,320]{3,2,1,0:T(8,128)(2,1)} %get-tuple-element.11, bf16[1,8,64,320]{3,2,1,0:T(8,128)(2,1)} %get-tuple-element.12, bf16[1,8,64,320]{3,2,1,0:T(8,128)(2,1)} %get-tuple-element.13, bf16[1,8,64,320]{3,2,1,0:T(8,128)(2,1)} %param.10, ...), dimensions={3} | concatenate | bytes 5898240 | tf_op jit(solution)/shard_map/concatenate | solution.py:19
  18.5 5.9 %convolution_bitcast_fusion = f32[320,2880]{0,1:T(8,128)} fusion(bf16[1,8,64,2880]{3,2,1,0:T(8,128)(2,1)} %concatenate.7, bf16[1,8,64,320]{3,2,1,0:T(8,128)(2,1)} %param.11), kind=kOutput, calls=%fused_computation.15 | convolution fusion | flops 943718400 | bytes 6963200 | tf_op jit(solution)/shard_map/dot_general | solution.py:41
  24.4 0.0 all-reduce.4.cloned.1.call-update
  24.4 0.0 copy-start.5
  24.4 20.5 %pad_slice_fusion = (bf16[8,8,64,320]{3,2,1,0:T(8,128)(2,1)}, bf16[8,8,64,320]{3,2,1,0:T(8,128)(2,1)}, bf16[8,8,64,320]{3,2,1,0:T(8,128)(2,1)}, bf16[8,8,64,320]...) fusion(bf16[8,8,64,320]{3,2,1,0:T(8,128)(2,1)} %param.8), kind=kLoop, calls=%fused_computation.7 | loop fusion | bytes 23592960 | tf_op jit(solution)/shard_map/slice | solution.py:15
  44.9 0.0 copy-done
  44.9 0.0 copy-done.5
  44.9 3.1 %convolution_convert_fusion.1 = bf16[4096,320]{0,1:T(8,128)(2,1)} fusion(bf16[4096,320]{1,0:T(8,128)(2,1)S(1)} %bitcast.34, bf16[320,320]{1,0:T(8,128)(2,1)S(1)} %copy-done.5), kind=kOutput, calls=%fused_computation.6 | convolution fusion | flops 840171520 | bytes 5447680 | tf_op jit(solution)/shard_map/dot_general | solution.py:49
  48.0 37.5 %concatenate.6 = bf16[8,8,64,2880]{3,2,1,0:T(8,128)(2,1)} concatenate(bf16[8,8,64,320]{3,2,1,0:T(8,128)(2,1)} %get-tuple-element.9, bf16[8,8,64,320]{3,2,1,0:T(8,128)(2,1)} %get-tuple-element.3, bf16[8,8,64,320]{3,2,1,0:T(8,128)(2,1)} %get-tuple-element.4, bf16[8,8,64,320]{3,2,1,0:T(8,128)(2,1)} %get-tuple-element.5, bf16[8,8,64,320]{3,2,1,0:T(8,128)(2,1)} %param.8, ...), dimensions={3} | concatenate | bytes 47185920 | tf_op jit(solution)/shard_map/concatenate | solution.py:19
  85.4 3.7 %all-gather.2.cloned.1.call-done = bf16[2880,720]{1,0:T(8,128)(2,1)} async-done(((bf16[360,720]{1,0:T(8,128)(2,1)}), bf16[2880,720]{1,0:T(8,128)(2,1)}) %all-gather.2.cloned.1.call-update) | async-done | bytes 4147216 | tf_op jit(solution)/shard_map/all_gather | solution.py:44
  89.2 0.0 copy-start.3
  89.2 23.5 %convolution_convert_fusion = bf16[4096,720]{0,1:T(8,128)(2,1)S(1)} fusion(bf16[4096,2880]{1,0:T(8,128)(2,1)} %bitcast.35, bf16[2880,720]{1,0:T(8,128)(2,1)} %all-gather.2.cloned.1.call-done), kind=kOutput, calls=%fused_computation.2 | convolution fusion | flops 16989880320 | bytes 33638400 | tf_op jit(solution)/shard_map/dot_general | solution.py:46
  112.7 0.0 copy-done.3
  112.7 5.3 %fusion.2 = f32[8,320,720]{2,1,0:T(8,128)} fusion(bf16[90,8,8,512]{3,2,1,0:T(8,128)(2,1)S(1)} %bitcast.37, bf16[40,8,8,512]{3,2,1,0:T(8,128)(2,1)S(1)} %bitcast.36), kind=kOutput, calls=%fused_computation.3 | convolution fusion | flops 1887436800 | bytes 15892480 | tf_op jit(solution)/shard_map/bpc,bpk->bck/dot_general | solution.py:54
  118.0 0.0 copy-start.6
  118.0 135.0 %all-reduce.4.cloned.1.call-done = f32[320,2880]{0,1:T(8,128)} async-done(((f32[320,2880]{0,1:T(8,128)}), f32[320,2880]{0,1:T(8,128)}) %all-reduce.4.cloned.1.call-update) | async-done | bytes 3686416 | tf_op jit(solution)/shard_map/psum | solution.py:43
  253.0 0.0 copy-start.2
  253.0 9.4 %fusion.5 = f32[320,720]{1,0:T(8,128)S(1)} fusion(bf16[2880,720]{1,0:T(8,128)(2,1)} %all-gather.2.cloned.1.call-done, f32[320,2880]{0,1:T(8,128)} %all-reduce.4.cloned.1.call-done), kind=kOutput, calls=%fused_computation.16 | convolution fusion | flops 7963545600 | bytes 8755200 | tf_op jit(solution)/shard_map/dot_general | solution.py:45
  262.4 0.0 copy-done.6
  262.4 1.0 fusion.11
  263.4 0.0 copy-start.4
  263.4 0.0 copy-start.1
  263.4 0.9 copy-done.4
  264.3 0.0 copy-done.2
  264.3 0.0 copy-start.7
  264.3 27.5 %fusion.12 = f32[8]{0:T(128)S(1)} fusion(f32[8,320,720]{2,1,0:T(8,128)S(1)} %copy-done.2, f32[320,720,1]{1,0,2:T(8,128)S(1)} %bitcast.38), kind=kOutput, calls=%fused_computation.24 | convolution fusion | flops 22118400 | bytes 8294432 | tf_op jit(solution)/shard_map/bck,ck->b/dot_general | solution.py:55
  291.8 6.8 %psum.15 = f32[8]{0:T(128)S(1)} all-reduce(f32[8]{0:T(128)S(1)} %fusion.12), channel_id=1, replica_groups=mesh['dp'=8,'factor'=4] {'factor'}, use_global_device_ids=true, to_apply=%region_1.2 | all-reduce | flops 8 | bytes 64 | tf_op jit(solution)/shard_map/psum | solution.py:56
  298.7 0.0 copy-done.7
  298.7 0.6 multiply_multiply_fusion
  299.2 0.0 copy-done.1
Async XLA Ops:
  7.2 37.7 %copy-start = (bf16[8,8,64,320]{3,2,1,0:T(8,128)(2,1)S(1)}, bf16[8,8,64,320]{3,2,1,0:T(8,128)(2,1)}, u32[]{:S(2)}) copy-start(bf16[8,8,64,320]{3,2,1,0:T(8,128)(2,1)} %param.9) | copy-start | bytes 7864324
  7.2 82.0 %all-gather.2.cloned.1.call-start = ((), (), s32[]{:S(2)}) async-start(), calls=%async_computation | async-start | bytes 4976640 | tf_op jit(solution)/shard_map/all_gather | solution.py:44
  7.9 245.1 %all-reduce.4.cloned.1.call-start = ((), (), s32[]{:S(2)}) async-start(), calls=%async_computation.1 | async-start | bytes 8847360 | tf_op jit(solution)/shard_map/psum | solution.py:43
  24.4 20.5 %copy-start.5 = (bf16[320,320]{1,0:T(8,128)(2,1)S(1)}, bf16[320,320]{1,0:T(8,128)(2,1)}, u32[]{:S(2)}) copy-start(bf16[320,320]{1,0:T(8,128)(2,1)} %param.14) | copy-start | bytes 614404
  89.2 23.5 %copy-start.3 = (bf16[4096,320]{0,1:T(8,128)(2,1)S(1)}, bf16[4096,320]{0,1:T(8,128)(2,1)}, u32[]{:S(2)}) copy-start(bf16[4096,320]{0,1:T(8,128)(2,1)} %convolution_convert_fusion.1) | copy-start | bytes 7864324
  118.0 144.4 %copy-start.6 = (f32[320,720]{1,0:T(8,128)S(1)}, f32[320,720]{1,0:T(8,128)}, u32[]{:S(2)}) copy-start(f32[320,720]{1,0:T(8,128)} %param.15) | copy-start | bytes 2764804
  253.0 11.4 %copy-start.2 = (f32[8,320,720]{2,1,0:T(8,128)S(1)}, f32[8,320,720]{2,1,0:T(8,128)}, u32[]{:S(2)}) copy-start(f32[8,320,720]{2,1,0:T(8,128)} %fusion.2) | copy-start | bytes 22118404
  263.4 0.9 copy-start.4
  263.4 35.8 %copy-start.1 = (bf16[8,8,64,320]{3,2,1,0:T(8,128)(2,1)S(1)}, bf16[8,8,64,320]{3,2,1,0:T(8,128)(2,1)}, u32[]{:S(2)}) copy-start(bf16[8,8,64,320]{3,2,1,0:T(8,128)(2,1)} %param.9) | copy-start | bytes 7864324
  264.3 34.3 %copy-start.7 = (s32[8]{0:T(128)S(1)}, s32[8]{0:T(128)}, u32[]{:S(2)}) copy-start(s32[8]{0:T(128)} %param.12) | copy-start | bytes 100
Sparse Core Ops, SparseCore 0:
  10.2 78.9 all-gather.1
  92.8 160.1 all-reduce.3
where the time goes:
time: 309 us; the launch traced here: 306 us
  waiting for transfers between devices  139 us (45%)
  matrix products  75.7 us (24%)
  local copies, waits for them, and re-layouts  69.4 us (22%)
  between operations  14.1 us (5%)
  blocking collectives  6.82 us (2%)
    psum x1, waiting for transfers between devices, on_device(): query_grad = lax.psum(partial_query, 'dp') / count  135 us
    concatenate x2, local copies, waits for them, and re-layouts, patch_matrix(): jnp.concatenate(taps, axis=-1)  43.6 us
    dot_general x1, matrix products, on_device(): jnp.einsum('bck,ck->b', train_proj, query_proj, precision=high)  27.5 us
    slice x2, local copies, waits for them, and re-layouts, patch_matrix(): padded[:, row_off:row_off + rows_count, col_off:col_off + cols_count, :]  24.9 us
    dot_general x1, matrix products, on_device(): jnp.dot(train_patches, piece, preferred_element_type=jnp.float32)  23.5 us
    dot_general x1, matrix products, on_device(): query_part = jnp.dot(query_grad, piece.astype(jnp.float32), precision=high)  9.37 us
    psum x1, blocking collectives, on_device(): raw_scores = lax.psum(partial_scores, 'factor')  6.82 us
  transfers between devices with their start and end apart: 2, of which 2 were waited for; matrix products, arithmetic and copies ran while one was open for 35% of the time, Pallas kernels for 0%

commit v1 on v0

v1 whole, which is shorter than its diff:
```python
import functools
import math

import jax
import jax.numpy as jnp
from jax import lax
from jax.experimental import pallas as pl
from jax.experimental.pallas import tpu as pltpu
from jax.sharding import PartitionSpec as P

damping = 0.01
bf16 = jnp.bfloat16
f32 = jnp.float32
first_dims = (((0,), (0,)), ((), ()))
mib = 2**20


def patch_matrix(activations):
    rows, cols, channels = activations.shape
    edge = jnp.zeros((rows, 1, channels), activations.dtype)
    before = jnp.concatenate([edge, activations[:, :-1]], axis=1)
    after = jnp.concatenate([activations[:, 1:], edge], axis=1)
    blank = jnp.zeros((cols, channels), activations.dtype)
    shifted = [
        jnp.concatenate([blank, part.reshape(rows * cols, channels), blank], axis=0)
        for part in (before, activations, after)
    ]
    taps = [
        shifted[col_off][row_off * cols : (row_off + rows) * cols]
        for row_off in range(3)
        for col_off in range(3)
    ]
    return jnp.concatenate(taps, axis=1)


def query_kernel(x_ref, c_ref, basis_ref, out_ref, *, scale):
    queries, rows, cols, channels = x_ref.shape
    blocks, own_rows, wide = out_ref.shape
    depth = 9 * channels // blocks
    total = jnp.zeros((own_rows, 9 * channels), f32)
    for query in range(queries):
        cot = c_ref[query].reshape(rows * cols, channels)
        rotated = jnp.dot(cot, basis_ref[...], preferred_element_type=f32)
        upper = rotated.astype(bf16)
        lower = (rotated - upper.astype(f32)).astype(bf16)
        patches = patch_matrix(x_ref[query])
        total += lax.dot_general(upper, patches, first_dims, preferred_element_type=f32)
        total += lax.dot_general(lower, patches, first_dims, preferred_element_type=f32)
    total = total * scale
    largest = jnp.max(jnp.max(jnp.abs(total), axis=1, keepdims=True), axis=0, keepdims=True)
    power = jnp.ceil(jnp.log(jnp.maximum(largest, 1e-30)) * (1 / math.log(2.0))) - 14.0
    total = total * jnp.exp2(-power)
    for block in range(blocks):
        out_ref[block, :, :depth] = total[:, block * depth : (block + 1) * depth]
        out_ref[block, :, depth:] = jnp.broadcast_to(power, (own_rows, wide - depth))


def query_partial(x, cot, basis, blocks, scale):
    channels = x.shape[-1]
    depth = 9 * channels // blocks
    wide = depth + 128 - depth % 128
    return pl.pallas_call(
        functools.partial(query_kernel, scale=scale),
        out_shape=jax.ShapeDtypeStruct((blocks, basis.shape[1], wide), f32),
        compiler_params=pltpu.CompilerParams(vmem_limit_bytes=32 * mib),
        cost_estimate=pl.CostEstimate(
            flops=4 * x.size * 9 * basis.shape[1], bytes_accessed=4 * x.size, transcendentals=0
        ),
        name="query_gradient",
    )(x, cot, basis)


def train_kernel(x_ref, c_ref, basis_ref, out_ref):
    rows, cols, channels = x_ref.shape[1:]
    blocks, _, _, depth = out_ref.shape
    cot = c_ref[0].reshape(rows * cols, channels)
    rotated = jnp.dot(cot, basis_ref[...], preferred_element_type=f32).astype(bf16)
    grad = lax.dot_general(
        rotated, patch_matrix(x_ref[0]), first_dims, preferred_element_type=f32
    ).astype(bf16)
    for block in range(blocks):
        out_ref[block, 0] = grad[:, block * depth : (block + 1) * depth]


def train_gradients(x, cot, basis, blocks):
    count, rows, cols, channels = x.shape
    depth = 9 * channels // blocks
    spec = pl.BlockSpec((1, rows, cols, channels), lambda i: (i, 0, 0, 0))
    return pl.pallas_call(
        train_kernel,
        grid=(count,),
        in_specs=[spec, spec, pl.BlockSpec((channels, channels), lambda i: (0, 0))],
        out_specs=pl.BlockSpec((blocks, 1, channels, depth), lambda i: (0, i, 0, 0)),
        out_shape=jax.ShapeDtypeStruct((blocks, count, channels, depth), bf16),
        compiler_params=pltpu.CompilerParams(vmem_limit_bytes=32 * mib),
        cost_estimate=pl.CostEstimate(
            flops=2 * x.size * 9 * channels, bytes_accessed=4 * x.size, transcendentals=0
        ),
        name="train_gradients",
    )(x, cot, basis)


def place_pair(scratch, slot, side, mine, other):
    depth = mine.shape[0]

    @pl.when(side == 0)
    def _():
        scratch[slot, :depth] = mine[...]
        scratch[slot, depth:] = other[...]

    @pl.when(side == 1)
    def _():
        scratch[slot, :depth] = other[...]
        scratch[slot, depth:] = mine[...]


def early_kernel(where, *refs, slots):
    grads, pieces, out_ref, basis = refs[:slots], refs[slots : 3 * slots], refs[-2], refs[-1]

    @pl.when(pl.program_id(0) == 0)
    def _():
        for slot in range(slots):
            place_pair(basis, slot, where[0], pieces[2 * slot], pieces[2 * slot + 1])

    count, channels, depth = grads[0].shape[1:]
    total = jnp.zeros((count * channels, out_ref.shape[-1]), f32)
    for slot in range(slots):
        total += jnp.dot(
            grads[slot][0].reshape(count * channels, depth),
            basis[slot],
            preferred_element_type=f32,
        )
    out_ref[...] = total.reshape(out_ref.shape)


def early_products(where, grads, pieces, step):
    blocks, count, channels, depth = grads.shape
    slots = len(pieces) // 2
    half, width = pieces[0].shape
    grad_specs = [
        pl.BlockSpec((1, step, channels, depth), lambda i, at, slot=slot: (at[1 + slot], i, 0, 0))
        for slot in range(slots)
    ]
    piece_specs = [pl.BlockSpec((half, width), lambda i, at: (0, 0))] * (2 * slots)
    return pl.pallas_call(
        functools.partial(early_kernel, slots=slots),
        grid_spec=pltpu.PrefetchScalarGridSpec(
            num_scalar_prefetch=1,
            grid=(count // step,),
            in_specs=grad_specs + piece_specs,
            out_specs=pl.BlockSpec((step, channels, width), lambda i, at: (i, 0, 0)),
            scratch_shapes=[pltpu.VMEM((slots, 2 * half, width), bf16)],
        ),
        out_shape=jax.ShapeDtypeStruct((count, channels, width), f32),
        compiler_params=pltpu.CompilerParams(vmem_limit_bytes=48 * mib),
        cost_estimate=pl.CostEstimate(
            flops=2 * slots * count * channels * depth * width,
            bytes_accessed=4 * count * channels * width,
            transcendentals=0,
        ),
        name="early_products",
    )(where, *([grads] * slots), *pieces)


def final_kernel(where, *refs, blocks, parts):
    grad_ref, early_ref, eigen_ref = refs[:3]
    query_refs = refs[3 : 3 + parts]
    pieces = refs[3 + parts : 3 + parts + 2 * blocks]
    score_ref, proj_ref, basis = refs[-3:]

    @pl.when(pl.program_id(0) == 0)
    def _():
        for slot in range(blocks):
            place_pair(basis, slot, where[0], pieces[2 * slot], pieces[2 * slot + 1])
        for part in range(parts):
            at = where[1 + blocks + part]
            total = jnp.dot(query_refs[part][0], basis[0], preferred_element_type=f32)
            for slot in range(1, blocks):
                total += jnp.dot(query_refs[part][slot], basis[slot], preferred_element_type=f32)
            proj_ref[at] = total / (eigen_ref[at] + damping)

    step, channels, depth = grad_ref.shape[1:]
    width = basis.shape[-1]
    proj = proj_ref[...].reshape(channels, width)
    late = jnp.dot(
        grad_ref[0].reshape(step * channels, depth), basis[blocks - 1], preferred_element_type=f32
    ).reshape(step, channels, width)
    for item in range(step):
        sums = jnp.sum((early_ref[item] + late[item]) * proj, axis=0, keepdims=True)
        total = jnp.sum(sums, axis=1, keepdims=True)
        score_ref[0, item : item + 1, :] = jnp.broadcast_to(total, (1, score_ref.shape[2]))


def final_products(where, grads, early, eigen, queries, pieces, step):
    blocks, count, channels, depth = grads.shape
    parts, own_rows, width = eigen.shape
    half = pieces[0].shape[0]
    whole3 = pl.BlockSpec((parts, own_rows, width), lambda i, at: (0, 0, 0))
    return pl.pallas_call(
        functools.partial(final_kernel, blocks=blocks, parts=parts),
        grid_spec=pltpu.PrefetchScalarGridSpec(
            num_scalar_prefetch=1,
            grid=(count // step,),
            in_specs=[
                pl.BlockSpec((1, step, channels, depth), lambda i, at: (at[blocks], i, 0, 0)),
                pl.BlockSpec((step, channels, width), lambda i, at: (i, 0, 0)),
                whole3,
            ]
            + [pl.BlockSpec((blocks, own_rows, depth), lambda i, at: (0, 0, 0))] * parts
            + [pl.BlockSpec((half, width), lambda i, at: (0, 0))] * (2 * blocks),
            out_specs=[
                pl.BlockSpec((1, step, 128), lambda i, at: (i, 0, 0)),
                whole3,
            ],
            scratch_shapes=[pltpu.VMEM((blocks, 2 * half, width), bf16)],
        ),
        out_shape=[
            jax.ShapeDtypeStruct((count // step, step, 128), f32),
            jax.ShapeDtypeStruct((parts, own_rows, width), f32),
        ],
        compiler_params=pltpu.CompilerParams(vmem_limit_bytes=48 * mib),
        cost_estimate=pl.CostEstimate(
            flops=2 * (count + blocks) * channels * depth * width,
            bytes_accessed=4 * count * channels * width,
            transcendentals=0,
        ),
        name="final_products",
    )(where, grads, early, eigen, *queries, *pieces)


def on_device(
    train_inputs,
    train_cotangents,
    query_inputs,
    query_cotangents,
    timesteps,
    input_basis,
    output_basis,
    eigenvalues,
):
    channels = output_basis.shape[0]
    sides = 2
    shards = lax.axis_size("dp")
    rings = shards // sides
    parts = lax.axis_size("factor")
    width = input_basis.shape[0] * shards
    own_rows = channels // parts
    depth = width // rings
    here = lax.axis_index("dp")
    ring, side = here // sides, here % sides
    part = lax.axis_index("factor")

    def along(array, shift):
        pairs = [
            (r * sides + s, (r + shift) % rings * sides + s)
            for r in range(rings)
            for s in range(sides)
        ]
        return lax.ppermute(array, "dp", pairs)

    def across(array):
        return lax.ppermute(array, "dp", [(d, d ^ 1) for d in range(shards)])

    def flip(array, bit):
        return lax.ppermute(array, "factor", [(p, p ^ bit) for p in range(parts)])

    forward = rings // 2
    backward = rings - 1 - forward
    columns = [input_basis]
    for _ in range(forward):
        columns.append(along(columns[-1], 1))
    last = input_basis
    back = []
    for _ in range(backward):
        last = along(last, -1)
        back.append(last)
    order = [0] + [s for pair in zip(range(1, forward + 1), range(rings - 1, forward, -1)) for s in pair]
    order += [s for s in range(1, rings) if s not in order]
    by_shift = {s: columns[s] for s in range(forward + 1)}
    for s, piece in enumerate(back):
        by_shift[rings - 1 - s] = piece
    pieces = []
    for s in order:
        pieces += [by_shift[s], across(by_shift[s])]

    count = query_inputs.shape[0] * shards
    own_basis = lax.dynamic_slice_in_dim(output_basis, part * own_rows, own_rows, axis=1)
    partial = query_partial(query_inputs, query_cotangents, own_basis, rings, 1.0 / count)
    sent = partial.astype(jnp.float16)

    def block_of(array, shift):
        return lax.dynamic_index_in_dim(array, (ring + shift) % rings, 0, keepdims=False)

    arrived = [block_of(sent, 0)] + [along(block_of(sent, s), s) for s in range(1, rings)]
    total = sum(
        item[:, :depth].astype(f32) * jnp.exp2(item[:, depth : depth + 1].astype(f32))
        for item in arrived
    )
    total = (total + across(total)).astype(bf16)
    stack = jnp.stack([total] + [along(total, s) if s else total for s in order[1:]])
    queries, spots = [stack], [0]
    bit = parts // 2
    while bit:
        queries = queries + [flip(item, bit) for item in queries]
        spots = spots + [spot ^ bit for spot in spots]
        bit //= 2

    grads = train_gradients(train_inputs, train_cotangents, output_basis, rings)
    where = jnp.stack(
        [side] + [(ring - s) % rings for s in order] + [part ^ spot for spot in spots]
    ).astype(jnp.int32)
    batch = train_inputs.shape[0]
    step = 2 if batch % 2 == 0 else 1
    early = early_products(where, grads, pieces[:-2], step)
    eigen = eigenvalues.reshape(parts, own_rows, eigenvalues.shape[1])
    sums, proj = final_products(where, grads, early, eigen, queries, pieces, step)
    query_proj = proj.reshape(eigenvalues.shape)
    partial_scores = sums[:, :, 0].reshape(batch)
    raw_scores = partial_scores
    bit = parts // 2
    while bit:
        raw_scores = raw_scores + flip(raw_scores, bit)
        bit //= 2
    phase = (timesteps.astype(f32) / 1000.0 + 0.008) / 1.008 * (math.pi / 2)
    weight = jnp.sin(phase)
    scores = raw_scores * weight / math.sqrt(channels * width)
    return (scores, query_proj)


def solution(mesh):
    in_specs = (
        P("dp", None, None, None),
        P("dp", None, None, None),
        P("dp", None, None, None),
        P("dp", None, None, None),
        P("dp"),
        P("dp", "factor"),
        P(),
        P(None, "factor"),
    )
    out_specs = (P("dp"), P(None, "factor"))
    return jax.shard_map(
        on_device, mesh=mesh, in_specs=in_specs, out_specs=out_specs, check_vma=False
    )
```

time: 309 us -> 129 us (0.42)
  waiting for transfers between devices: 139 us -> 44.6 us
  matrix products: 75.7 us -> 0 us
  local copies, waits for them, and re-layouts: 69.4 us -> 14.4 us
  Pallas kernels: 0 us -> 42 us
  starting transfers between devices: 0.08 us -> 25.5 us
  between operations: 14.1 us -> 0.89 us
  blocking collectives: 6.82 us -> 0 us
    psum x1 -> x0, waiting for transfers between devices: 135 us -> none  [on_device(): query_grad = lax.psum(partial_query, 'dp') / count]
    dot_general x7 -> x0, matrix products: 75.7 us -> none  [the longest x1 27.5 us: on_device(): jnp.einsum('bck,ck->b', train_proj, query_proj, precision=high)]
    ppermute x0 -> x19, waiting for transfers between devices: none -> 44.6 us  [the longest x9 34 us: along(): return lax.ppermute(array, 'dp', pairs)]
    concatenate x2 -> x0, local copies, waits for them, and re-layouts: 43.6 us -> none  [patch_matrix(): jnp.concatenate(taps, axis=-1)]
    pallas_call x0 -> x4, Pallas kernels: none -> 42 us  [the longest x1 14.4 us: train_gradients(): pl.pallas_call(train_kernel, grid=(count,), in_specs=[spec, spec, pl.Bloc...]
    ppermute x0 -> x19, starting transfers between devices: none -> 25.5 us  [the longest x9 17.3 us: along(): return lax.ppermute(array, 'dp', pairs)]
    slice x2 -> x1, local copies, waits for them, and re-layouts: 24.9 us -> 0.09 us  [on_device(): partial_scores = sums[:, :, 0].reshape(batch)]
    unnamed x16 -> x18, local copies, waits for them, and re-layouts: 0.97 us -> 13 us
  transfers between devices with their start and end apart: 2 -> 19, of which waited for: 2 -> 8; matrix products, arithmetic and copies ran while one was open for 35% -> 1% of each run, Pallas kernels for 0% -> 22%
where the time goes in v1:
time: 129 us
  waiting for transfers between devices  44.6 us (35%)
  Pallas kernels  42 us (33%)
  starting transfers between devices  25.5 us (20%)
  local copies, waits for them, and re-layouts  14.4 us (11%)
  other arithmetic  1.63 us (1%)
    ppermute x9, waiting for transfers between devices, along(): return lax.ppermute(array, 'dp', pairs)  34 us
    ppermute x9, starting transfers between devices, along(): return lax.ppermute(array, 'dp', pairs)  17.3 us
    pallas_call x1, Pallas kernels, train_gradients(): pl.pallas_call(train_kernel, grid=(count,), in_specs=[spec, spec, pl.Bloc...  14.4 us
    pallas_call x1, Pallas kernels, early_products(): pl.pallas_call(functools.partial(early_kernel, slots=slots), grid_spec=pl...  13.9 us
    unnamed x18, local copies, waits for them, and re-layouts  13 us
    pallas_call x1, Pallas kernels, final_products(): pl.pallas_call(functools.partial(final_kernel, blocks=blocks, parts=parts...  11.8 us
    ppermute x5, waiting for transfers between devices, across(): return lax.ppermute(array, 'dp', [(d, d ^ 1) for d in range(shards)])  7.41 us
    ppermute x5, starting transfers between devices, across(): return lax.ppermute(array, 'dp', [(d, d ^ 1) for d in range(shards)])  4.63 us
  transfers between devices with their start and end apart: 19, of which 8 were waited for; matrix products, arithmetic and copies ran while one was open for 1% of the time, Pallas kernels for 22%

profile of v1, /device:TPU:0, one launch (start us, length us, event | category | flops | bytes accessed | tf_op | source)
XLA Modules:
  0.0 129.0 jit_solution(7143737578272040736)
XLA Ops:
  0.7 1.0 constant_dynamic-slice_fusion.basis_ref
  1.7 0.0 copy-start.2
  1.8 1.0 copy-done.2
  2.7 1.0 copy-done.3
  3.7 1.9 %query_gradient.1 = f32[4,80,768]{2,1,0:T(8,128)S(1)} custom-call(bf16[1,8,64,320]{3,2,1,0:T(8,128)(2,1)S(1)} %copy-done.2, bf16[1,8,64,320]{3,2,1,0:T(8,128)(2,1)S(1)} %copy-done.3, bf16[320,80]{1,0:T(8,128)(2,1)S(1)} %constant_dynamic-slice_fusion.basis_ref), custom_call_target="tpu_custom_call" | custom-call | flops 471859200 | bytes 655360 | tf_op jit(solution)/shard_map/query_gradient/pallas_call | solution.py:62
  5.6 0.1 convert_element_type.33
  5.7 0.1 dynamic-slice_bitcast_fusion.3
  5.8 5.1 %collective-permute-start.7 = (f16[80,768]{1,0:T(8,128)(2,1)S(1)}, f16[80,768]{1,0:T(8,128)(2,1)S(1)}, u32[]{:S(2)}, u32[]{:S(2)}) collective-permute-start(f16[80,768]{1,0:T(8,128)(2,1)S(1)} %get-tuple-element.7), channel_id=1, source_target_pairs={{0,24},{4,28},{8,0},{12,4},{16,8},{20,12},{24,16},{28,20},{1,25},{... | collective-permute-start | bytes 368648 | tf_op jit(solution)/shard_map/ppermute | solution.py:259
  10.9 0.0 collective-permute-start.6
  10.9 1.0 collective-permute-start.5
  11.9 0.2 exponential_reduce_fusion.3
  12.1 2.5 %collective-permute-done.7 = f16[80,768]{1,0:T(8,128)(2,1)S(1)} collective-permute-done((f16[80,768]{1,0:T(8,128)(2,1)S(1)}, f16[80,768]{1,0:T(8,128)(2,1)S(1)}, u32[]{:S(2)}, u32[]{:S(2)}) %collective-permute-start.7) | collective-permute-done | bytes 122912 | tf_op jit(solution)/shard_map/ppermute | solution.py:259
  14.6 0.2 exponential_reduce_fusion
  14.8 6.7 %collective-permute-done.6 = f16[80,768]{1,0:T(8,128)(2,1)S(1)} collective-permute-done((f16[80,768]{1,0:T(8,128)(2,1)S(1)}, f16[80,768]{1,0:T(8,128)(2,1)S(1)}, u32[]{:S(2)}, u32[]{:S(2)}) %collective-permute-start.6) | collective-permute-done | bytes 122912 | tf_op jit(solution)/shard_map/ppermute | solution.py:259
  21.5 0.2 exponential_reduce_fusion.1
  21.7 0.0 collective-permute-done.5
  21.7 0.2 exponential_reduce_fusion.2
  21.9 0.2 multiply_add_fusion
  22.1 1.6 %collective-permute-start.8 = (f32[80,720]{1,0:T(8,128)S(1)}, f32[80,720]{1,0:T(8,128)S(1)}, u32[]{:S(2)}, u32[]{:S(2)}) collective-permute-start(f32[80,720]{1,0:T(8,128)S(1)} %multiply_add_fusion), channel_id=1, source_target_pairs={{0,4},{4,0},{8,12},{12,8},{16,20},{20,16},{24,28},{28,24},{1,5},{5... | collective-permute-start | bytes 691208 | tf_op jit(solution)/shard_map/ppermute | solution.py:262
  23.7 0.4 collective-permute-start.1
  24.1 3.4 %collective-permute-start.3 = (bf16[360,720]{1,0:T(8,128)(2,1)}, bf16[360,720]{1,0:T(8,128)(2,1)S(1)}, u32[]{:S(2)}, u32[]{:S(2)}) collective-permute-start(bf16[360,720]{1,0:T(8,128)(2,1)} %refs_7_.1), channel_id=1, source_target_pairs={{0,24},{4,28},{8,0},{12,4},{16,8},{20,12},{24,16},{28,20},{1,25},{... | collective-permute-start | bytes 1555208 | tf_op jit(solution)/shard_map/ppermute | solution.py:259
  27.5 1.9 %collective-permute-done.8 = f32[80,720]{1,0:T(8,128)S(1)} collective-permute-done((f32[80,720]{1,0:T(8,128)S(1)}, f32[80,720]{1,0:T(8,128)S(1)}, u32[]{:S(2)}, u32[]{:S(2)}) %collective-permute-start.8) | collective-permute-done | bytes 230432 | tf_op jit(solution)/shard_map/ppermute | solution.py:262
  29.4 2.3 %collective-permute-start.11 = (bf16[80,720]{1,0:T(8,128)(2,1)S(1)}, bf16[80,720]{1,0:T(8,128)(2,1)S(1)}, u32[]{:S(2)}, u32[]{:S(2)}) collective-permute-start(bf16[80,720]{1,0:T(8,128)(2,1)S(1)} %add_convert_fusion), channel_id=1, source_target_pairs={{0,16},{4,20},{8,24},{12,28},{16,0},{20,4},{24,8},{28,12},{1,17},{... | collective-permute-start | bytes 345608 | tf_op jit(solution)/shard_map/ppermute | solution.py:259
  31.7 0.4 collective-permute-start.10
  32.1 1.6 %collective-permute-start.9 = (bf16[80,720]{1,0:T(8,128)(2,1)S(1)}, bf16[80,720]{1,0:T(8,128)(2,1)S(1)}, u32[]{:S(2)}, u32[]{:S(2)}) collective-permute-start(bf16[80,720]{1,0:T(8,128)(2,1)S(1)} %add_convert_fusion), channel_id=1, source_target_pairs={{0,8},{4,12},{8,16},{12,20},{16,24},{20,28},{24,0},{28,4},{1,9},{5... | collective-permute-start | bytes 345608 | tf_op jit(solution)/shard_map/ppermute | solution.py:259
  33.7 0.1 stack.54.where
  33.8 23.9 %collective-permute-done.11 = bf16[80,720]{1,0:T(8,128)(2,1)S(1)} collective-permute-done((bf16[80,720]{1,0:T(8,128)(2,1)S(1)}, bf16[80,720]{1,0:T(8,128)(2,1)S(1)}, u32[]{:S(2)}, u32[]{:S(2)}) %collective-permute-start.11) | collective-permute-done | bytes 115232 | tf_op jit(solution)/shard_map/ppermute | solution.py:259
  57.7 0.5 collective-permute-start
  58.2 0.0 collective-permute-done.10
  58.2 0.9 collective-permute-done.9
  59.1 0.1 pad_maximum_fusion.refs_3_
  59.2 0.0 copy-start.1
  59.2 1.6 %collective-permute-start.12 = (bf16[4,80,720]{2,1,0:T(8,128)(2,1)S(1)}, bf16[4,80,720]{2,1,0:T(8,128)(2,1)S(1)}, u32[]{:S(2)}, u32[]{:S(2)}) collective-permute-start(bf16[4,80,720]{2,1,0:T(8,128)(2,1)S(1)} %pad_maximum_fusion.refs_3_), channel_id=1, source_target_pairs={{0,2},{1,3},{2,0},{3,1},{4,6},{5,7},{6,4},{7,5},{8,10},{9,11},{10,... | collective-permute-start | bytes 1382408 | tf_op jit(solution)/shard_map/ppermute | solution.py:265
  60.8 0.0 collective-permute-done.1.refs_5_.refs_9_
  60.8 3.0 %collective-permute-start.15 = (bf16[360,720]{1,0:T(8,128)(2,1)S(1)}, bf16[360,720]{1,0:T(8,128)(2,1)S(1)}, u32[]{:S(2)}, u32[]{:S(2)}) collective-permute-start(bf16[360,720]{1,0:T(8,128)(2,1)S(1)} %collective-permute-done.1.refs_5_.refs_9_), channel_id=1, source_target_pairs={{0,8},{4,12},{8,16},{12,20},{16,24},{20,28},{24,0},{28,4},{1,9},{5... | collective-permute-start | bytes 1555208 | tf_op jit(solution)/shard_map/ppermute | solution.py:259
  63.8 0.5 collective-permute-start.2
  64.3 0.0 collective-permute-done.3.refs_7_.refs_11_
  64.3 1.5 %collective-permute-start.4 = (bf16[360,720]{1,0:T(8,128)(2,1)S(1)}, bf16[360,720]{1,0:T(8,128)(2,1)S(1)}, u32[]{:S(2)}, u32[]{:S(2)}) collective-permute-start(bf16[360,720]{1,0:T(8,128)(2,1)S(1)} %collective-permute-done.3.refs_7_.refs_11_), channel_id=1, source_target_pairs={{0,4},{4,0},{8,12},{12,8},{16,20},{20,16},{24,28},{28,24},{1,5},{5... | collective-permute-start | bytes 1555208 | tf_op jit(solution)/shard_map/ppermute | solution.py:262
  65.8 0.9 copy-done.4
  66.8 1.9 %copy-done.5 = bf16[8,8,64,320]{3,2,1,0:T(8,128)(2,1)S(1)} copy-done((bf16[8,8,64,320]{3,2,1,0:T(8,128)(2,1)S(1)}, bf16[8,8,64,320]{3,2,1,0:T(8,128)(2,1)}, u32[]{:S(2)}) %copy-start.5) | copy-done | bytes 2621464
  68.6 1.9 %copy-done.6 = bf16[8,8,64,320]{3,2,1,0:T(8,128)(2,1)S(1)} copy-done((bf16[8,8,64,320]{3,2,1,0:T(8,128)(2,1)S(1)}, bf16[8,8,64,320]{3,2,1,0:T(8,128)(2,1)}, u32[]{:S(2)}) %copy-start.6) | copy-done | bytes 2621464
  70.5 14.4 %train_gradients.1.refs_0_.refs_1_.refs_2_ = bf16[4,8,320,720]{3,2,1,0:T(8,128)(2,1)S(1)} custom-call(bf16[8,8,64,320]{3,2,1,0:T(8,128)(2,1)S(1)} %copy-done.5, bf16[8,8,64,320]{3,2,1,0:T(8,128)(2,1)S(1)} %copy-done.6, bf16[320,320]{1,0:T(8,128)(2,1)S(1)} %copy-done.4), custom_call_target="tpu_custom_call" | custom-call | flops 7549747200 | bytes 5242880 | tf_op jit(solution)/shard_map/train_gradients/pallas_call | solution.py:89
  85.0 5.5 %copy-done = bf16[4,8,320,720]{3,2,1,0:T(8,128)(2,1)} copy-done((bf16[4,8,320,720]{3,2,1,0:T(8,128)(2,1)}, bf16[4,8,320,720]{3,2,1,0:T(8,128)(2,1)S(1)}, u32[]{:S(2)}) %copy-start) | copy-done | bytes 14745624
  90.5 0.0 collective-permute-done.refs_4_.refs_8_
  90.5 0.0 collective-permute-start.13
  90.5 0.0 collective-permute-done.12.refs_4_
  90.5 0.5 collective-permute-start.14
  91.0 0.0 collective-permute-done.15.refs_13_
  91.0 0.5 collective-permute-start.16
  91.5 5.5 %collective-permute-done.4.refs_8_.refs_12_ = bf16[360,720]{1,0:T(8,128)(2,1)S(1)} collective-permute-done((bf16[360,720]{1,0:T(8,128)(2,1)S(1)}, bf16[360,720]{1,0:T(8,128)(2,1)S(1)}, u32[]{:S(2)}, u32[]{:S(2)}) %collective-permute-start.4) | collective-permute-done | bytes 518432 | tf_op jit(solution)/shard_map/ppermute | solution.py:262
  97.0 0.0 collective-permute-done.2.refs_6_.refs_10_
  97.0 13.9 %early_products.1.refs_1_ = f32[8,320,720]{2,1,0:T(8,128)} custom-call(s32[9]{0:T(128)S(1)} %stack.54.where, bf16[4,8,320,720]{3,2,1,0:T(8,128)(2,1)} %copy-done, bf16[4,8,320,720]{3,2,1,0:T(8,128)(2,1)} %copy-done, bf16[4,8,320,720]{3,2,1,0:T(8,128)(2,1)} %copy-done, bf16[360,720]{1,0:T(8,128)(2,1)S(1)} %copy-done.1, ...), custom_call_target="tpu_custom_call" | custom-call | flops 7962624000 | bytes 7372800 | tf_op jit(solution)/shard_map/early_products/pallas_call | solution.py:145
  111.0 0.0 collective-permute-done.13.refs_5_
  111.0 0.0 collective-permute-done.14.refs_6_
  111.0 0.0 collective-permute-done.16.refs_14_
  111.0 0.8 copy-done.7
  111.8 11.8 %final_products.1 = (f32[4,2,128]{2,1,0:T(2,128)S(1)}, f32[4,80,720]{2,1,0:T(8,128)}) custom-call(s32[9]{0:T(128)S(1)} %stack.54.where, bf16[4,8,320,720]{3,2,1,0:T(8,128)(2,1)} %copy-done, f32[8,320,720]{2,1,0:T(8,128)} %early_products.1.refs_1_, f32[4,80,720]{2,1,0:T(8,128)} %bitcast.23, bf16[4,80,720]{2,1,0:T(8,128)(2,1)S(1)} %pad_maximum_fusion.refs_3_, ...), custom_call_target="tpu_custom_call" | custom-call | flops 3981312000 | bytes 7372800 | tf_op jit(solution)/shard_map/final_products/pallas_call | solution.py:199
  123.6 0.1 slice_reduce_fusion
  123.7 0.1 reshape_squeeze.3
  123.7 1.5 %collective-permute-start.17 = (f32[8]{0:T(128)S(1)}, f32[8]{0:T(128)S(1)}, u32[]{:S(2)}, u32[]{:S(2)}) collective-permute-start(f32[8]{0:T(128)S(1)} %reshape_squeeze.3), channel_id=1, source_target_pairs={{0,2},{1,3},{2,0},{3,1},{4,6},{5,7},{6,4},{7,5},{8,10},{9,11},{10,... | collective-permute-start | bytes 104 | tf_op jit(solution)/shard_map/ppermute | solution.py:265
  125.2 2.1 %collective-permute-done.17 = f32[8]{0:T(128)S(1)} collective-permute-done((f32[8]{0:T(128)S(1)}, f32[8]{0:T(128)S(1)}, u32[]{:S(2)}, u32[]{:S(2)}) %collective-permute-start.17) | collective-permute-done | bytes 64 | tf_op jit(solution)/shard_map/ppermute | solution.py:265
  127.3 0.0 collective-permute-start.18
  127.3 1.1 collective-permute-done.18
  128.4 0.6 multiply_multiply_fusion
  (11 shorter events, 0.0 us)
Async XLA Ops:
  1.7 1.0 copy-start.2
  2.7 1.0 copy-start.3
  5.8 8.8 %collective-permute-start.7 = (f16[80,768]{1,0:T(8,128)(2,1)S(1)}, f16[80,768]{1,0:T(8,128)(2,1)S(1)}, u32[]{:S(2)}, u32[]{:S(2)}) collective-permute-start(f16[80,768]{1,0:T(8,128)(2,1)S(1)} %get-tuple-element.7), channel_id=1, source_target_pairs={{0,24},{4,28},{8,0},{12,4},{16,8},{20,12},{24,16},{28,20},{1,25},{... | collective-permute-start | bytes 368648 | tf_op jit(solution)/shard_map/ppermute | solution.py:259
  10.9 10.6 %collective-permute-start.6 = (f16[80,768]{1,0:T(8,128)(2,1)S(1)}, f16[80,768]{1,0:T(8,128)(2,1)S(1)}, u32[]{:S(2)}, u32[]{:S(2)}) collective-permute-start(f16[80,768]{1,0:T(8,128)(2,1)S(1)} %get-tuple-element.8), channel_id=1, source_target_pairs={{0,16},{4,20},{8,24},{12,28},{16,0},{20,4},{24,8},{28,12},{1,17},{... | collective-permute-start | bytes 368648 | tf_op jit(solution)/shard_map/ppermute | solution.py:259
  10.9 10.8 %collective-permute-start.5 = (f16[80,768]{1,0:T(8,128)(2,1)S(1)}, f16[80,768]{1,0:T(8,128)(2,1)S(1)}, u32[]{:S(2)}, u32[]{:S(2)}) collective-permute-start(f16[80,768]{1,0:T(8,128)(2,1)S(1)} %get-tuple-element.9), channel_id=1, source_target_pairs={{0,8},{4,12},{8,16},{12,20},{16,24},{20,28},{24,0},{28,4},{1,9},{5... | collective-permute-start | bytes 368648 | tf_op jit(solution)/shard_map/ppermute | solution.py:259
  22.1 7.3 %collective-permute-start.8 = (f32[80,720]{1,0:T(8,128)S(1)}, f32[80,720]{1,0:T(8,128)S(1)}, u32[]{:S(2)}, u32[]{:S(2)}) collective-permute-start(f32[80,720]{1,0:T(8,128)S(1)} %multiply_add_fusion), channel_id=1, source_target_pairs={{0,4},{4,0},{8,12},{12,8},{16,20},{20,16},{24,28},{28,24},{1,5},{5... | collective-permute-start | bytes 691208 | tf_op jit(solution)/shard_map/ppermute | solution.py:262
  23.7 37.1 %collective-permute-start.1 = (bf16[360,720]{1,0:T(8,128)(2,1)}, bf16[360,720]{1,0:T(8,128)(2,1)S(1)}, u32[]{:S(2)}, u32[]{:S(2)}) collective-permute-start(bf16[360,720]{1,0:T(8,128)(2,1)} %refs_7_.1), channel_id=1, source_target_pairs={{0,8},{4,12},{8,16},{12,20},{16,24},{20,28},{24,0},{28,4},{1,9},{5... | collective-permute-start | bytes 1555208 | tf_op jit(solution)/shard_map/ppermute | solution.py:259
  24.1 40.2 %collective-permute-start.3 = (bf16[360,720]{1,0:T(8,128)(2,1)}, bf16[360,720]{1,0:T(8,128)(2,1)S(1)}, u32[]{:S(2)}, u32[]{:S(2)}) collective-permute-start(bf16[360,720]{1,0:T(8,128)(2,1)} %refs_7_.1), channel_id=1, source_target_pairs={{0,24},{4,28},{8,0},{12,4},{16,8},{20,12},{24,16},{28,20},{1,25},{... | collective-permute-start | bytes 1555208 | tf_op jit(solution)/shard_map/ppermute | solution.py:259
  29.4 28.3 %collective-permute-start.11 = (bf16[80,720]{1,0:T(8,128)(2,1)S(1)}, bf16[80,720]{1,0:T(8,128)(2,1)S(1)}, u32[]{:S(2)}, u32[]{:S(2)}) collective-permute-start(bf16[80,720]{1,0:T(8,128)(2,1)S(1)} %add_convert_fusion), channel_id=1, source_target_pairs={{0,16},{4,20},{8,24},{12,28},{16,0},{20,4},{24,8},{28,12},{1,17},{... | collective-permute-start | bytes 345608 | tf_op jit(solution)/shard_map/ppermute | solution.py:259
  31.7 26.6 %collective-permute-start.10 = (bf16[80,720]{1,0:T(8,128)(2,1)S(1)}, bf16[80,720]{1,0:T(8,128)(2,1)S(1)}, u32[]{:S(2)}, u32[]{:S(2)}) collective-permute-start(bf16[80,720]{1,0:T(8,128)(2,1)S(1)} %add_convert_fusion), channel_id=1, source_target_pairs={{0,24},{4,28},{8,0},{12,4},{16,8},{20,12},{24,16},{28,20},{1,25},{... | collective-permute-start | bytes 345608 | tf_op jit(solution)/shard_map/ppermute | solution.py:259
  32.1 27.0 %collective-permute-start.9 = (bf16[80,720]{1,0:T(8,128)(2,1)S(1)}, bf16[80,720]{1,0:T(8,128)(2,1)S(1)}, u32[]{:S(2)}, u32[]{:S(2)}) collective-permute-start(bf16[80,720]{1,0:T(8,128)(2,1)S(1)} %add_convert_fusion), channel_id=1, source_target_pairs={{0,8},{4,12},{8,16},{12,20},{16,24},{20,28},{24,0},{28,4},{1,9},{5... | collective-permute-start | bytes 345608 | tf_op jit(solution)/shard_map/ppermute | solution.py:259
  57.7 32.8 %collective-permute-start = (bf16[360,720]{1,0:T(8,128)(2,1)}, bf16[360,720]{1,0:T(8,128)(2,1)S(1)}, u32[]{:S(2)}, u32[]{:S(2)}) collective-permute-start(bf16[360,720]{1,0:T(8,128)(2,1)} %refs_7_.1), channel_id=1, source_target_pairs={{0,4},{4,0},{8,12},{12,8},{16,20},{20,16},{24,28},{28,24},{1,5},{5... | collective-permute-start | bytes 1555208 | tf_op jit(solution)/shard_map/ppermute | solution.py:262
  59.2 37.9 %copy-start.1 = (bf16[360,720]{1,0:T(8,128)(2,1)S(1)}, bf16[360,720]{1,0:T(8,128)(2,1)}, u32[]{:S(2)}) copy-start(bf16[360,720]{1,0:T(8,128)(2,1)} %refs_7_.1) | copy-start | bytes 1555204
  59.2 31.3 %collective-permute-start.12 = (bf16[4,80,720]{2,1,0:T(8,128)(2,1)S(1)}, bf16[4,80,720]{2,1,0:T(8,128)(2,1)S(1)}, u32[]{:S(2)}, u32[]{:S(2)}) collective-permute-start(bf16[4,80,720]{2,1,0:T(8,128)(2,1)S(1)} %pad_maximum_fusion.refs_3_), channel_id=1, source_target_pairs={{0,2},{1,3},{2,0},{3,1},{4,6},{5,7},{6,4},{7,5},{8,10},{9,11},{10,... | collective-permute-start | bytes 1382408 | tf_op jit(solution)/shard_map/ppermute | solution.py:265
  60.8 30.2 %collective-permute-start.15 = (bf16[360,720]{1,0:T(8,128)(2,1)S(1)}, bf16[360,720]{1,0:T(8,128)(2,1)S(1)}, u32[]{:S(2)}, u32[]{:S(2)}) collective-permute-start(bf16[360,720]{1,0:T(8,128)(2,1)S(1)} %collective-permute-done.1.refs_5_.refs_9_), channel_id=1, source_target_pairs={{0,8},{4,12},{8,16},{12,20},{16,24},{20,28},{24,0},{28,4},{1,9},{5... | collective-permute-start | bytes 1555208 | tf_op jit(solution)/shard_map/ppermute | solution.py:259
  63.8 33.3 %collective-permute-start.2 = (bf16[360,720]{1,0:T(8,128)(2,1)S(1)}, bf16[360,720]{1,0:T(8,128)(2,1)S(1)}, u32[]{:S(2)}, u32[]{:S(2)}) collective-permute-start(bf16[360,720]{1,0:T(8,128)(2,1)S(1)} %collective-permute-done.1.refs_5_.refs_9_), channel_id=1, source_target_pairs={{0,4},{4,0},{8,12},{12,8},{16,20},{20,16},{24,28},{28,24},{1,5},{5... | collective-permute-start | bytes 1555208 | tf_op jit(solution)/shard_map/ppermute | solution.py:262
  64.3 32.7 %collective-permute-start.4 = (bf16[360,720]{1,0:T(8,128)(2,1)S(1)}, bf16[360,720]{1,0:T(8,128)(2,1)S(1)}, u32[]{:S(2)}, u32[]{:S(2)}) collective-permute-start(bf16[360,720]{1,0:T(8,128)(2,1)S(1)} %collective-permute-done.3.refs_7_.refs_11_), channel_id=1, source_target_pairs={{0,4},{4,0},{8,12},{12,8},{16,20},{20,16},{24,28},{28,24},{1,5},{5... | collective-permute-start | bytes 1555208 | tf_op jit(solution)/shard_map/ppermute | solution.py:262
  65.8 0.9 copy-start.4
  66.8 1.9 %copy-start.5 = (bf16[8,8,64,320]{3,2,1,0:T(8,128)(2,1)S(1)}, bf16[8,8,64,320]{3,2,1,0:T(8,128)(2,1)}, u32[]{:S(2)}) copy-start(bf16[8,8,64,320]{3,2,1,0:T(8,128)(2,1)} %x_ref.2) | copy-start | bytes 7864324
  68.6 1.9 %copy-start.6 = (bf16[8,8,64,320]{3,2,1,0:T(8,128)(2,1)S(1)}, bf16[8,8,64,320]{3,2,1,0:T(8,128)(2,1)}, u32[]{:S(2)}) copy-start(bf16[8,8,64,320]{3,2,1,0:T(8,128)(2,1)} %c_ref.2) | copy-start | bytes 7864324
  85.0 5.5 %copy-start = (bf16[4,8,320,720]{3,2,1,0:T(8,128)(2,1)}, bf16[4,8,320,720]{3,2,1,0:T(8,128)(2,1)S(1)}, u32[]{:S(2)}) copy-start(bf16[4,8,320,720]{3,2,1,0:T(8,128)(2,1)S(1)} %train_gradients.1.refs_0_.refs_1_.refs_2_) | copy-start | bytes 44236804
  90.5 20.5 %collective-permute-start.13 = (bf16[4,80,720]{2,1,0:T(8,128)(2,1)S(1)}, bf16[4,80,720]{2,1,0:T(8,128)(2,1)S(1)}, u32[]{:S(2)}, u32[]{:S(2)}) collective-permute-start(bf16[4,80,720]{2,1,0:T(8,128)(2,1)S(1)} %pad_maximum_fusion.refs_3_), channel_id=1, source_target_pairs={{0,1},{1,0},{2,3},{3,2},{4,5},{5,4},{6,7},{7,6},{8,9},{9,8},{10,11... | collective-permute-start | bytes 1382408 | tf_op jit(solution)/shard_map/ppermute | solution.py:265
  90.5 20.5 %collective-permute-start.14 = (bf16[4,80,720]{2,1,0:T(8,128)(2,1)S(1)}, bf16[4,80,720]{2,1,0:T(8,128)(2,1)S(1)}, u32[]{:S(2)}, u32[]{:S(2)}) collective-permute-start(bf16[4,80,720]{2,1,0:T(8,128)(2,1)S(1)} %collective-permute-done.12.refs_4_), channel_id=1, source_target_pairs={{0,1},{1,0},{2,3},{3,2},{4,5},{5,4},{6,7},{7,6},{8,9},{9,8},{10,11... | collective-permute-start | bytes 1382408 | tf_op jit(solution)/shard_map/ppermute | solution.py:265
  91.0 20.0 %collective-permute-start.16 = (bf16[360,720]{1,0:T(8,128)(2,1)S(1)}, bf16[360,720]{1,0:T(8,128)(2,1)S(1)}, u32[]{:S(2)}, u32[]{:S(2)}) collective-permute-start(bf16[360,720]{1,0:T(8,128)(2,1)S(1)} %collective-permute-done.15.refs_13_), channel_id=1, source_target_pairs={{0,4},{4,0},{8,12},{12,8},{16,20},{20,16},{24,28},{28,24},{1,5},{5... | collective-permute-start | bytes 1555208 | tf_op jit(solution)/shard_map/ppermute | solution.py:262
  111.0 0.8 copy-start.7
  111.8 16.6 %copy-start.8 = (s32[8]{0:T(128)S(1)}, s32[8]{0:T(128)}, u32[]{:S(2)}) copy-start(s32[8]{0:T(128)} %param.12) | copy-start | bytes 100
  123.7 3.5 %collective-permute-start.17 = (f32[8]{0:T(128)S(1)}, f32[8]{0:T(128)S(1)}, u32[]{:S(2)}, u32[]{:S(2)}) collective-permute-start(f32[8]{0:T(128)S(1)} %reshape_squeeze.3), channel_id=1, source_target_pairs={{0,2},{1,3},{2,0},{3,1},{4,6},{5,7},{6,4},{7,5},{8,10},{9,11},{10,... | collective-permute-start | bytes 104 | tf_op jit(solution)/shard_map/ppermute | solution.py:265
  127.3 1.1 collective-permute-start.18

commit v2 on v0

v2 whole, which is shorter than its diff:
```python
import functools
import math

import jax
import jax.numpy as jnp
from jax import lax
from jax.experimental import pallas as pl
from jax.experimental.pallas import tpu as pltpu
from jax.sharding import PartitionSpec as P

damping = 0.01
levels = 32000.0
bf16 = jnp.bfloat16
f32 = jnp.float32
i16 = jnp.int16
i32 = jnp.int32
first_dims = (((0,), (0,)), ((), ()))
last_dims = (((1,), (1,)), ((), ()))
fence = lax.optimization_barrier
mib = 2**20
in_vmem = pl.BlockSpec(memory_space=pltpu.VMEM)
anywhere = pl.BlockSpec(memory_space=pl.ANY)


def padded(size, unit):
    return size + (-size) % unit


def with_scale(size):
    return size + 128 - size % 128


def cheap(flops=1000):
    return pl.CostEstimate(flops=flops, bytes_accessed=1000, transcendentals=0)


def params():
    return pltpu.CompilerParams(vmem_limit_bytes=24 * mib)


def position(groups, parts):
    me, place = lax.axis_index("dp"), lax.axis_index("factor")
    return me, lax.rem(me, groups), lax.div(place, parts), lax.rem(place, parts)


def power_of(*arrays):
    tops = [jnp.max(jnp.max(jnp.abs(a), axis=1, keepdims=True), axis=0, keepdims=True) for a in arrays]
    largest = functools.reduce(jnp.maximum, tops)
    return jnp.ceil(jnp.log(jnp.maximum(largest, 1e-30)) * (1 / math.log(2.0)))


def encode(array, power):
    return jnp.round(array * (jnp.exp2(-power) * levels)).astype(i32).astype(i16)


def put(ref, at, array, power):
    rows, size = array.shape
    wide = ref.shape[-1]
    marks = jnp.broadcast_to(power, (rows, wide - size)).astype(i32).astype(i16)
    if at is None:
        ref[:, :size] = encode(array, power)
        ref[:, size:] = marks
    else:
        ref[at, :, :size] = encode(array, power)
        ref[at, :, size:] = marks


def decode(sent, size):
    values = sent[:, :size].astype(i32).astype(f32)
    power = sent[:, size : size + 1].astype(i32).astype(f32)
    return values * (jnp.exp2(power) * (1 / levels))


def halves(array):
    upper = array.astype(bf16)
    lower = (array - upper.astype(f32)).astype(bf16)
    return upper, lower


def both_halves(array):
    upper = array.astype(bf16).astype(f32)
    return jnp.concatenate([upper, array - upper], axis=0).astype(bf16)


def shifted_inputs(activations):
    rows, cols, channels = activations.shape
    edge = jnp.zeros((rows, 1, channels), activations.dtype)
    before = jnp.concatenate([edge, activations[:, :-1]], axis=1)
    after = jnp.concatenate([activations[:, 1:], edge], axis=1)
    blank = jnp.zeros((cols, channels), activations.dtype)
    return [
        jnp.concatenate([blank, part.reshape(rows * cols, channels), blank], axis=0)
        for part in (before, activations, after)
    ]


def patch_columns(shifted, rows, cols, start, stop):
    channels = shifted[0].shape[1]
    taps = []
    for tap in range(start // channels, -(-stop // channels)):
        row_off, col_off = divmod(tap, 3)
        low, high = max(start - tap * channels, 0), min(stop - tap * channels, channels)
        taps.append(shifted[col_off][row_off * cols : (row_off + rows) * cols, low:high])
    return jnp.concatenate(taps, axis=1)


def fence_blocks(blocks, near, *others):
    held, rest, others = fence(([b for _, b in blocks], [b for _, b in near], others))
    named = [(spot, b) for (spot, _), b in zip(blocks, held)]
    return named, [(spot, b) for (spot, _), b in zip(near, rest)], *others


def query_kernel(x_ref, c_ref, basis_ref, out, chosen_ref, total, *, groups, parts, own_rows, scale):
    queries, rows, cols, channels = x_ref.shape
    shards, high_rows, depth = total.shape
    _, _, side, part = position(groups, parts)
    span = groups * high_rows
    row_at = lax.broadcasted_iota(i32, (channels, span), 0)
    col_at = lax.broadcasted_iota(i32, (channels, span), 1)
    group, item = lax.div(col_at, high_rows), lax.rem(col_at, high_rows)
    wanted = part * groups * own_rows + group * own_rows + item
    chosen = jnp.where((row_at == wanted) & (item < own_rows), 1.0, 0.0).astype(bf16)
    own_basis = jnp.dot(basis_ref[...], chosen, preferred_element_type=f32).astype(bf16)
    chosen_ref[...] = own_basis

    for value in range(2):

        @pl.when(side == value)
        def _(value=value):
            sums = [jnp.zeros((span, depth), f32) for _ in range(2)]
            for query in range(queries):
                cot = c_ref[query].reshape(rows * cols, channels)
                upper, lower = halves(jnp.dot(cot, own_basis, preferred_element_type=f32))
                shifted = shifted_inputs(x_ref[query])
                for half in range(2):
                    start = (2 * half + value) * depth
                    patches = patch_columns(shifted, rows, cols, start, start + depth)
                    for piece in (upper, lower):
                        sums[half] += lax.dot_general(
                            piece, patches, first_dims, preferred_element_type=f32
                        )
            for half in range(2):
                for group in range(groups):
                    total[half * groups + group] = (
                        sums[half][group * high_rows : (group + 1) * high_rows] * scale
                    )

    power = power_of(*[total[shard] for shard in range(shards)])
    for shard in range(shards):
        put(out, shard, total[shard], power)


def query_partial(x, cot, basis, shards, groups, parts, own_rows, scale):
    channels = x.shape[-1]
    high_rows = padded(own_rows, 8)
    depth = 9 * channels // 4
    return pl.pallas_call(
        functools.partial(
            query_kernel, groups=groups, parts=parts, own_rows=own_rows, scale=scale
        ),
        in_specs=[in_vmem] * 3,
        out_specs=[in_vmem] * 2,
        out_shape=[
            jax.ShapeDtypeStruct((shards, high_rows, with_scale(depth)), i16),
            jax.ShapeDtypeStruct((channels, groups * high_rows), bf16),
        ],
        scratch_shapes=[pltpu.VMEM((shards, high_rows, depth), f32)],
        compiler_params=params(),
        cost_estimate=cheap(),
        name="query_gradient",
    )(x, cot, basis)


def train_kernel(basis_ref, x_ref, c_ref, out_ref, *, parts):
    _, rows, cols, channels = x_ref.shape
    shards, _, high_rows, depth = out_ref.shape
    groups = shards // 2
    _, _, side, _ = position(groups, parts)
    cot = c_ref[0].reshape(rows * cols, channels)
    rotated = jnp.dot(cot, basis_ref[...], preferred_element_type=f32).astype(bf16)
    for value in range(2):

        @pl.when(side == value)
        def _(value=value):
            shifted = shifted_inputs(x_ref[0])
            for half in range(2):
                start = (2 * half + value) * depth
                patches = patch_columns(shifted, rows, cols, start, start + depth)
                grad = lax.dot_general(rotated, patches, first_dims, preferred_element_type=f32)
                for group in range(groups):
                    out_ref[half * groups + group, 0] = grad[
                        group * high_rows : (group + 1) * high_rows
                    ]


def train_gradients(chosen, x, cot, shards, parts, first, count, flops):
    _, rows, cols, channels = x.shape
    high_rows = chosen.shape[1] // (shards // 2)
    depth = 9 * channels // 4
    spec = pl.BlockSpec((1, rows, cols, channels), lambda i: (first + i, 0, 0, 0))
    return pl.pallas_call(
        functools.partial(train_kernel, parts=parts),
        grid=(count,),
        in_specs=[pl.BlockSpec(chosen.shape, lambda i: (0, 0)), spec, spec],
        out_specs=pl.BlockSpec((shards, 1, high_rows, depth), lambda i: (0, i, 0, 0)),
        out_shape=jax.ShapeDtypeStruct((shards, count, high_rows, depth), f32),
        compiler_params=params(),
        cost_estimate=cheap(flops),
        name="train_gradients",
    )(chosen, x, cot)


def merge_kernel(arrived, keep_ref, send_ref):
    total = decode(arrived[0], keep_ref.shape[1])
    for shard in range(1, arrived.shape[0]):
        total += decode(arrived[shard], keep_ref.shape[1])
    keep_ref[...] = total
    put(send_ref, None, total, power_of(total))


def merge(arrived, depth):
    _, high_rows, wide = arrived.shape
    return pl.pallas_call(
        merge_kernel,
        in_specs=[in_vmem],
        out_specs=[in_vmem] * 2,
        out_shape=[
            jax.ShapeDtypeStruct((high_rows, depth), f32),
            jax.ShapeDtypeStruct((high_rows, wide), i16),
        ],
        compiler_params=params(),
        cost_estimate=cheap(),
        name="merge",
    )(arrived)


def project_kernel(own_ref, other_ref, *refs, spots, groups, parts):
    pieces, (out, stacked) = refs[: len(spots)], refs[len(spots) :]
    high_rows, depth = own_ref.shape
    rows = depth * 2 // groups
    _, group, side, _ = position(groups, parts)
    own, other = own_ref[...], decode(other_ref, depth)
    for half, value in enumerate(
        (jnp.where(side == 0, own, other), jnp.where(side == 0, other, own))
    ):
        both = both_halves(value)
        for at in range(groups // 2):
            stacked[half * (groups // 2) + at] = both[:, at * rows : (at + 1) * rows]
    results = [0.0] * parts
    for piece, (row, part, start, stop) in zip(pieces, spots):
        left = stacked[jnp.bitwise_xor(group, row)][:, start:stop]
        results[part] += jnp.dot(left, piece[...], preferred_element_type=f32)
    results = [total[:high_rows] + total[high_rows:] for total in results]
    power = power_of(*results)
    for part in range(parts):
        put(out, part, results[part], power)


def project(own, other, blocks, groups, parts):
    spots = [spot for spot, _ in blocks]
    pieces = [piece for _, piece in blocks]
    high_rows, depth = own.shape
    return pl.pallas_call(
        functools.partial(project_kernel, spots=spots, groups=groups, parts=parts),
        in_specs=[in_vmem] * (2 + len(pieces)),
        out_specs=in_vmem,
        out_shape=jax.ShapeDtypeStruct((parts, high_rows, with_scale(pieces[0].shape[1])), i16),
        scratch_shapes=[pltpu.VMEM((groups, 2 * high_rows, depth * 2 // groups), bf16)],
        compiler_params=params(),
        cost_estimate=cheap(),
        name="project",
    )(own, other, *pieces)


def back_kernel(own_ref, other_ref, *refs, spots, groups, parts):
    eigen, refs = refs[:parts], refs[parts:]
    pieces, refs = refs[: len(spots)], refs[len(spots) :]
    proj_ref, keep_ref, send_ref, ordered = refs
    high_rows, width = eigen[0].shape
    _, group, side, _ = position(groups, parts)
    results, stacked = [], []
    for part in range(parts):
        total = decode(own_ref[part], width) + decode(other_ref[part], width)
        results.append(total / (eigen[part][...] + damping))
        stacked.append(both_halves(results[part]))
    sums = {}
    for piece, (row, part, start, stop) in zip(pieces, spots):
        total = lax.dot_general(
            stacked[part], piece[...], last_dims, preferred_element_type=f32
        )
        sums[row, start, stop] = sums.get((row, start, stop), 0.0) + total
    for (row, start, stop), total in sums.items():
        ordered[jnp.bitwise_xor(group, row), :, start:stop] = total[:high_rows] + total[high_rows:]
    sides = [
        jnp.concatenate(
            [ordered[half * (groups // 2) + at] for at in range(groups // 2)], axis=1
        )
        for half in range(2)
    ]
    keep = jnp.where(side == 0, sides[0], sides[1])
    send = jnp.where(side == 0, sides[1], sides[0])
    power = power_of(keep, send)
    put(keep_ref, None, keep, power)
    put(send_ref, None, send, power)
    power = power_of(*results)
    for part in range(parts):
        put(proj_ref, part, results[part], power)


def project_back(own, other, eigen, blocks, rows, groups, parts):
    spots = [spot for spot, _ in blocks]
    pieces = [piece for _, piece in blocks]
    high_rows = eigen[0].shape[0]
    half = jax.ShapeDtypeStruct((high_rows, with_scale(groups * rows // 2)), i16)
    return pl.pallas_call(
        functools.partial(back_kernel, spots=spots, groups=groups, parts=parts),
        in_specs=[in_vmem] * (2 + parts + len(pieces)),
        out_specs=[in_vmem] * 3,
        out_shape=[jax.ShapeDtypeStruct(own.shape, i16), half, half],
        scratch_shapes=[pltpu.VMEM((groups, high_rows, rows), f32)],
        compiler_params=params(),
        cost_estimate=cheap(),
        name="project_back",
    )(own, other, *eigen, *pieces)


def score_kernel(even_ref, odd_ref, *refs):
    grads, out = refs[:-1], refs[-1]
    pairs = even_ref.shape[0]
    count, high_rows, depth = grads[0].shape[1:]
    me = lax.axis_index("dp")
    blocks = []
    for away in range(2 * pairs):
        values = (odd_ref if away % 2 else even_ref)[away // 2]
        blocks.append((jnp.bitwise_xor(me, away), decode(values, depth)))
    for chunk, grad in enumerate(grads):
        for item in range(count):
            total = jnp.zeros((high_rows, depth), f32)
            for at, values in blocks:
                total += grad[at, item] * values
            total = jnp.sum(jnp.sum(total, axis=0, keepdims=True), axis=1, keepdims=True)
            at = chunk * count + item
            out[at : at + 1, :] = jnp.broadcast_to(total, (1, out.shape[1]))


def score_products(even, odd, grads):
    return pl.pallas_call(
        score_kernel,
        in_specs=[in_vmem] * (2 + len(grads)),
        out_specs=in_vmem,
        out_shape=jax.ShapeDtypeStruct((len(grads) * grads[0].shape[1], 128), f32),
        compiler_params=params(),
        cost_estimate=cheap(),
        name="score_products",
    )(even, odd, *grads)


def output_kernel(*refs):
    found, out = refs[:-1], refs[-1]
    parts, groups, own_rows, jump = out.shape
    _, group, _, part = position(groups, parts)
    for pair in range(groups // 2):
        for odd in range(2):
            for away in range(parts):
                value = decode(found[pair][odd, away], jump)
                row = jnp.bitwise_xor(group, 2 * pair + odd)
                out[jnp.bitwise_xor(part, away), row] = value[:own_rows]


def output_rows(found, groups, parts, own_rows, jump):
    return pl.pallas_call(
        output_kernel,
        in_specs=[in_vmem] * len(found),
        out_specs=in_vmem,
        out_shape=jax.ShapeDtypeStruct((parts, groups, own_rows, jump), f32),
        compiler_params=params(),
        cost_estimate=cheap(),
        name="output_rows",
    )(*found)


def on_device(
    train_inputs,
    train_cotangents,
    query_inputs,
    query_cotangents,
    timesteps,
    input_basis,
    output_basis,
    eigenvalues,
):
    channels = output_basis.shape[0]
    shards = lax.axis_size("dp")
    factor = lax.axis_size("factor")
    groups, parts = shards // 2, factor // 2
    width = input_basis.shape[0] * shards
    depth = width // 4
    own_rows = channels // (groups * parts)
    high_rows = padded(own_rows, 8)
    jump = input_basis.shape[1]
    group, part = lax.axis_index("dp") % groups, lax.axis_index("factor") % parts
    early, late = 10**3, 10**10
    batch = train_inputs.shape[0]
    chunks = 2 if batch % 2 == 0 else 1
    rows = input_basis.shape[0]
    cut = padded(rows // 2, 16)

    def swap(array, away):
        return lax.ppermute(array, "dp", [(d, d ^ away) for d in range(shards)])

    def flip(array, away):
        return lax.ppermute(array, "factor", [(p, p ^ away) for p in range(factor)])

    def train(chunk, chosen):
        size = batch // chunks
        return train_gradients(
            chosen, train_inputs, train_cotangents, shards, parts, chunk * size, size, late if chunk else early
        )

    blocks = [((0, 0, 0, rows), input_basis)]
    for away in range(1, groups):
        if away != 3:
            blocks.append(((away, 0, 0, rows), swap(input_basis, away)))
    near = [((0, away, 0, rows), flip(input_basis, away)) for away in range(1, parts)]
    count = query_inputs.shape[0] * shards
    partial, chosen = query_partial(
        query_inputs, query_cotangents, output_basis, shards, groups, parts, own_rows, 1.0 / count
    )
    arrived = lax.all_to_all(partial, "dp", 0, 0)
    trained = [train(0, chosen)]
    blocks, near, trained, chosen = fence_blocks(blocks, near, trained, chosen)

    if groups > 3:
        blocks.append(((3, 0, 0, cut), swap(blocks[2][1][:cut], 1)))
        blocks.append(((3, 0, cut, rows), swap(blocks[1][1][cut:], 2)))
    trained += [train(chunk, chosen) for chunk in range(1, chunks)]
    eigen = []
    for away in range(parts):
        start = ((part ^ away) * groups + group) * own_rows
        lines = lax.dynamic_slice_in_dim(eigenvalues, start, own_rows, axis=0)
        if high_rows > own_rows:
            lines = jnp.pad(lines, ((0, high_rows - own_rows), (0, 0)), constant_values=1.0)
        eigen.append(flip(lines, away) if away else lines)
    blocks, near, trained, arrived, eigen = fence_blocks(blocks, near, trained, arrived, eigen)

    total, sent = merge(arrived, depth)
    other = flip(sent, parts)
    for away in range(1, parts):
        for (row, _, start, stop), piece in blocks[1:]:
            near.append(((row, away, start, stop), flip(piece, away)))
    blocks, near, total, other = fence_blocks(blocks, near, total, other)
    blocks = blocks + near

    own = project(total, other, blocks, groups, parts)
    other = swap(own, groups)
    own, other, eigen = fence((own, other, eigen))

    proj, keep, send = project_back(own, other, eigen, blocks, rows, groups, parts)
    other = flip(send, parts)
    mine = [proj[0]] + [flip(proj[away], away) for away in range(1, parts)]
    keep, other, mine = fence((keep, other, mine))

    power_keep = keep[:, depth : depth + 1].astype(f32)
    power_other = other[:, depth : depth + 1].astype(f32)
    power = jnp.maximum(power_keep, power_other) + 1.0
    values = keep.astype(f32) * jnp.exp2(power_keep - power)
    values += other.astype(f32) * jnp.exp2(power_other - power)
    marked = lax.broadcasted_iota(i32, keep.shape, 1) >= depth
    whole = jnp.where(marked, power, jnp.round(values)).astype(i16)
    even = [whole] + [swap(whole, away) for away in range(2, shards, 2)]
    mine = jnp.stack(mine)
    pair = [mine, swap(mine, 1)]
    even, pair = fence((even, pair))

    even, pair = jnp.stack(even), jnp.stack(pair)
    odd = swap(even, 1)
    found = [pair] + [swap(pair, away) for away in range(2, groups, 2)]
    even, odd, found = fence((even, odd, found))

    sums = score_products(even, odd, trained)
    terms = [sums[:, 0]]
    terms += [flip(terms[0], away) for away in range(1, factor)]
    while len(terms) > 1:
        terms = [terms[at] + terms[at + 1] for at in range(0, len(terms), 2)]
    raw_scores = terms[0]
    query_proj = output_rows(found, groups, parts, own_rows, jump).reshape(channels, jump)
    phase = (timesteps.astype(f32) / 1000.0 + 0.008) / 1.008 * (math.pi / 2)
    weight = jnp.sin(phase)
    scores = raw_scores * weight / math.sqrt(channels * width)
    return (scores, query_proj)


def solution(mesh):
    in_specs = (
        P("dp", None, None, None),
        P("dp", None, None, None),
        P("dp", None, None, None),
        P("dp", None, None, None),
        P("dp"),
        P("dp", "factor"),
        P(),
        P(None, "factor"),
    )
    out_specs = (P("dp"), P(None, "factor"))
    return jax.shard_map(
        on_device, mesh=mesh, in_specs=in_specs, out_specs=out_specs, check_vma=False
    )
```

time: 309 us -> 83.4 us (0.27)
  waiting for transfers between devices: 139 us -> 20.2 us
  matrix products: 75.7 us -> 0 us
  local copies, waits for them, and re-layouts: 69.4 us -> 12.3 us
  starting transfers between devices: 0.08 us -> 30.5 us
  Pallas kernels: 0 us -> 17.8 us
  between operations: 14.1 us -> 0.83 us
  blocking collectives: 6.82 us -> 0 us
    psum x1 -> x0, waiting for transfers between devices: 135 us -> none  [on_device(): query_grad = lax.psum(partial_query, 'dp') / count]
    dot_general x7 -> x0, matrix products: 75.7 us -> none  [the longest x1 27.5 us: on_device(): jnp.einsum('bck,ck->b', train_proj, query_proj, precision=high)]
    concatenate x2 -> x0, local copies, waits for them, and re-layouts: 43.6 us -> none  [patch_matrix(): jnp.concatenate(taps, axis=-1)]
    ppermute x0 -> x23, starting transfers between devices: none -> 26.6 us  [the longest x11 18.3 us: swap(): return lax.ppermute(array, 'dp', [(d, d ^ away) for d in range(shards)])]
    slice x2 -> x3, local copies, waits for them, and re-layouts: 24.9 us -> 0.16 us  [the longest x1 0.12 us: on_device(): terms = [sums[:, 0]]]
    ppermute x0 -> x23, waiting for transfers between devices: none -> 20.2 us  [the longest x11 14.8 us: swap(): return lax.ppermute(array, 'dp', [(d, d ^ away) for d in range(shards)])]
    pallas_call x0 -> x8, Pallas kernels: none -> 17.8 us  [the longest x2 8.36 us: train_gradients(): pl.pallas_call(functools.partial(train_kernel, parts=parts), grid=(count,...]
    unnamed x16 -> x22, local copies, waits for them, and re-layouts: 0.97 us -> 10.5 us
  transfers between devices with their start and end apart: 2 -> 24, of which waited for: 2 -> 9; matrix products, arithmetic and copies ran while one was open for 35% -> 3% of each run, Pallas kernels for 0% -> 15%
where the time goes in v2:
time: 83.4 us; the launch traced here: 82.5 us
  starting transfers between devices  30.5 us (37%)
  waiting for transfers between devices  20.2 us (24%)
  Pallas kernels  17.8 us (21%)
  local copies, waits for them, and re-layouts  12.3 us (15%)
  other arithmetic  0.96 us (1%)
    ppermute x11, starting transfers between devices, swap(): return lax.ppermute(array, 'dp', [(d, d ^ away) for d in range(shards)])  18.3 us
    ppermute x11, waiting for transfers between devices, swap(): return lax.ppermute(array, 'dp', [(d, d ^ away) for d in range(shards)])  14.8 us
    unnamed x22, local copies, waits for them, and re-layouts  10.5 us
    pallas_call x2, Pallas kernels, train_gradients(): pl.pallas_call(functools.partial(train_kernel, parts=parts), grid=(count,...  8.36 us
    ppermute x12, starting transfers between devices, flip(): return lax.ppermute(array, 'factor', [(p, p ^ away) for p in range(factor)])  8.26 us
    ppermute x12, waiting for transfers between devices, flip(): return lax.ppermute(array, 'factor', [(p, p ^ away) for p in range(factor)])  5.38 us
    all_to_all x1, starting transfers between devices, on_device(): arrived = lax.all_to_all(partial, 'dp', 0, 0)  3.86 us
    pallas_call x1, Pallas kernels, project_back(): pl.pallas_call(functools.partial(back_kernel, spots=spots, groups=groups,...  2.81 us
  transfers between devices with their start and end apart: 24, of which 9 were waited for; matrix products, arithmetic and copies ran while one was open for 3% of the time, Pallas kernels for 15%

profile of v2, /device:TPU:0, one launch (start us, length us, event | category | flops | bytes accessed | tf_op | source)
XLA Modules:
  0.0 82.5 jit_solution(5478373320025797564)
XLA Ops:
  0.6 3.1 %collective-permute-start.1 = (bf16[360,720]{1,0:T(8,128)(2,1)}, bf16[360,720]{1,0:T(8,128)(2,1)S(1)}, u32[]{:S(2)}, u32[]{:S(2)}) collective-permute-start(bf16[360,720]{1,0:T(8,128)(2,1)} %refs_2_), channel_id=1, source_target_pairs={{0,8},{4,12},{8,0},{12,4},{16,24},{20,28},{24,16},{28,20},{1,9},{5... | collective-permute-start | bytes 1555208 | tf_op jit(solution)/shard_map/ppermute | solution.py:409
  3.7 1.5 %collective-permute-start = (bf16[360,720]{1,0:T(8,128)(2,1)}, bf16[360,720]{1,0:T(8,128)(2,1)S(1)}, u32[]{:S(2)}, u32[]{:S(2)}) collective-permute-start(bf16[360,720]{1,0:T(8,128)(2,1)} %refs_2_), channel_id=1, source_target_pairs={{0,4},{4,0},{8,12},{12,8},{16,20},{20,16},{24,28},{28,24},{1,5},{5... | collective-permute-start | bytes 1555208 | tf_op jit(solution)/shard_map/ppermute | solution.py:409
  5.2 0.0 collective-permute-start.2
  5.2 1.7 %constant_dynamic-slice_fusion = (f32[40,720]{1,0:T(8,128)}, f32[40,720]{1,0:T(8,128)S(1)}) fusion(f32[320,720]{1,0:T(8,128)} %param.15, s32[]{:T(128)S(6)} %select_n.24, s32[]{:T(128)S(6)} %select_n.23), kind=kLoop, calls=%fused_computation.20 | loop fusion | bytes 460808 | tf_op jit(solution)/shard_map/dynamic_slice | solution.py:440
  6.9 0.5 collective-permute-start.5
  7.4 1.0 %copy-done.7 = bf16[1,8,64,320]{3,2,1,0:T(8,128)(2,1)S(1)} copy-done((bf16[1,8,64,320]{3,2,1,0:T(8,128)(2,1)S(1)}, bf16[1,8,64,320]{3,2,1,0:T(8,128)(2,1)}, u32[]{:S(2)}) %copy-start.7) | copy-done | bytes 327704
  8.4 1.0 %copy-done.8 = bf16[1,8,64,320]{3,2,1,0:T(8,128)(2,1)S(1)} copy-done((bf16[1,8,64,320]{3,2,1,0:T(8,128)(2,1)S(1)}, bf16[1,8,64,320]{3,2,1,0:T(8,128)(2,1)}, u32[]{:S(2)}) %copy-start.8) | copy-done | bytes 327704
  9.4 0.9 %copy-done.9 = bf16[320,320]{1,0:T(8,128)(2,1)S(1)} copy-done((bf16[320,320]{1,0:T(8,128)(2,1)S(1)}, bf16[320,320]{1,0:T(8,128)(2,1)}, u32[]{:S(2)}) %copy-start.9) | copy-done | bytes 204824
  10.3 2.5 %query_gradient.1 = (s16[8,40,768]{2,1,0:T(8,128)(2,1)}, bf16[320,160]{1,0:T(8,128)(2,1)S(1)}) custom-call(bf16[1,8,64,320]{3,2,1,0:T(8,128)(2,1)S(1)} %copy-done.7, bf16[1,8,64,320]{3,2,1,0:T(8,128)(2,1)S(1)} %copy-done.8, bf16[320,320]{1,0:T(8,128)(2,1)S(1)} %copy-done.9), custom_call_target="tpu_custom_call" | custom-call | flops 1000 | bytes 1000 | tf_op jit(solution)/shard_map/query_gradient/pallas_call | solution.py:157
  12.8 3.9 %all-to-all-start = ((s16[8,40,768]{2,1,0:T(8,128)(2,1)}), s16[8,40,768]{2,1,0:T(8,128)(2,1)S(1)}, u32[]{:S(2)}, u32[]{:S(2)}) async-start(s16[8,40,768]{2,1,0:T(8,128)(2,1)} %get-tuple-element.63), calls=%async_computation | async-start | bytes 983040 | tf_op jit(solution)/shard_map/all_to_all | solution.py:429
  16.7 1.9 %copy-done.4 = bf16[8,8,64,320]{3,2,1,0:T(8,128)(2,1)S(1)} copy-done((bf16[8,8,64,320]{3,2,1,0:T(8,128)(2,1)S(1)}, bf16[8,8,64,320]{3,2,1,0:T(8,128)(2,1)}, u32[]{:S(2)}) %copy-start.4) | copy-done | bytes 2621464
  18.6 1.9 %copy-done.5 = bf16[8,8,64,320]{3,2,1,0:T(8,128)(2,1)S(1)} copy-done((bf16[8,8,64,320]{3,2,1,0:T(8,128)(2,1)S(1)}, bf16[8,8,64,320]{3,2,1,0:T(8,128)(2,1)}, u32[]{:S(2)}) %copy-start.5) | copy-done | bytes 2621464
  20.4 4.2 %train_gradients.2.refs_0_ = f32[8,4,40,720]{3,2,1,0:T(8,128)S(1)} custom-call(bf16[320,160]{1,0:T(8,128)(2,1)S(1)} %get-tuple-element.62.basis_ref, bf16[8,8,64,320]{3,2,1,0:T(8,128)(2,1)S(1)} %copy-done.4, bf16[8,8,64,320]{3,2,1,0:T(8,128)(2,1)S(1)} %copy-done.5), custom_call_target="tpu_custom_call" | custom-call | flops 1000 | bytes 1000 | tf_op jit(solution)/shard_map/train_gradients/pallas_call | solution.py:201
  24.6 1.9 %copy-done = f32[8,4,40,720]{3,2,1,0:T(8,128)} copy-done((f32[8,4,40,720]{3,2,1,0:T(8,128)}, f32[8,4,40,720]{3,2,1,0:T(8,128)S(1)}, u32[]{:S(2)}) %copy-start) | copy-done | bytes 3686424
  26.5 0.0 collective-permute-done.1.refs_2_.refs_4_
  26.5 0.0 collective-permute-done.refs_1_.refs_3_
  26.5 0.0 collective-permute-done.2.refs_5_.refs_7_
  26.5 2.1 %collective-permute-start.4 = (bf16[168,720]{1,0:T(8,128)(2,1)S(1)}, bf16[168,720]{1,0:T(8,128)(2,1)S(1)}, u32[]{:S(2)}, u32[]{:S(2)}) collective-permute-start(bf16[168,720]{1,0:T(8,128)(2,1)S(1)} %slice.22), channel_id=1, source_target_pairs={{0,8},{4,12},{8,0},{12,4},{16,24},{20,28},{24,16},{28,20},{1,9},{5... | collective-permute-start | bytes 725768 | tf_op jit(solution)/shard_map/ppermute | solution.py:409
  28.7 0.0 copy-start.6
  28.7 1.5 %collective-permute-start.3 = (bf16[192,720]{1,0:T(8,128)(2,1)S(1)}, bf16[192,720]{1,0:T(8,128)(2,1)S(1)}, u32[]{:S(2)}, u32[]{:S(2)}) collective-permute-start(bf16[192,720]{1,0:T(8,128)(2,1)S(1)} %slice.21), channel_id=1, source_target_pairs={{0,4},{4,0},{8,12},{12,8},{16,20},{20,16},{24,28},{28,24},{1,5},{5... | collective-permute-start | bytes 829448 | tf_op jit(solution)/shard_map/ppermute | solution.py:409
  30.2 4.2 %train_gradients.3.refs_1_ = f32[8,4,40,720]{3,2,1,0:T(8,128)S(1)} custom-call(bf16[320,160]{1,0:T(8,128)(2,1)S(1)} %get-tuple-element.62.basis_ref, bf16[8,8,64,320]{3,2,1,0:T(8,128)(2,1)S(1)} %copy-done.4, bf16[8,8,64,320]{3,2,1,0:T(8,128)(2,1)S(1)} %copy-done.5), custom_call_target="tpu_custom_call" | custom-call | flops 10000000000 | bytes 1000 | tf_op jit(solution)/shard_map/train_gradients/pallas_call | solution.py:201
  34.4 1.9 %copy-done.2 = f32[8,4,40,720]{3,2,1,0:T(8,128)} copy-done((f32[8,4,40,720]{3,2,1,0:T(8,128)}, f32[8,4,40,720]{3,2,1,0:T(8,128)S(1)}, u32[]{:S(2)}) %copy-start.2) | copy-done | bytes 3686424
  36.3 0.0 collective-permute-done.5.refs_1_
  36.3 0.5 collective-permute-done.3.refs_3_.refs_5_
  36.8 0.5 collective-permute-start.7
  37.3 0.0 collective-permute-start.8
  37.3 0.5 collective-permute-start.9
  37.8 0.3 merge.1
  38.2 3.1 %collective-permute-start.10 = (s16[40,768]{1,0:T(8,128)(2,1)S(1)}, s16[40,768]{1,0:T(8,128)(2,1)S(1)}, u32[]{:S(2)}, u32[]{:S(2)}) collective-permute-start(s16[40,768]{1,0:T(8,128)(2,1)S(1)} %get-tuple-element.72), channel_id=1, source_target_pairs={{0,2},{1,3},{2,0},{3,1},{4,6},{5,7},{6,4},{7,5},{8,10},{9,11},{10,... | collective-permute-start | bytes 184328 | tf_op jit(solution)/shard_map/ppermute | solution.py:412
  41.3 2.2 %collective-permute-done.10.other_ref = s16[40,768]{1,0:T(8,128)(2,1)S(1)} collective-permute-done((s16[40,768]{1,0:T(8,128)(2,1)S(1)}, s16[40,768]{1,0:T(8,128)(2,1)S(1)}, u32[]{:S(2)}, u32[]{:S(2)}) %collective-permute-start.10) | collective-permute-done | bytes 61472 | tf_op jit(solution)/shard_map/ppermute | solution.py:412
  43.5 0.0 collective-permute-done.6.refs_6_.refs_8_
  43.5 0.0 collective-permute-done.7.refs_7_.refs_9_
  43.5 1.2 %project.1.own_ref = s16[2,40,768]{2,1,0:T(8,128)(2,1)S(1)} custom-call(f32[40,720]{1,0:T(8,128)S(1)} %get-tuple-element.73.own_ref, s16[40,768]{1,0:T(8,128)(2,1)S(1)} %collective-permute-done.10.other_ref, bf16[360,720]{1,0:T(8,128)(2,1)S(1)} %copy-done.6, bf16[360,720]{1,0:T(8,128)(2,1)S(1)} %collective-permute-done.refs_1_.refs_3_, ...), custom_call_target="tpu_custom_call" | custom-call | flops 1000 | bytes 1000 | tf_op jit(solution)/shard_map/project/pallas_call | solution.py:263
  44.7 2.4 %collective-permute-start.11 = (s16[2,40,768]{2,1,0:T(8,128)(2,1)S(1)}, s16[2,40,768]{2,1,0:T(8,128)(2,1)S(1)}, u32[]{:S(2)}, u32[]{:S(2)}) collective-permute-start(s16[2,40,768]{2,1,0:T(8,128)(2,1)S(1)} %project.1.own_ref), channel_id=1, source_target_pairs={{0,16},{4,20},{8,24},{12,28},{16,0},{20,4},{24,8},{28,12},{1,17},{... | collective-permute-start | bytes 368648 | tf_op jit(solution)/shard_map/ppermute | solution.py:409
  47.2 5.9 %collective-permute-done.11.other_ref = s16[2,40,768]{2,1,0:T(8,128)(2,1)S(1)} collective-permute-done((s16[2,40,768]{2,1,0:T(8,128)(2,1)S(1)}, s16[2,40,768]{2,1,0:T(8,128)(2,1)S(1)}, u32[]{:S(2)}, u32[]{:S(2)}) %collective-permute-start.11) | collective-permute-done | bytes 122912 | tf_op jit(solution)/shard_map/ppermute | solution.py:409
  53.1 2.8 %project_back.1 = (s16[2,40,768]{2,1,0:T(8,128)(2,1)S(1)}, s16[40,768]{1,0:T(8,128)(2,1)S(1)}, s16[40,768]{1,0:T(8,128)(2,1)S(1)}) custom-call(s16[2,40,768]{2,1,0:T(8,128)(2,1)S(1)} %project.1.own_ref, s16[2,40,768]{2,1,0:T(8,128)(2,1)S(1)} %collective-permute-done.11.other_ref, f32[40,720]{1,0:T(8,128)S(1)} %get-tuple-element.89.refs_0_, ...), custom_call_target="tpu_custom_call" | custom-call | flops 1000 | bytes 1000 | tf_op jit(solution)/shard_map/project_back/pallas_call | solution.py:315
  55.9 1.4 %collective-permute-start.12 = (s16[40,768]{1,0:T(8,128)(2,1)S(1)}, s16[40,768]{1,0:T(8,128)(2,1)S(1)}, u32[]{:S(2)}, u32[]{:S(2)}) collective-permute-start(s16[40,768]{1,0:T(8,128)(2,1)S(1)} %get-tuple-element.92), channel_id=1, source_target_pairs={{0,2},{1,3},{2,0},{3,1},{4,6},{5,7},{6,4},{7,5},{8,10},{9,11},{10,... | collective-permute-start | bytes 184328 | tf_op jit(solution)/shard_map/ppermute | solution.py:412
  57.4 0.1 collective-permute-start.13
  57.4 2.8 %collective-permute-done.12 = s16[40,768]{1,0:T(8,128)(2,1)S(1)} collective-permute-done((s16[40,768]{1,0:T(8,128)(2,1)S(1)}, s16[40,768]{1,0:T(8,128)(2,1)S(1)}, u32[]{:S(2)}, u32[]{:S(2)}) %collective-permute-start.12) | collective-permute-done | bytes 61472 | tf_op jit(solution)/shard_map/ppermute | solution.py:412
  60.2 0.0 collective-permute-done.13
  60.2 0.6 collective-permute-start.17
  60.8 0.2 fusion.4
  61.1 0.1 select_convert_fusion
  61.2 2.4 %collective-permute-start.16 = (s16[40,768]{1,0:T(8,128)(2,1)S(1)}, s16[40,768]{1,0:T(8,128)(2,1)S(1)}, u32[]{:S(2)}, u32[]{:S(2)}) collective-permute-start(s16[40,768]{1,0:T(8,128)(2,1)S(1)} %select_convert_fusion), channel_id=1, source_target_pairs={{0,24},{4,28},{8,16},{12,20},{16,8},{20,12},{24,0},{28,4},{1,25},{... | collective-permute-start | bytes 184328 | tf_op jit(solution)/shard_map/ppermute | solution.py:409
  63.6 2.0 %collective-permute-start.14 = (s16[40,768]{1,0:T(8,128)(2,1)S(1)}, s16[40,768]{1,0:T(8,128)(2,1)S(1)}, u32[]{:S(2)}, u32[]{:S(2)}) collective-permute-start(s16[40,768]{1,0:T(8,128)(2,1)S(1)} %select_convert_fusion), channel_id=1, source_target_pairs={{0,8},{4,12},{8,0},{12,4},{16,24},{20,28},{24,16},{28,20},{1,9},{5... | collective-permute-start | bytes 184328 | tf_op jit(solution)/shard_map/ppermute | solution.py:409
  65.7 2.2 %collective-permute-done.16 = s16[40,768]{1,0:T(8,128)(2,1)S(1)} collective-permute-done((s16[40,768]{1,0:T(8,128)(2,1)S(1)}, s16[40,768]{1,0:T(8,128)(2,1)S(1)}, u32[]{:S(2)}, u32[]{:S(2)}) %collective-permute-start.16) | collective-permute-done | bytes 61472 | tf_op jit(solution)/shard_map/ppermute | solution.py:409
  67.8 1.5 %collective-permute-done.15 = s16[40,768]{1,0:T(8,128)(2,1)S(1)} collective-permute-done((s16[40,768]{1,0:T(8,128)(2,1)S(1)}, s16[40,768]{1,0:T(8,128)(2,1)S(1)}, u32[]{:S(2)}, u32[]{:S(2)}) %collective-permute-start.15) | collective-permute-done | bytes 61472 | tf_op jit(solution)/shard_map/ppermute | solution.py:409
  69.3 0.0 collective-permute-done.14
  69.3 0.0 collective-permute-done.17
  69.3 1.0 %collective-permute-start.19 = (s16[2,2,40,768]{3,2,1,0:T(8,128)(2,1)S(1)}, s16[2,2,40,768]{3,2,1,0:T(8,128)(2,1)S(1)}, u32[]{:S(2)}, u32[]{:S(2)}) collective-permute-start(s16[2,2,40,768]{3,2,1,0:T(8,128)(2,1)S(1)} %pad_add_fusion.1.refs_0_), channel_id=1, source_target_pairs={{0,8},{4,12},{8,0},{12,4},{16,24},{20,28},{24,16},{28,20},{1,9},{5... | collective-permute-start | bytes 737288 | tf_op jit(solution)/shard_map/ppermute | solution.py:409
  70.4 0.0 copy-start.10
  70.4 1.6 %collective-permute-start.18 = (s16[4,40,768]{2,1,0:T(8,128)(2,1)S(1)}, s16[4,40,768]{2,1,0:T(8,128)(2,1)S(1)}, u32[]{:S(2)}, u32[]{:S(2)}) collective-permute-start(s16[4,40,768]{2,1,0:T(8,128)(2,1)S(1)} %pad_add_fusion.even_ref), channel_id=1, source_target_pairs={{0,4},{4,0},{8,12},{12,8},{16,20},{20,16},{24,28},{28,24},{1,5},{5... | collective-permute-start | bytes 737288 | tf_op jit(solution)/shard_map/ppermute | solution.py:409
  72.0 3.6 %collective-permute-done.19.refs_1_ = s16[2,2,40,768]{3,2,1,0:T(8,128)(2,1)S(1)} collective-permute-done((s16[2,2,40,768]{3,2,1,0:T(8,128)(2,1)S(1)}, s16[2,2,40,768]{3,2,1,0:T(8,128)(2,1)S(1)}, u32[]{:S(2)}, u32[]{:S(2)}) %collective-permute-start.19) | collective-permute-done | bytes 245792 | tf_op jit(solution)/shard_map/ppermute | solution.py:409
  75.6 1.1 %collective-permute-done.18.odd_ref = s16[4,40,768]{2,1,0:T(8,128)(2,1)S(1)} collective-permute-done((s16[4,40,768]{2,1,0:T(8,128)(2,1)S(1)}, s16[4,40,768]{2,1,0:T(8,128)(2,1)S(1)}, u32[]{:S(2)}, u32[]{:S(2)}) %collective-permute-start.18) | collective-permute-done | bytes 245792 | tf_op jit(solution)/shard_map/ppermute | solution.py:409
  76.7 1.5 %score_products.1 = f32[8,128]{1,0:T(8,128)S(1)} custom-call(s16[4,40,768]{2,1,0:T(8,128)(2,1)S(1)} %pad_add_fusion.even_ref, s16[4,40,768]{2,1,0:T(8,128)(2,1)S(1)} %collective-permute-done.18.odd_ref, f32[8,4,40,720]{3,2,1,0:T(8,128)S(1)} %copy-done.1, f32[8,4,40,720]{3,2,1,0:T(8,128)S(1)} %copy-done.3), custom_call_target="tpu_custom_call" | custom-call | flops 1000 | bytes 1000 | tf_op jit(solution)/shard_map/score_products/pallas_call | solution.py:347
  78.1 0.1 slice_reduce_fusion
  78.2 0.1 collective-permute-start.22
  78.3 2.1 %collective-permute-start.21 = (f32[8]{0:T(128)S(1)}, f32[8]{0:T(128)S(1)}, u32[]{:S(2)}, u32[]{:S(2)}) collective-permute-start(f32[8]{0:T(128)S(1)} %slice_reduce_fusion), channel_id=1, source_target_pairs={{0,2},{1,3},{2,0},{3,1},{4,6},{5,7},{6,4},{7,5},{8,10},{9,11},{10,... | collective-permute-start | bytes 104 | tf_op jit(solution)/shard_map/ppermute | solution.py:412
  80.4 0.0 collective-permute-start.20
  80.4 1.2 %output_rows.1 = f32[2,4,40,720]{3,2,1,0:T(8,128)} custom-call(s16[2,2,40,768]{3,2,1,0:T(8,128)(2,1)S(1)} %pad_add_fusion.1.refs_0_, s16[2,2,40,768]{3,2,1,0:T(8,128)(2,1)S(1)} %collective-permute-done.19.refs_1_), custom_call_target="tpu_custom_call" | custom-call | flops 1000 | bytes 1000 | tf_op jit(solution)/shard_map/output_rows/pallas_call | solution.py:371
  81.6 0.0 collective-permute-done.22
  81.6 0.3 collective-permute-done.21
  81.9 0.0 collective-permute-done.20
  81.9 0.6 multiply_multiply_fusion
  (26 shorter events, 0.1 us)
Async XLA Ops:
  0.6 25.9 %collective-permute-start.1 = (bf16[360,720]{1,0:T(8,128)(2,1)}, bf16[360,720]{1,0:T(8,128)(2,1)S(1)}, u32[]{:S(2)}, u32[]{:S(2)}) collective-permute-start(bf16[360,720]{1,0:T(8,128)(2,1)} %refs_2_), channel_id=1, source_target_pairs={{0,8},{4,12},{8,0},{12,4},{16,24},{20,28},{24,16},{28,20},{1,9},{5... | collective-permute-start | bytes 1555208 | tf_op jit(solution)/shard_map/ppermute | solution.py:409
  3.7 22.8 %collective-permute-start = (bf16[360,720]{1,0:T(8,128)(2,1)}, bf16[360,720]{1,0:T(8,128)(2,1)S(1)}, u32[]{:S(2)}, u32[]{:S(2)}) collective-permute-start(bf16[360,720]{1,0:T(8,128)(2,1)} %refs_2_), channel_id=1, source_target_pairs={{0,4},{4,0},{8,12},{12,8},{16,20},{20,16},{24,28},{28,24},{1,5},{5... | collective-permute-start | bytes 1555208 | tf_op jit(solution)/shard_map/ppermute | solution.py:409
  5.2 21.3 %collective-permute-start.2 = (bf16[360,720]{1,0:T(8,128)(2,1)}, bf16[360,720]{1,0:T(8,128)(2,1)S(1)}, u32[]{:S(2)}, u32[]{:S(2)}) collective-permute-start(bf16[360,720]{1,0:T(8,128)(2,1)} %refs_2_), channel_id=1, source_target_pairs={{0,1},{1,0},{2,3},{3,2},{4,5},{5,4},{6,7},{7,6},{8,9},{9,8},{10,11... | collective-permute-start | bytes 1555208 | tf_op jit(solution)/shard_map/ppermute | solution.py:412
  6.9 29.4 %collective-permute-start.5 = (f32[40,720]{1,0:T(8,128)}, f32[40,720]{1,0:T(8,128)}, u32[]{:S(2)}, u32[]{:S(2)}) collective-permute-start(f32[40,720]{1,0:T(8,128)} %get-tuple-element.113), channel_id=1, source_target_pairs={{0,1},{1,0},{2,3},{3,2},{4,5},{5,4},{6,7},{7,6},{8,9},{9,8},{10,11... | collective-permute-start | bytes 345608 | tf_op jit(solution)/shard_map/ppermute | solution.py:412
  7.4 1.0 %copy-start.7 = (bf16[1,8,64,320]{3,2,1,0:T(8,128)(2,1)S(1)}, bf16[1,8,64,320]{3,2,1,0:T(8,128)(2,1)}, u32[]{:S(2)}) copy-start(bf16[1,8,64,320]{3,2,1,0:T(8,128)(2,1)} %x_ref.3) | copy-start | bytes 983044
  8.4 1.0 %copy-start.8 = (bf16[1,8,64,320]{3,2,1,0:T(8,128)(2,1)S(1)}, bf16[1,8,64,320]{3,2,1,0:T(8,128)(2,1)}, u32[]{:S(2)}) copy-start(bf16[1,8,64,320]{3,2,1,0:T(8,128)(2,1)} %c_ref.3) | copy-start | bytes 983044
  9.4 0.9 %copy-start.9 = (bf16[320,320]{1,0:T(8,128)(2,1)S(1)}, bf16[320,320]{1,0:T(8,128)(2,1)}, u32[]{:S(2)}) copy-start(bf16[320,320]{1,0:T(8,128)(2,1)} %basis_ref.1) | copy-start | bytes 614404
  12.8 24.0 %all-to-all-start = ((s16[8,40,768]{2,1,0:T(8,128)(2,1)}), s16[8,40,768]{2,1,0:T(8,128)(2,1)S(1)}, u32[]{:S(2)}, u32[]{:S(2)}) async-start(s16[8,40,768]{2,1,0:T(8,128)(2,1)} %get-tuple-element.63), calls=%async_computation | async-start | bytes 983040 | tf_op jit(solution)/shard_map/all_to_all | solution.py:429
  16.7 1.9 %copy-start.4 = (bf16[8,8,64,320]{3,2,1,0:T(8,128)(2,1)S(1)}, bf16[8,8,64,320]{3,2,1,0:T(8,128)(2,1)}, u32[]{:S(2)}) copy-start(bf16[8,8,64,320]{3,2,1,0:T(8,128)(2,1)} %x_ref.5) | copy-start | bytes 7864324
  18.6 1.9 %copy-start.5 = (bf16[8,8,64,320]{3,2,1,0:T(8,128)(2,1)S(1)}, bf16[8,8,64,320]{3,2,1,0:T(8,128)(2,1)}, u32[]{:S(2)}) copy-start(bf16[8,8,64,320]{3,2,1,0:T(8,128)(2,1)} %c_ref.5) | copy-start | bytes 7864324
  24.6 1.9 %copy-start = (f32[8,4,40,720]{3,2,1,0:T(8,128)}, f32[8,4,40,720]{3,2,1,0:T(8,128)S(1)}, u32[]{:S(2)}) copy-start(f32[8,4,40,720]{3,2,1,0:T(8,128)S(1)} %train_gradients.2.refs_0_) | copy-start | bytes 11059204
  26.5 9.8 %collective-permute-start.4 = (bf16[168,720]{1,0:T(8,128)(2,1)S(1)}, bf16[168,720]{1,0:T(8,128)(2,1)S(1)}, u32[]{:S(2)}, u32[]{:S(2)}) collective-permute-start(bf16[168,720]{1,0:T(8,128)(2,1)S(1)} %slice.22), channel_id=1, source_target_pairs={{0,8},{4,12},{8,0},{12,4},{16,24},{20,28},{24,16},{28,20},{1,9},{5... | collective-permute-start | bytes 725768 | tf_op jit(solution)/shard_map/ppermute | solution.py:409
  28.7 14.9 %copy-start.6 = (bf16[360,720]{1,0:T(8,128)(2,1)S(1)}, bf16[360,720]{1,0:T(8,128)(2,1)}, u32[]{:S(2)}) copy-start(bf16[360,720]{1,0:T(8,128)(2,1)} %refs_2_) | copy-start | bytes 1555204
  28.7 8.2 %collective-permute-start.3 = (bf16[192,720]{1,0:T(8,128)(2,1)S(1)}, bf16[192,720]{1,0:T(8,128)(2,1)S(1)}, u32[]{:S(2)}, u32[]{:S(2)}) collective-permute-start(bf16[192,720]{1,0:T(8,128)(2,1)S(1)} %slice.21), channel_id=1, source_target_pairs={{0,4},{4,0},{8,12},{12,8},{16,20},{20,16},{24,28},{28,24},{1,5},{5... | collective-permute-start | bytes 829448 | tf_op jit(solution)/shard_map/ppermute | solution.py:409
  34.4 1.9 %copy-start.2 = (f32[8,4,40,720]{3,2,1,0:T(8,128)}, f32[8,4,40,720]{3,2,1,0:T(8,128)S(1)}, u32[]{:S(2)}) copy-start(f32[8,4,40,720]{3,2,1,0:T(8,128)S(1)} %train_gradients.3.refs_1_) | copy-start | bytes 11059204
  36.8 6.7 %collective-permute-start.6 = (bf16[360,720]{1,0:T(8,128)(2,1)S(1)}, bf16[360,720]{1,0:T(8,128)(2,1)S(1)}, u32[]{:S(2)}, u32[]{:S(2)}) collective-permute-start(bf16[360,720]{1,0:T(8,128)(2,1)S(1)} %collective-permute-done.refs_1_.refs_3_), channel_id=1, source_target_pairs={{0,1},{1,0},{2,3},{3,2},{4,5},{5,4},{6,7},{7,6},{8,9},{9,8},{10,11... | collective-permute-start | bytes 1555208 | tf_op jit(solution)/shard_map/ppermute | solution.py:412
  36.8 6.7 %collective-permute-start.7 = (bf16[360,720]{1,0:T(8,128)(2,1)S(1)}, bf16[360,720]{1,0:T(8,128)(2,1)S(1)}, u32[]{:S(2)}, u32[]{:S(2)}) collective-permute-start(bf16[360,720]{1,0:T(8,128)(2,1)S(1)} %collective-permute-done.1.refs_2_.refs_4_), channel_id=1, source_target_pairs={{0,1},{1,0},{2,3},{3,2},{4,5},{5,4},{6,7},{7,6},{8,9},{9,8},{10,11... | collective-permute-start | bytes 1555208 | tf_op jit(solution)/shard_map/ppermute | solution.py:412
  37.3 6.2 %collective-permute-start.8 = (bf16[192,720]{1,0:T(8,128)(2,1)S(1)}, bf16[192,720]{1,0:T(8,128)(2,1)S(1)}, u32[]{:S(2)}, u32[]{:S(2)}) collective-permute-start(bf16[192,720]{1,0:T(8,128)(2,1)S(1)} %collective-permute-done.3.refs_3_.refs_5_), channel_id=1, source_target_pairs={{0,1},{1,0},{2,3},{3,2},{4,5},{5,4},{6,7},{7,6},{8,9},{9,8},{10,11... | collective-permute-start | bytes 829448 | tf_op jit(solution)/shard_map/ppermute | solution.py:412
  37.3 6.2 %collective-permute-start.9 = (bf16[168,720]{1,0:T(8,128)(2,1)S(1)}, bf16[168,720]{1,0:T(8,128)(2,1)S(1)}, u32[]{:S(2)}, u32[]{:S(2)}) collective-permute-start(bf16[168,720]{1,0:T(8,128)(2,1)S(1)} %collective-permute-done.4.refs_4_.refs_6_), channel_id=1, source_target_pairs={{0,1},{1,0},{2,3},{3,2},{4,5},{5,4},{6,7},{7,6},{8,9},{9,8},{10,11... | collective-permute-start | bytes 725768 | tf_op jit(solution)/shard_map/ppermute | solution.py:412
  38.2 5.3 %collective-permute-start.10 = (s16[40,768]{1,0:T(8,128)(2,1)S(1)}, s16[40,768]{1,0:T(8,128)(2,1)S(1)}, u32[]{:S(2)}, u32[]{:S(2)}) collective-permute-start(s16[40,768]{1,0:T(8,128)(2,1)S(1)} %get-tuple-element.72), channel_id=1, source_target_pairs={{0,2},{1,3},{2,0},{3,1},{4,6},{5,7},{6,4},{7,5},{8,10},{9,11},{10,... | collective-permute-start | bytes 184328 | tf_op jit(solution)/shard_map/ppermute | solution.py:412
  43.5 33.1 %copy-start.3 = (f32[8,4,40,720]{3,2,1,0:T(8,128)S(1)}, f32[8,4,40,720]{3,2,1,0:T(8,128)}, u32[]{:S(2)}) copy-start(f32[8,4,40,720]{3,2,1,0:T(8,128)} %copy-done.2) | copy-start | bytes 11059204
  44.7 31.9 %copy-start.1 = (f32[8,4,40,720]{3,2,1,0:T(8,128)S(1)}, f32[8,4,40,720]{3,2,1,0:T(8,128)}, u32[]{:S(2)}) copy-start(f32[8,4,40,720]{3,2,1,0:T(8,128)} %copy-done) | copy-start | bytes 11059204
  44.7 8.4 %collective-permute-start.11 = (s16[2,40,768]{2,1,0:T(8,128)(2,1)S(1)}, s16[2,40,768]{2,1,0:T(8,128)(2,1)S(1)}, u32[]{:S(2)}, u32[]{:S(2)}) collective-permute-start(s16[2,40,768]{2,1,0:T(8,128)(2,1)S(1)} %project.1.own_ref), channel_id=1, source_target_pairs={{0,16},{4,20},{8,24},{12,28},{16,0},{20,4},{24,8},{28,12},{1,17},{... | collective-permute-start | bytes 368648 | tf_op jit(solution)/shard_map/ppermute | solution.py:409
  55.9 4.3 %collective-permute-start.12 = (s16[40,768]{1,0:T(8,128)(2,1)S(1)}, s16[40,768]{1,0:T(8,128)(2,1)S(1)}, u32[]{:S(2)}, u32[]{:S(2)}) collective-permute-start(s16[40,768]{1,0:T(8,128)(2,1)S(1)} %get-tuple-element.92), channel_id=1, source_target_pairs={{0,2},{1,3},{2,0},{3,1},{4,6},{5,7},{6,4},{7,5},{8,10},{9,11},{10,... | collective-permute-start | bytes 184328 | tf_op jit(solution)/shard_map/ppermute | solution.py:412
  57.4 2.9 %collective-permute-start.13 = (s16[40,768]{1,0:T(8,128)(2,1)S(1)}, s16[40,768]{1,0:T(8,128)(2,1)S(1)}, u32[]{:S(2)}, u32[]{:S(2)}) collective-permute-start(s16[40,768]{1,0:T(8,128)(2,1)S(1)} %get-tuple-element.115), channel_id=1, source_target_pairs={{0,1},{1,0},{2,3},{3,2},{4,5},{5,4},{6,7},{7,6},{8,9},{9,8},{10,11... | collective-permute-start | bytes 184328 | tf_op jit(solution)/shard_map/ppermute | solution.py:412
  60.2 9.1 %collective-permute-start.17 = (s16[2,40,768]{2,1,0:T(8,128)(2,1)S(1)}, s16[2,40,768]{2,1,0:T(8,128)(2,1)S(1)}, u32[]{:S(2)}, u32[]{:S(2)}) collective-permute-start(s16[2,40,768]{2,1,0:T(8,128)(2,1)S(1)} %pad_add_fusion.2), channel_id=1, source_target_pairs={{0,4},{4,0},{8,12},{12,8},{16,20},{20,16},{24,28},{28,24},{1,5},{5... | collective-permute-start | bytes 368648 | tf_op jit(solution)/shard_map/ppermute | solution.py:409
  61.2 6.6 %collective-permute-start.16 = (s16[40,768]{1,0:T(8,128)(2,1)S(1)}, s16[40,768]{1,0:T(8,128)(2,1)S(1)}, u32[]{:S(2)}, u32[]{:S(2)}) collective-permute-start(s16[40,768]{1,0:T(8,128)(2,1)S(1)} %select_convert_fusion), channel_id=1, source_target_pairs={{0,24},{4,28},{8,16},{12,20},{16,8},{20,12},{24,0},{28,4},{1,25},{... | collective-permute-start | bytes 184328 | tf_op jit(solution)/shard_map/ppermute | solution.py:409
  63.6 5.7 %collective-permute-start.15 = (s16[40,768]{1,0:T(8,128)(2,1)S(1)}, s16[40,768]{1,0:T(8,128)(2,1)S(1)}, u32[]{:S(2)}, u32[]{:S(2)}) collective-permute-start(s16[40,768]{1,0:T(8,128)(2,1)S(1)} %select_convert_fusion), channel_id=1, source_target_pairs={{0,16},{4,20},{8,24},{12,28},{16,0},{20,4},{24,8},{28,12},{1,17},{... | collective-permute-start | bytes 184328 | tf_op jit(solution)/shard_map/ppermute | solution.py:409
  63.6 5.7 %collective-permute-start.14 = (s16[40,768]{1,0:T(8,128)(2,1)S(1)}, s16[40,768]{1,0:T(8,128)(2,1)S(1)}, u32[]{:S(2)}, u32[]{:S(2)}) collective-permute-start(s16[40,768]{1,0:T(8,128)(2,1)S(1)} %select_convert_fusion), channel_id=1, source_target_pairs={{0,8},{4,12},{8,0},{12,4},{16,24},{20,28},{24,16},{28,20},{1,9},{5... | collective-permute-start | bytes 184328 | tf_op jit(solution)/shard_map/ppermute | solution.py:409
  69.3 6.3 %collective-permute-start.19 = (s16[2,2,40,768]{3,2,1,0:T(8,128)(2,1)S(1)}, s16[2,2,40,768]{3,2,1,0:T(8,128)(2,1)S(1)}, u32[]{:S(2)}, u32[]{:S(2)}) collective-permute-start(s16[2,2,40,768]{3,2,1,0:T(8,128)(2,1)S(1)} %pad_add_fusion.1.refs_0_), channel_id=1, source_target_pairs={{0,8},{4,12},{8,0},{12,4},{16,24},{20,28},{24,16},{28,20},{1,9},{5... | collective-permute-start | bytes 737288 | tf_op jit(solution)/shard_map/ppermute | solution.py:409
  70.4 11.5 %copy-start.10 = (s32[8]{0:T(128)S(1)}, s32[8]{0:T(128)}, u32[]{:S(2)}) copy-start(s32[8]{0:T(128)} %param.12) | copy-start | bytes 100
  70.4 6.3 %collective-permute-start.18 = (s16[4,40,768]{2,1,0:T(8,128)(2,1)S(1)}, s16[4,40,768]{2,1,0:T(8,128)(2,1)S(1)}, u32[]{:S(2)}, u32[]{:S(2)}) collective-permute-start(s16[4,40,768]{2,1,0:T(8,128)(2,1)S(1)} %pad_add_fusion.even_ref), channel_id=1, source_target_pairs={{0,4},{4,0},{8,12},{12,8},{16,20},{20,16},{24,28},{28,24},{1,5},{5... | collective-permute-start | bytes 737288 | tf_op jit(solution)/shard_map/ppermute | solution.py:409
  78.2 3.3 %collective-permute-start.22 = (f32[8]{0:T(128)S(1)}, f32[8]{0:T(128)S(1)}, u32[]{:S(2)}, u32[]{:S(2)}) collective-permute-start(f32[8]{0:T(128)S(1)} %slice_reduce_fusion), channel_id=1, source_target_pairs={{0,3},{1,2},{2,1},{3,0},{4,7},{5,6},{6,5},{7,4},{8,11},{9,10},{10,... | collective-permute-start | bytes 104 | tf_op jit(solution)/shard_map/ppermute | solution.py:412
  78.3 3.6 %collective-permute-start.21 = (f32[8]{0:T(128)S(1)}, f32[8]{0:T(128)S(1)}, u32[]{:S(2)}, u32[]{:S(2)}) collective-permute-start(f32[8]{0:T(128)S(1)} %slice_reduce_fusion), channel_id=1, source_target_pairs={{0,2},{1,3},{2,0},{3,1},{4,6},{5,7},{6,4},{7,5},{8,10},{9,11},{10,... | collective-permute-start | bytes 104 | tf_op jit(solution)/shard_map/ppermute | solution.py:412
  80.4 1.5 %collective-permute-start.20 = (f32[8]{0:T(128)S(1)}, f32[8]{0:T(128)S(1)}, u32[]{:S(2)}, u32[]{:S(2)}) collective-permute-start(f32[8]{0:T(128)S(1)} %slice_reduce_fusion), channel_id=1, source_target_pairs={{0,1},{1,0},{2,3},{3,2},{4,5},{5,4},{6,7},{7,6},{8,9},{9,8},{10,11... | collective-permute-start | bytes 104 | tf_op jit(solution)/shard_map/ppermute | solution.py:412

commit v3 on v2

--- a/solution.py
+++ b/solution.py
@@ -20,6 +20,14 @@
 mib = 2**20
 in_vmem = pl.BlockSpec(memory_space=pltpu.VMEM)
 anywhere = pl.BlockSpec(memory_space=pl.ANY)
+
+
+def in_space(array, space):
+    return pltpu.with_memory_space_constraint(array, space)
+
+
+def in_hbm(array):
+    return in_space(array, pltpu.HBM)
 
 
 def padded(size, unit):
@@ -168,7 +176,7 @@
         compiler_params=params(),
         cost_estimate=cheap(),
         name="query_gradient",
-    )(x, cot, basis)
+    )(in_hbm(x), in_hbm(cot), in_hbm(basis))
 
 
 def train_kernel(basis_ref, x_ref, c_ref, out_ref, *, parts):
@@ -203,11 +211,11 @@
         grid=(count,),
         in_specs=[pl.BlockSpec(chosen.shape, lambda i: (0, 0)), spec, spec],
         out_specs=pl.BlockSpec((shards, 1, high_rows, depth), lambda i: (0, i, 0, 0)),
-        out_shape=jax.ShapeDtypeStruct((shards, count, high_rows, depth), f32),
+        out_shape=pltpu.HBM((shards, count, high_rows, depth), f32),
         compiler_params=params(),
         cost_estimate=cheap(flops),
         name="train_gradients",
-    )(chosen, x, cot)
+    )(chosen, in_hbm(x), in_hbm(cot))
 
 
 def merge_kernel(arrived, keep_ref, send_ref):
@@ -428,7 +436,9 @@
     )
     arrived = lax.all_to_all(partial, "dp", 0, 0)
     trained = [train(0, chosen)]
-    blocks, near, trained, chosen = fence_blocks(blocks, near, trained, chosen)
+    blocks, near, trained, chosen, eigenvalues = fence_blocks(
+        blocks, near, trained, chosen, eigenvalues
+    )
 
     if groups > 3:
         blocks.append(((3, 0, 0, cut), swap(blocks[2][1][:cut], 1)))

time: 83.4 us -> 77.7 us (0.932)
  local copies, waits for them, and re-layouts: 12.3 us -> 1.84 us
  Pallas kernels: 17.8 us -> 22.8 us
  starting transfers between devices: 30.5 us -> 27.9 us
  waiting for transfers between devices: 20.2 us -> 22.5 us
    unnamed x22 -> x12, local copies, waits for them, and re-layouts: 10.5 us -> 0.7 us
    pallas_call x2, Pallas kernels: 8.36 us -> 13.1 us  [train_gradients(): pl.pallas_call(functools.partial(train_kernel, parts=parts), grid=(count,...]
    ppermute x12, starting transfers between devices: 8.26 us -> 6.15 us  [flip(): return lax.ppermute(array, 'factor', [(p, p ^ away) for p in range(factor)])]
    ppermute x11, waiting for transfers between devices: 14.8 us -> 16.4 us  [swap(): return lax.ppermute(array, 'dp', [(d, d ^ away) for d in range(shards)])]
    pallas_call x1, Pallas kernels: 2.47 us -> 3.65 us  [query_partial(): pl.pallas_call(functools.partial(query_kernel, groups=groups, parts=parts...]
    pallas_call x1, Pallas kernels: 2.81 us -> 1.95 us  [project_back(): pl.pallas_call(functools.partial(back_kernel, spots=spots, groups=groups,...]
  transfers between devices with their start and end apart: 24 -> 24, of which waited for: 9 -> 10; matrix products, arithmetic and copies ran while one was open for 3% -> 2% of each run, Pallas kernels for 15% -> 24%
where the time goes in v3:
time: 77.7 us; the launch traced here: 76.8 us
  starting transfers between devices  27.9 us (36%)
  Pallas kernels  22.8 us (29%)
  waiting for transfers between devices  22.5 us (29%)
  local copies, waits for them, and re-layouts  1.84 us (2%)
  other arithmetic  0.96 us (1%)
  between operations  0.8 us (1%)
    ppermute x11, starting transfers between devices, swap(): return lax.ppermute(array, 'dp', [(d, d ^ away) for d in range(shards)])  17.9 us
    ppermute x11, waiting for transfers between devices, swap(): return lax.ppermute(array, 'dp', [(d, d ^ away) for d in range(shards)])  16.4 us
    pallas_call x2, Pallas kernels, train_gradients(): pl.pallas_call(functools.partial(train_kernel, parts=parts), grid=(count,...  13.1 us
    ppermute x12, starting transfers between devices, flip(): return lax.ppermute(array, 'factor', [(p, p ^ away) for p in range(factor)])  6.15 us
    ppermute x12, waiting for transfers between devices, flip(): return lax.ppermute(array, 'factor', [(p, p ^ away) for p in range(factor)])  6.11 us
    all_to_all x1, starting transfers between devices, on_device(): arrived = lax.all_to_all(partial, 'dp', 0, 0)  3.86 us
    pallas_call x1, Pallas kernels, query_partial(): pl.pallas_call(functools.partial(query_kernel, groups=groups, parts=parts...  3.65 us
    pallas_call x1, Pallas kernels, project_back(): pl.pallas_call(functools.partial(back_kernel, spots=spots, groups=groups,...  1.95 us
  transfers between devices with their start and end apart: 24, of which 10 were waited for; matrix products, arithmetic and copies ran while one was open for 2% of the time, Pallas kernels for 24%

profile of v3, /device:TPU:0, one launch (start us, length us, event | category | flops | bytes accessed | tf_op | source)
XLA Modules:
  0.0 76.8 jit_solution(10571275292249390922)
XLA Ops:
  0.6 3.1 %collective-permute-start.1 = (bf16[360,720]{1,0:T(8,128)(2,1)}, bf16[360,720]{1,0:T(8,128)(2,1)S(1)}, u32[]{:S(2)}, u32[]{:S(2)}) collective-permute-start(bf16[360,720]{1,0:T(8,128)(2,1)} %refs_2_), channel_id=1, source_target_pairs={{0,8},{4,12},{8,0},{12,4},{16,24},{20,28},{24,16},{28,20},{1,9},{5... | collective-permute-start | bytes 1555208 | tf_op jit(solution)/shard_map/ppermute | solution.py:417
  3.7 1.5 %collective-permute-start = (bf16[360,720]{1,0:T(8,128)(2,1)}, bf16[360,720]{1,0:T(8,128)(2,1)S(1)}, u32[]{:S(2)}, u32[]{:S(2)}) collective-permute-start(bf16[360,720]{1,0:T(8,128)(2,1)} %refs_2_), channel_id=1, source_target_pairs={{0,4},{4,0},{8,12},{12,8},{16,20},{20,16},{24,28},{28,24},{1,5},{5... | collective-permute-start | bytes 1555208 | tf_op jit(solution)/shard_map/ppermute | solution.py:417
  5.2 0.0 collective-permute-start.2
  5.2 3.6 %query_gradient.1 = (s16[8,40,768]{2,1,0:T(8,128)(2,1)}, bf16[320,160]{1,0:T(8,128)(2,1)S(1)}) custom-call(bf16[1,8,64,320]{3,2,1,0:T(8,128)(2,1)} %x_ref.3, bf16[1,8,64,320]{3,2,1,0:T(8,128)(2,1)} %c_ref.3, bf16[320,320]{1,0:T(8,128)(2,1)} %basis_ref.1), custom_call_target="tpu_custom_call" | custom-call | flops 1000 | bytes 1000 | tf_op jit(solution)/shard_map/query_gradient/pallas_call | solution.py:165
  8.9 3.9 %all-to-all-start = ((s16[8,40,768]{2,1,0:T(8,128)(2,1)}), s16[8,40,768]{2,1,0:T(8,128)(2,1)S(1)}, u32[]{:S(2)}, u32[]{:S(2)}) async-start(s16[8,40,768]{2,1,0:T(8,128)(2,1)} %get-tuple-element.64), calls=%async_computation | async-start | bytes 983040 | tf_op jit(solution)/shard_map/all_to_all | solution.py:437
  12.8 6.6 %train_gradients.2.refs_0_ = f32[8,4,40,720]{3,2,1,0:T(8,128)} custom-call(bf16[320,160]{1,0:T(8,128)(2,1)S(1)} %get-tuple-element.63.basis_ref, bf16[8,8,64,320]{3,2,1,0:T(8,128)(2,1)} %x_ref.5, bf16[8,8,64,320]{3,2,1,0:T(8,128)(2,1)} %c_ref.5), custom_call_target="tpu_custom_call" | custom-call | flops 1000 | bytes 1000 | tf_op jit(solution)/shard_map/train_gradients/pallas_call | solution.py:209
  19.3 0.0 collective-permute-done.1.refs_2_.refs_4_
  19.3 1.8 %collective-permute-done.refs_1_.refs_3_ = bf16[360,720]{1,0:T(8,128)(2,1)S(1)} collective-permute-done((bf16[360,720]{1,0:T(8,128)(2,1)}, bf16[360,720]{1,0:T(8,128)(2,1)S(1)}, u32[]{:S(2)}, u32[]{:S(2)}) %collective-permute-start) | collective-permute-done | bytes 518432 | tf_op jit(solution)/shard_map/ppermute | solution.py:417
  21.1 0.0 collective-permute-done.2.refs_5_.refs_7_
  21.1 1.0 %constant_dynamic-slice_fusion = (f32[40,720]{1,0:T(8,128)S(1)}, f32[40,720]{1,0:T(8,128)S(1)}) fusion(f32[320,720]{1,0:T(8,128)} %param.15, s32[]{:T(128)S(6)} %select_n.24, s32[]{:T(128)S(6)} %select_n.23), kind=kLoop, calls=%fused_computation.20 | loop fusion | bytes 460808 | tf_op jit(solution)/shard_map/dynamic_slice | solution.py:450
  22.1 0.1 collective-permute-start.5
  22.2 0.3 collective-permute-start.4
  22.5 0.0 copy-start.2
  22.6 2.4 %collective-permute-start.3 = (bf16[192,720]{1,0:T(8,128)(2,1)S(1)}, bf16[192,720]{1,0:T(8,128)(2,1)S(1)}, u32[]{:S(2)}, u32[]{:S(2)}) collective-permute-start(bf16[192,720]{1,0:T(8,128)(2,1)S(1)} %slice.21), channel_id=1, source_target_pairs={{0,4},{4,0},{8,12},{12,8},{16,20},{20,16},{24,28},{28,24},{1,5},{5... | collective-permute-start | bytes 829448 | tf_op jit(solution)/shard_map/ppermute | solution.py:417
  24.9 6.6 %train_gradients.3.refs_1_ = f32[8,4,40,720]{3,2,1,0:T(8,128)} custom-call(bf16[320,160]{1,0:T(8,128)(2,1)S(1)} %get-tuple-element.63.basis_ref, bf16[8,8,64,320]{3,2,1,0:T(8,128)(2,1)} %x_ref.5, bf16[8,8,64,320]{3,2,1,0:T(8,128)(2,1)} %c_ref.5), custom_call_target="tpu_custom_call" | custom-call | flops 10000000000 | bytes 1000 | tf_op jit(solution)/shard_map/train_gradients/pallas_call | solution.py:209
  31.5 0.0 collective-permute-done.5.refs_1_
  31.5 0.7 copy-done.3
  32.2 0.0 collective-permute-done.4.refs_4_.refs_6_
  32.2 0.9 %collective-permute-done.3.refs_3_.refs_5_ = bf16[192,720]{1,0:T(8,128)(2,1)S(1)} collective-permute-done((bf16[192,720]{1,0:T(8,128)(2,1)S(1)}, bf16[192,720]{1,0:T(8,128)(2,1)S(1)}, u32[]{:S(2)}, u32[]{:S(2)}) %collective-permute-start.3) | collective-permute-done | bytes 276512 | tf_op jit(solution)/shard_map/ppermute | solution.py:417
  33.1 0.0 all-to-all-done.arrived
  33.1 0.0 collective-permute-start.6
  33.1 0.5 collective-permute-start.7
  33.6 0.0 collective-permute-start.8
  33.6 0.5 collective-permute-start.9
  34.1 0.3 merge.1
  34.5 1.5 %collective-permute-start.10 = (s16[40,768]{1,0:T(8,128)(2,1)S(1)}, s16[40,768]{1,0:T(8,128)(2,1)S(1)}, u32[]{:S(2)}, u32[]{:S(2)}) collective-permute-start(s16[40,768]{1,0:T(8,128)(2,1)S(1)} %get-tuple-element.74), channel_id=1, source_target_pairs={{0,2},{1,3},{2,0},{3,1},{4,6},{5,7},{6,4},{7,5},{8,10},{9,11},{10,... | collective-permute-start | bytes 184328 | tf_op jit(solution)/shard_map/ppermute | solution.py:420
  35.9 2.8 %collective-permute-done.10.other_ref = s16[40,768]{1,0:T(8,128)(2,1)S(1)} collective-permute-done((s16[40,768]{1,0:T(8,128)(2,1)S(1)}, s16[40,768]{1,0:T(8,128)(2,1)S(1)}, u32[]{:S(2)}, u32[]{:S(2)}) %collective-permute-start.10) | collective-permute-done | bytes 61472 | tf_op jit(solution)/shard_map/ppermute | solution.py:420
  38.7 0.0 collective-permute-done.9.refs_9_.refs_11_
  38.7 0.0 collective-permute-done.8.refs_8_.refs_10_
  38.7 0.0 collective-permute-done.6.refs_6_.refs_8_
  38.8 0.0 collective-permute-done.7.refs_7_.refs_9_
  38.8 1.2 %project.1.own_ref = s16[2,40,768]{2,1,0:T(8,128)(2,1)S(1)} custom-call(f32[40,720]{1,0:T(8,128)S(1)} %get-tuple-element.75.own_ref, s16[40,768]{1,0:T(8,128)(2,1)S(1)} %collective-permute-done.10.other_ref, bf16[360,720]{1,0:T(8,128)(2,1)S(1)} %copy-done.2, bf16[360,720]{1,0:T(8,128)(2,1)S(1)} %collective-permute-done.refs_1_.refs_3_, ...), custom_call_target="tpu_custom_call" | custom-call | flops 1000 | bytes 1000 | tf_op jit(solution)/shard_map/project/pallas_call | solution.py:271
  40.0 3.3 %collective-permute-start.11 = (s16[2,40,768]{2,1,0:T(8,128)(2,1)S(1)}, s16[2,40,768]{2,1,0:T(8,128)(2,1)S(1)}, u32[]{:S(2)}, u32[]{:S(2)}) collective-permute-start(s16[2,40,768]{2,1,0:T(8,128)(2,1)S(1)} %project.1.own_ref), channel_id=1, source_target_pairs={{0,16},{4,20},{8,24},{12,28},{16,0},{20,4},{24,8},{28,12},{1,17},{... | collective-permute-start | bytes 368648 | tf_op jit(solution)/shard_map/ppermute | solution.py:417
  43.3 5.0 %collective-permute-done.11.other_ref = s16[2,40,768]{2,1,0:T(8,128)(2,1)S(1)} collective-permute-done((s16[2,40,768]{2,1,0:T(8,128)(2,1)S(1)}, s16[2,40,768]{2,1,0:T(8,128)(2,1)S(1)}, u32[]{:S(2)}, u32[]{:S(2)}) %collective-permute-start.11) | collective-permute-done | bytes 122912 | tf_op jit(solution)/shard_map/ppermute | solution.py:417
  48.3 1.9 %project_back.1 = (s16[2,40,768]{2,1,0:T(8,128)(2,1)S(1)}, s16[40,768]{1,0:T(8,128)(2,1)S(1)}, s16[40,768]{1,0:T(8,128)(2,1)S(1)}) custom-call(s16[2,40,768]{2,1,0:T(8,128)(2,1)S(1)} %project.1.own_ref, s16[2,40,768]{2,1,0:T(8,128)(2,1)S(1)} %collective-permute-done.11.other_ref, f32[40,720]{1,0:T(8,128)S(1)} %get-tuple-element.91.refs_0_, ...), custom_call_target="tpu_custom_call" | custom-call | flops 1000 | bytes 1000 | tf_op jit(solution)/shard_map/project_back/pallas_call | solution.py:323
  50.3 1.2 %collective-permute-start.12 = (s16[40,768]{1,0:T(8,128)(2,1)S(1)}, s16[40,768]{1,0:T(8,128)(2,1)S(1)}, u32[]{:S(2)}, u32[]{:S(2)}) collective-permute-start(s16[40,768]{1,0:T(8,128)(2,1)S(1)} %get-tuple-element.94), channel_id=1, source_target_pairs={{0,2},{1,3},{2,0},{3,1},{4,6},{5,7},{6,4},{7,5},{8,10},{9,11},{10,... | collective-permute-start | bytes 184328 | tf_op jit(solution)/shard_map/ppermute | solution.py:420
  51.5 0.1 collective-permute-start.13
  51.6 2.9 %collective-permute-done.12 = s16[40,768]{1,0:T(8,128)(2,1)S(1)} collective-permute-done((s16[40,768]{1,0:T(8,128)(2,1)S(1)}, s16[40,768]{1,0:T(8,128)(2,1)S(1)}, u32[]{:S(2)}, u32[]{:S(2)}) %collective-permute-start.12) | collective-permute-done | bytes 61472 | tf_op jit(solution)/shard_map/ppermute | solution.py:420
  54.5 0.0 collective-permute-done.13
  54.6 0.9 %collective-permute-start.17 = (s16[2,40,768]{2,1,0:T(8,128)(2,1)S(1)}, s16[2,40,768]{2,1,0:T(8,128)(2,1)S(1)}, u32[]{:S(2)}, u32[]{:S(2)}) collective-permute-start(s16[2,40,768]{2,1,0:T(8,128)(2,1)S(1)} %pad_add_fusion.2), channel_id=1, source_target_pairs={{0,4},{4,0},{8,12},{12,8},{16,20},{20,16},{24,28},{28,24},{1,5},{5... | collective-permute-start | bytes 368648 | tf_op jit(solution)/shard_map/ppermute | solution.py:417
  55.4 0.2 fusion.4
  55.6 0.1 select_convert_fusion
  55.8 3.2 %collective-permute-start.16 = (s16[40,768]{1,0:T(8,128)(2,1)S(1)}, s16[40,768]{1,0:T(8,128)(2,1)S(1)}, u32[]{:S(2)}, u32[]{:S(2)}) collective-permute-start(s16[40,768]{1,0:T(8,128)(2,1)S(1)} %select_convert_fusion), channel_id=1, source_target_pairs={{0,24},{4,28},{8,16},{12,20},{16,8},{20,12},{24,0},{28,4},{1,25},{... | collective-permute-start | bytes 184328 | tf_op jit(solution)/shard_map/ppermute | solution.py:417
  59.0 0.0 collective-permute-start.15
  59.0 1.3 %collective-permute-start.14 = (s16[40,768]{1,0:T(8,128)(2,1)S(1)}, s16[40,768]{1,0:T(8,128)(2,1)S(1)}, u32[]{:S(2)}, u32[]{:S(2)}) collective-permute-start(s16[40,768]{1,0:T(8,128)(2,1)S(1)} %select_convert_fusion), channel_id=1, source_target_pairs={{0,8},{4,12},{8,0},{12,4},{16,24},{20,28},{24,16},{28,20},{1,9},{5... | collective-permute-start | bytes 184328 | tf_op jit(solution)/shard_map/ppermute | solution.py:417
  60.2 1.7 %collective-permute-done.16 = s16[40,768]{1,0:T(8,128)(2,1)S(1)} collective-permute-done((s16[40,768]{1,0:T(8,128)(2,1)S(1)}, s16[40,768]{1,0:T(8,128)(2,1)S(1)}, u32[]{:S(2)}, u32[]{:S(2)}) %collective-permute-start.16) | collective-permute-done | bytes 61472 | tf_op jit(solution)/shard_map/ppermute | solution.py:417
  62.0 2.1 %collective-permute-done.15 = s16[40,768]{1,0:T(8,128)(2,1)S(1)} collective-permute-done((s16[40,768]{1,0:T(8,128)(2,1)S(1)}, s16[40,768]{1,0:T(8,128)(2,1)S(1)}, u32[]{:S(2)}, u32[]{:S(2)}) %collective-permute-start.15) | collective-permute-done | bytes 61472 | tf_op jit(solution)/shard_map/ppermute | solution.py:417
  64.1 0.0 collective-permute-done.14
  64.1 0.0 collective-permute-done.17
  64.1 0.5 collective-permute-start.19
  64.7 0.0 copy-start.5
  64.7 1.5 %collective-permute-start.18 = (s16[4,40,768]{2,1,0:T(8,128)(2,1)S(1)}, s16[4,40,768]{2,1,0:T(8,128)(2,1)S(1)}, u32[]{:S(2)}, u32[]{:S(2)}) collective-permute-start(s16[4,40,768]{2,1,0:T(8,128)(2,1)S(1)} %pad_add_fusion.even_ref), channel_id=1, source_target_pairs={{0,4},{4,0},{8,12},{12,8},{16,20},{20,16},{24,28},{28,24},{1,5},{5... | collective-permute-start | bytes 737288 | tf_op jit(solution)/shard_map/ppermute | solution.py:417
  66.1 4.3 %collective-permute-done.19.refs_1_ = s16[2,2,40,768]{3,2,1,0:T(8,128)(2,1)S(1)} collective-permute-done((s16[2,2,40,768]{3,2,1,0:T(8,128)(2,1)S(1)}, s16[2,2,40,768]{3,2,1,0:T(8,128)(2,1)S(1)}, u32[]{:S(2)}, u32[]{:S(2)}) %collective-permute-start.19) | collective-permute-done | bytes 245792 | tf_op jit(solution)/shard_map/ppermute | solution.py:417
  70.4 0.6 collective-permute-done.18.odd_ref
  70.9 1.4 %score_products.1 = f32[8,128]{1,0:T(8,128)S(1)} custom-call(s16[4,40,768]{2,1,0:T(8,128)(2,1)S(1)} %pad_add_fusion.even_ref, s16[4,40,768]{2,1,0:T(8,128)(2,1)S(1)} %collective-permute-done.18.odd_ref, f32[8,4,40,720]{3,2,1,0:T(8,128)S(1)} %copy-done, f32[8,4,40,720]{3,2,1,0:T(8,128)S(1)} %copy-done.1), custom_call_target="tpu_custom_call" | custom-call | flops 1000 | bytes 1000 | tf_op jit(solution)/shard_map/score_products/pallas_call | solution.py:355
  72.4 0.1 slice_reduce_fusion
  72.5 0.1 collective-permute-start.22
  72.6 2.2 %collective-permute-start.21 = (f32[8]{0:T(128)S(1)}, f32[8]{0:T(128)S(1)}, u32[]{:S(2)}, u32[]{:S(2)}) collective-permute-start(f32[8]{0:T(128)S(1)} %slice_reduce_fusion), channel_id=1, source_target_pairs={{0,2},{1,3},{2,0},{3,1},{4,6},{5,7},{6,4},{7,5},{8,10},{9,11},{10,... | collective-permute-start | bytes 104 | tf_op jit(solution)/shard_map/ppermute | solution.py:420
  74.7 0.0 collective-permute-start.20
  74.8 1.2 %output_rows.1 = f32[2,4,40,720]{3,2,1,0:T(8,128)} custom-call(s16[2,2,40,768]{3,2,1,0:T(8,128)(2,1)S(1)} %pad_add_fusion.1.refs_0_, s16[2,2,40,768]{3,2,1,0:T(8,128)(2,1)S(1)} %collective-permute-done.19.refs_1_), custom_call_target="tpu_custom_call" | custom-call | flops 1000 | bytes 1000 | tf_op jit(solution)/shard_map/output_rows/pallas_call | solution.py:379
  75.9 0.0 collective-permute-done.22
  75.9 0.3 collective-permute-done.21
  76.2 0.0 collective-permute-done.20
  76.3 0.6 multiply_multiply_fusion
  (16 shorter events, 0.1 us)
Async XLA Ops:
  0.6 18.7 %collective-permute-start.1 = (bf16[360,720]{1,0:T(8,128)(2,1)}, bf16[360,720]{1,0:T(8,128)(2,1)S(1)}, u32[]{:S(2)}, u32[]{:S(2)}) collective-permute-start(bf16[360,720]{1,0:T(8,128)(2,1)} %refs_2_), channel_id=1, source_target_pairs={{0,8},{4,12},{8,0},{12,4},{16,24},{20,28},{24,16},{28,20},{1,9},{5... | collective-permute-start | bytes 1555208 | tf_op jit(solution)/shard_map/ppermute | solution.py:417
  3.7 17.4 %collective-permute-start = (bf16[360,720]{1,0:T(8,128)(2,1)}, bf16[360,720]{1,0:T(8,128)(2,1)S(1)}, u32[]{:S(2)}, u32[]{:S(2)}) collective-permute-start(bf16[360,720]{1,0:T(8,128)(2,1)} %refs_2_), channel_id=1, source_target_pairs={{0,4},{4,0},{8,12},{12,8},{16,20},{20,16},{24,28},{28,24},{1,5},{5... | collective-permute-start | bytes 1555208 | tf_op jit(solution)/shard_map/ppermute | solution.py:417
  5.2 15.9 %collective-permute-start.2 = (bf16[360,720]{1,0:T(8,128)(2,1)}, bf16[360,720]{1,0:T(8,128)(2,1)S(1)}, u32[]{:S(2)}, u32[]{:S(2)}) collective-permute-start(bf16[360,720]{1,0:T(8,128)(2,1)} %refs_2_), channel_id=1, source_target_pairs={{0,1},{1,0},{2,3},{3,2},{4,5},{5,4},{6,7},{7,6},{8,9},{9,8},{10,11... | collective-permute-start | bytes 1555208 | tf_op jit(solution)/shard_map/ppermute | solution.py:420
  8.9 24.2 %all-to-all-start = ((s16[8,40,768]{2,1,0:T(8,128)(2,1)}), s16[8,40,768]{2,1,0:T(8,128)(2,1)S(1)}, u32[]{:S(2)}, u32[]{:S(2)}) async-start(s16[8,40,768]{2,1,0:T(8,128)(2,1)} %get-tuple-element.64), calls=%async_computation | async-start | bytes 983040 | tf_op jit(solution)/shard_map/all_to_all | solution.py:437
  22.1 9.4 %collective-permute-start.5 = (f32[40,720]{1,0:T(8,128)S(1)}, f32[40,720]{1,0:T(8,128)S(1)}, u32[]{:S(2)}, u32[]{:S(2)}) collective-permute-start(f32[40,720]{1,0:T(8,128)S(1)} %get-tuple-element.115), channel_id=1, source_target_pairs={{0,1},{1,0},{2,3},{3,2},{4,5},{5,4},{6,7},{7,6},{8,9},{9,8},{10,11... | collective-permute-start | bytes 345608 | tf_op jit(solution)/shard_map/ppermute | solution.py:420
  22.2 9.9 %collective-permute-start.4 = (bf16[168,720]{1,0:T(8,128)(2,1)S(1)}, bf16[168,720]{1,0:T(8,128)(2,1)S(1)}, u32[]{:S(2)}, u32[]{:S(2)}) collective-permute-start(bf16[168,720]{1,0:T(8,128)(2,1)S(1)} %slice.22), channel_id=1, source_target_pairs={{0,8},{4,12},{8,0},{12,4},{16,24},{20,28},{24,16},{28,20},{1,9},{5... | collective-permute-start | bytes 725768 | tf_op jit(solution)/shard_map/ppermute | solution.py:417
  22.5 16.2 %copy-start.2 = (bf16[360,720]{1,0:T(8,128)(2,1)S(1)}, bf16[360,720]{1,0:T(8,128)(2,1)}, u32[]{:S(2)}) copy-start(bf16[360,720]{1,0:T(8,128)(2,1)} %refs_2_) | copy-start | bytes 1555204
  22.6 10.5 %collective-permute-start.3 = (bf16[192,720]{1,0:T(8,128)(2,1)S(1)}, bf16[192,720]{1,0:T(8,128)(2,1)S(1)}, u32[]{:S(2)}, u32[]{:S(2)}) collective-permute-start(bf16[192,720]{1,0:T(8,128)(2,1)S(1)} %slice.21), channel_id=1, source_target_pairs={{0,4},{4,0},{8,12},{12,8},{16,20},{20,16},{24,28},{28,24},{1,5},{5... | collective-permute-start | bytes 829448 | tf_op jit(solution)/shard_map/ppermute | solution.py:417
  31.5 0.7 copy-start.3
  32.2 16.1 %copy-start.4 = (f32[40,720]{1,0:T(8,128)S(1)}, f32[40,720]{1,0:T(8,128)}, u32[]{:S(2)}) copy-start(f32[40,720]{1,0:T(8,128)} %copy-done.3) | copy-start | bytes 345604
  33.1 5.7 %collective-permute-start.6 = (bf16[360,720]{1,0:T(8,128)(2,1)S(1)}, bf16[360,720]{1,0:T(8,128)(2,1)S(1)}, u32[]{:S(2)}, u32[]{:S(2)}) collective-permute-start(bf16[360,720]{1,0:T(8,128)(2,1)S(1)} %collective-permute-done.refs_1_.refs_3_), channel_id=1, source_target_pairs={{0,1},{1,0},{2,3},{3,2},{4,5},{5,4},{6,7},{7,6},{8,9},{9,8},{10,11... | collective-permute-start | bytes 1555208 | tf_op jit(solution)/shard_map/ppermute | solution.py:420
  33.1 5.7 %collective-permute-start.7 = (bf16[360,720]{1,0:T(8,128)(2,1)S(1)}, bf16[360,720]{1,0:T(8,128)(2,1)S(1)}, u32[]{:S(2)}, u32[]{:S(2)}) collective-permute-start(bf16[360,720]{1,0:T(8,128)(2,1)S(1)} %collective-permute-done.1.refs_2_.refs_4_), channel_id=1, source_target_pairs={{0,1},{1,0},{2,3},{3,2},{4,5},{5,4},{6,7},{7,6},{8,9},{9,8},{10,11... | collective-permute-start | bytes 1555208 | tf_op jit(solution)/shard_map/ppermute | solution.py:420
  33.6 5.1 %collective-permute-start.8 = (bf16[192,720]{1,0:T(8,128)(2,1)S(1)}, bf16[192,720]{1,0:T(8,128)(2,1)S(1)}, u32[]{:S(2)}, u32[]{:S(2)}) collective-permute-start(bf16[192,720]{1,0:T(8,128)(2,1)S(1)} %collective-permute-done.3.refs_3_.refs_5_), channel_id=1, source_target_pairs={{0,1},{1,0},{2,3},{3,2},{4,5},{5,4},{6,7},{7,6},{8,9},{9,8},{10,11... | collective-permute-start | bytes 829448 | tf_op jit(solution)/shard_map/ppermute | solution.py:420
  33.6 5.1 %collective-permute-start.9 = (bf16[168,720]{1,0:T(8,128)(2,1)S(1)}, bf16[168,720]{1,0:T(8,128)(2,1)S(1)}, u32[]{:S(2)}, u32[]{:S(2)}) collective-permute-start(bf16[168,720]{1,0:T(8,128)(2,1)S(1)} %collective-permute-done.4.refs_4_.refs_6_), channel_id=1, source_target_pairs={{0,1},{1,0},{2,3},{3,2},{4,5},{5,4},{6,7},{7,6},{8,9},{9,8},{10,11... | collective-permute-start | bytes 725768 | tf_op jit(solution)/shard_map/ppermute | solution.py:420
  34.5 4.3 %collective-permute-start.10 = (s16[40,768]{1,0:T(8,128)(2,1)S(1)}, s16[40,768]{1,0:T(8,128)(2,1)S(1)}, u32[]{:S(2)}, u32[]{:S(2)}) collective-permute-start(s16[40,768]{1,0:T(8,128)(2,1)S(1)} %get-tuple-element.74), channel_id=1, source_target_pairs={{0,2},{1,3},{2,0},{3,1},{4,6},{5,7},{6,4},{7,5},{8,10},{9,11},{10,... | collective-permute-start | bytes 184328 | tf_op jit(solution)/shard_map/ppermute | solution.py:420
  38.8 32.2 %copy-start.1 = (f32[8,4,40,720]{3,2,1,0:T(8,128)S(1)}, f32[8,4,40,720]{3,2,1,0:T(8,128)}, u32[]{:S(2)}) copy-start(f32[8,4,40,720]{3,2,1,0:T(8,128)} %train_gradients.3.refs_1_) | copy-start | bytes 11059204
  40.0 31.0 %copy-start = (f32[8,4,40,720]{3,2,1,0:T(8,128)S(1)}, f32[8,4,40,720]{3,2,1,0:T(8,128)}, u32[]{:S(2)}) copy-start(f32[8,4,40,720]{3,2,1,0:T(8,128)} %train_gradients.2.refs_0_) | copy-start | bytes 11059204
  40.0 8.3 %collective-permute-start.11 = (s16[2,40,768]{2,1,0:T(8,128)(2,1)S(1)}, s16[2,40,768]{2,1,0:T(8,128)(2,1)S(1)}, u32[]{:S(2)}, u32[]{:S(2)}) collective-permute-start(s16[2,40,768]{2,1,0:T(8,128)(2,1)S(1)} %project.1.own_ref), channel_id=1, source_target_pairs={{0,16},{4,20},{8,24},{12,28},{16,0},{20,4},{24,8},{28,12},{1,17},{... | collective-permute-start | bytes 368648 | tf_op jit(solution)/shard_map/ppermute | solution.py:417
  50.3 4.3 %collective-permute-start.12 = (s16[40,768]{1,0:T(8,128)(2,1)S(1)}, s16[40,768]{1,0:T(8,128)(2,1)S(1)}, u32[]{:S(2)}, u32[]{:S(2)}) collective-permute-start(s16[40,768]{1,0:T(8,128)(2,1)S(1)} %get-tuple-element.94), channel_id=1, source_target_pairs={{0,2},{1,3},{2,0},{3,1},{4,6},{5,7},{6,4},{7,5},{8,10},{9,11},{10,... | collective-permute-start | bytes 184328 | tf_op jit(solution)/shard_map/ppermute | solution.py:420
  51.5 3.0 %collective-permute-start.13 = (s16[40,768]{1,0:T(8,128)(2,1)S(1)}, s16[40,768]{1,0:T(8,128)(2,1)S(1)}, u32[]{:S(2)}, u32[]{:S(2)}) collective-permute-start(s16[40,768]{1,0:T(8,128)(2,1)S(1)} %get-tuple-element.117), channel_id=1, source_target_pairs={{0,1},{1,0},{2,3},{3,2},{4,5},{5,4},{6,7},{7,6},{8,9},{9,8},{10,11... | collective-permute-start | bytes 184328 | tf_op jit(solution)/shard_map/ppermute | solution.py:420
  54.6 9.5 %collective-permute-start.17 = (s16[2,40,768]{2,1,0:T(8,128)(2,1)S(1)}, s16[2,40,768]{2,1,0:T(8,128)(2,1)S(1)}, u32[]{:S(2)}, u32[]{:S(2)}) collective-permute-start(s16[2,40,768]{2,1,0:T(8,128)(2,1)S(1)} %pad_add_fusion.2), channel_id=1, source_target_pairs={{0,4},{4,0},{8,12},{12,8},{16,20},{20,16},{24,28},{28,24},{1,5},{5... | collective-permute-start | bytes 368648 | tf_op jit(solution)/shard_map/ppermute | solution.py:417
  55.8 6.2 %collective-permute-start.16 = (s16[40,768]{1,0:T(8,128)(2,1)S(1)}, s16[40,768]{1,0:T(8,128)(2,1)S(1)}, u32[]{:S(2)}, u32[]{:S(2)}) collective-permute-start(s16[40,768]{1,0:T(8,128)(2,1)S(1)} %select_convert_fusion), channel_id=1, source_target_pairs={{0,24},{4,28},{8,16},{12,20},{16,8},{20,12},{24,0},{28,4},{1,25},{... | collective-permute-start | bytes 184328 | tf_op jit(solution)/shard_map/ppermute | solution.py:417
  59.0 5.1 %collective-permute-start.15 = (s16[40,768]{1,0:T(8,128)(2,1)S(1)}, s16[40,768]{1,0:T(8,128)(2,1)S(1)}, u32[]{:S(2)}, u32[]{:S(2)}) collective-permute-start(s16[40,768]{1,0:T(8,128)(2,1)S(1)} %select_convert_fusion), channel_id=1, source_target_pairs={{0,16},{4,20},{8,24},{12,28},{16,0},{20,4},{24,8},{28,12},{1,17},{... | collective-permute-start | bytes 184328 | tf_op jit(solution)/shard_map/ppermute | solution.py:417
  59.0 5.1 %collective-permute-start.14 = (s16[40,768]{1,0:T(8,128)(2,1)S(1)}, s16[40,768]{1,0:T(8,128)(2,1)S(1)}, u32[]{:S(2)}, u32[]{:S(2)}) collective-permute-start(s16[40,768]{1,0:T(8,128)(2,1)S(1)} %select_convert_fusion), channel_id=1, source_target_pairs={{0,8},{4,12},{8,0},{12,4},{16,24},{20,28},{24,16},{28,20},{1,9},{5... | collective-permute-start | bytes 184328 | tf_op jit(solution)/shard_map/ppermute | solution.py:417
  64.1 6.3 %collective-permute-start.19 = (s16[2,2,40,768]{3,2,1,0:T(8,128)(2,1)S(1)}, s16[2,2,40,768]{3,2,1,0:T(8,128)(2,1)S(1)}, u32[]{:S(2)}, u32[]{:S(2)}) collective-permute-start(s16[2,2,40,768]{3,2,1,0:T(8,128)(2,1)S(1)} %pad_add_fusion.1.refs_0_), channel_id=1, source_target_pairs={{0,8},{4,12},{8,0},{12,4},{16,24},{20,28},{24,16},{28,20},{1,9},{5... | collective-permute-start | bytes 737288 | tf_op jit(solution)/shard_map/ppermute | solution.py:417
  64.7 11.6 %copy-start.5 = (s32[8]{0:T(128)S(1)}, s32[8]{0:T(128)}, u32[]{:S(2)}) copy-start(s32[8]{0:T(128)} %param.12) | copy-start | bytes 100
  64.7 6.3 %collective-permute-start.18 = (s16[4,40,768]{2,1,0:T(8,128)(2,1)S(1)}, s16[4,40,768]{2,1,0:T(8,128)(2,1)S(1)}, u32[]{:S(2)}, u32[]{:S(2)}) collective-permute-start(s16[4,40,768]{2,1,0:T(8,128)(2,1)S(1)} %pad_add_fusion.even_ref), channel_id=1, source_target_pairs={{0,4},{4,0},{8,12},{12,8},{16,20},{20,16},{24,28},{28,24},{1,5},{5... | collective-permute-start | bytes 737288 | tf_op jit(solution)/shard_map/ppermute | solution.py:417
  72.5 3.4 %collective-permute-start.22 = (f32[8]{0:T(128)S(1)}, f32[8]{0:T(128)S(1)}, u32[]{:S(2)}, u32[]{:S(2)}) collective-permute-start(f32[8]{0:T(128)S(1)} %slice_reduce_fusion), channel_id=1, source_target_pairs={{0,3},{1,2},{2,1},{3,0},{4,7},{5,6},{6,5},{7,4},{8,11},{9,10},{10,... | collective-permute-start | bytes 104 | tf_op jit(solution)/shard_map/ppermute | solution.py:420
  72.6 3.7 %collective-permute-start.21 = (f32[8]{0:T(128)S(1)}, f32[8]{0:T(128)S(1)}, u32[]{:S(2)}, u32[]{:S(2)}) collective-permute-start(f32[8]{0:T(128)S(1)} %slice_reduce_fusion), channel_id=1, source_target_pairs={{0,2},{1,3},{2,0},{3,1},{4,6},{5,7},{6,4},{7,5},{8,10},{9,11},{10,... | collective-permute-start | bytes 104 | tf_op jit(solution)/shard_map/ppermute | solution.py:420
  74.7 1.5 %collective-permute-start.20 = (f32[8]{0:T(128)S(1)}, f32[8]{0:T(128)S(1)}, u32[]{:S(2)}, u32[]{:S(2)}) collective-permute-start(f32[8]{0:T(128)S(1)} %slice_reduce_fusion), channel_id=1, source_target_pairs={{0,1},{1,0},{2,3},{3,2},{4,5},{5,4},{6,7},{7,6},{8,9},{9,8},{10,11... | collective-permute-start | bytes 104 | tf_op jit(solution)/shard_map/ppermute | solution.py:420

commit v4 on v3

--- a/solution.py
+++ b/solution.py
@@ -332,47 +332,45 @@
     )(own, other, *eigen, *pieces)
 
 
-def score_kernel(even_ref, odd_ref, *refs):
+def score_kernel(found, *refs, offset):
     grads, out = refs[:-1], refs[-1]
-    pairs = even_ref.shape[0]
-    count, high_rows, depth = grads[0].shape[1:]
+    high_rows, depth = grads[0].shape[2:]
     me = lax.axis_index("dp")
     blocks = []
-    for away in range(2 * pairs):
-        values = (odd_ref if away % 2 else even_ref)[away // 2]
-        blocks.append((jnp.bitwise_xor(me, away), decode(values, depth)))
-    for chunk, grad in enumerate(grads):
-        for item in range(count):
+    for pair in range(found.shape[0]):
+        at = jnp.bitwise_xor(me, 2 * pair + offset)
+        blocks.append((at, decode(found[pair], depth)))
+    line = 0
+    for grad in grads:
+        for item in range(grad.shape[1]):
             total = jnp.zeros((high_rows, depth), f32)
             for at, values in blocks:
                 total += grad[at, item] * values
             total = jnp.sum(jnp.sum(total, axis=0, keepdims=True), axis=1, keepdims=True)
-            at = chunk * count + item
-            out[at : at + 1, :] = jnp.broadcast_to(total, (1, out.shape[1]))
-
-
-def score_products(even, odd, grads):
-    return pl.pallas_call(
-        score_kernel,
-        in_specs=[in_vmem] * (2 + len(grads)),
+            out[line : line + 1, :] = jnp.broadcast_to(total, (1, out.shape[1]))
+            line += 1
+
+
+def score_products(found, grads, offset, flops):
+    return pl.pallas_call(
+        functools.partial(score_kernel, offset=offset),
+        in_specs=[in_vmem] * (1 + len(grads)),
         out_specs=in_vmem,
-        out_shape=jax.ShapeDtypeStruct((len(grads) * grads[0].shape[1], 128), f32),
-        compiler_params=params(),
-        cost_estimate=cheap(),
+        out_shape=jax.ShapeDtypeStruct((sum(grad.shape[1] for grad in grads), 128), f32),
+        compiler_params=params(),
+        cost_estimate=cheap(flops),
         name="score_products",
-    )(even, odd, *grads)
-
-
-def output_kernel(*refs):
-    found, out = refs[:-1], refs[-1]
+    )(found, *grads)
+
+
+def output_kernel(own_ref, *refs):
+    found, out = (own_ref,) + refs[:-1], refs[-1]
     parts, groups, own_rows, jump = out.shape
     _, group, _, part = position(groups, parts)
-    for pair in range(groups // 2):
-        for odd in range(2):
-            for away in range(parts):
-                value = decode(found[pair][odd, away], jump)
-                row = jnp.bitwise_xor(group, 2 * pair + odd)
-                out[jnp.bitwise_xor(part, away), row] = value[:own_rows]
+    for away in range(parts):
+        for row in range(groups):
+            value = decode(found[away][row], jump)
+            out[jnp.bitwise_xor(part, away), jnp.bitwise_xor(group, row)] = value[:own_rows]
 
 
 def output_rows(found, groups, parts, own_rows, jump):
@@ -407,9 +405,8 @@
     high_rows = padded(own_rows, 8)
     jump = input_basis.shape[1]
     group, part = lax.axis_index("dp") % groups, lax.axis_index("factor") % parts
-    early, late = 10**3, 10**10
     batch = train_inputs.shape[0]
-    chunks = 2 if batch % 2 == 0 else 1
+    bounds = [0, batch * 4 // 8, batch * 8 // 8, batch]
     rows = input_basis.shape[0]
     cut = padded(rows // 2, 16)
 
@@ -419,11 +416,14 @@
     def flip(array, away):
         return lax.ppermute(array, "factor", [(p, p ^ away) for p in range(factor)])
 
-    def train(chunk, chosen):
-        size = batch // chunks
-        return train_gradients(
-            chosen, train_inputs, train_cotangents, shards, parts, chunk * size, size, late if chunk else early
-        )
+    def train(chunk, chosen, flops=10**3):
+        first, last = bounds[chunk], bounds[chunk + 1]
+        if first == last:
+            return []
+        inputs = (train_inputs, train_cotangents)
+        return [
+            train_gradients(chosen, *inputs, shards, parts, first, last - first, flops)
+        ]
 
     blocks = [((0, 0, 0, rows), input_basis)]
     for away in range(1, groups):
@@ -435,7 +435,7 @@
         query_inputs, query_cotangents, output_basis, shards, groups, parts, own_rows, 1.0 / count
     )
     arrived = lax.all_to_all(partial, "dp", 0, 0)
-    trained = [train(0, chosen)]
+    trained = train(0, chosen)
     blocks, near, trained, chosen, eigenvalues = fence_blocks(
         blocks, near, trained, chosen, eigenvalues
     )
@@ -443,7 +443,7 @@
     if groups > 3:
         blocks.append(((3, 0, 0, cut), swap(blocks[2][1][:cut], 1)))
         blocks.append(((3, 0, cut, rows), swap(blocks[1][1][cut:], 2)))
-    trained += [train(chunk, chosen) for chunk in range(1, chunks)]
+    trained += train(1, chosen, 10**10)
     eigen = []
     for away in range(parts):
         start = ((part ^ away) * groups + group) * own_rows
@@ -451,14 +451,17 @@
         if high_rows > own_rows:
             lines = jnp.pad(lines, ((0, high_rows - own_rows), (0, 0)), constant_values=1.0)
         eigen.append(flip(lines, away) if away else lines)
-    blocks, near, trained, arrived, eigen = fence_blocks(blocks, near, trained, arrived, eigen)
+    blocks, near, trained, chosen, arrived, eigen = fence_blocks(
+        blocks, near, trained, chosen, arrived, eigen
+    )
 
     total, sent = merge(arrived, depth)
     other = flip(sent, parts)
     for away in range(1, parts):
         for (row, _, start, stop), piece in blocks[1:]:
             near.append(((row, away, start, stop), flip(piece, away)))
-    blocks, near, total, other = fence_blocks(blocks, near, total, other)
+    trained += train(2, chosen)
+    blocks, near, total, other, trained = fence_blocks(blocks, near, total, other, trained)
     blocks = blocks + near
 
     own = project(total, other, blocks, groups, parts)
@@ -467,8 +470,8 @@
 
     proj, keep, send = project_back(own, other, eigen, blocks, rows, groups, parts)
     other = flip(send, parts)
-    mine = [proj[0]] + [flip(proj[away], away) for away in range(1, parts)]
-    keep, other, mine = fence((keep, other, mine))
+    pair = [proj, swap(proj, 1)]
+    keep, other = fence((keep, other))
 
     power_keep = keep[:, depth : depth + 1].astype(f32)
     power_other = other[:, depth : depth + 1].astype(f32)
@@ -478,26 +481,26 @@
     marked = lax.broadcasted_iota(i32, keep.shape, 1) >= depth
     whole = jnp.where(marked, power, jnp.round(values)).astype(i16)
     even = [whole] + [swap(whole, away) for away in range(2, shards, 2)]
-    mine = jnp.stack(mine)
-    pair = [mine, swap(mine, 1)]
-    even, pair = fence((even, pair))
+    even, pair, timesteps = fence((even, pair, timesteps))
 
     even, pair = jnp.stack(even), jnp.stack(pair)
     odd = swap(even, 1)
     found = [pair] + [swap(pair, away) for away in range(2, groups, 2)]
-    even, odd, found = fence((even, odd, found))
-
-    sums = score_products(even, odd, trained)
+    phase = (timesteps.astype(f32) / 1000.0 + 0.008) / 1.008 * (math.pi / 2)
+    weight = jnp.sin(phase) * (1 / math.sqrt(channels * width))
+    sums = score_products(even, trained, 0, 10**10)
+    odd, found, sums, weight = fence((odd, found, sums, weight))
+
+    sums = sums + score_products(odd, trained, 1, 10**3)
+    found = jnp.concatenate(found)
     terms = [sums[:, 0]]
     terms += [flip(terms[0], away) for away in range(1, factor)]
+    rows_found = [found[:, 0]] + [flip(found[:, away], away) for away in range(1, parts)]
+    query_proj = output_rows(rows_found, groups, parts, own_rows, jump).reshape(channels, jump)
+    terms, query_proj = fence((terms, query_proj))
     while len(terms) > 1:
         terms = [terms[at] + terms[at + 1] for at in range(0, len(terms), 2)]
-    raw_scores = terms[0]
-    query_proj = output_rows(found, groups, parts, own_rows, jump).reshape(channels, jump)
-    phase = (timesteps.astype(f32) / 1000.0 + 0.008) / 1.008 * (math.pi / 2)
-    weight = jnp.sin(phase)
-    scores = raw_scores * weight / math.sqrt(channels * width)
-    return (scores, query_proj)
+    return (terms[0] * weight, query_proj)
 
 
 def solution(mesh):

time: 77.7 us -> 77.3 us (level)
    pallas_call x1 -> x2, Pallas kernels: 1.42 us -> 1.65 us  [score_products(): pl.pallas_call(functools.partial(score_kernel, offset=offset), in_specs=[...]
  transfers between devices with their start and end apart: 24 -> 24, of which waited for: 10 -> 10; matrix products, arithmetic and copies ran while one was open for 2% -> 2% of each run, Pallas kernels for 24% -> 26%
where the time goes in v4:
time: 77.3 us; the launch traced here: 76.8 us
  starting transfers between devices  28.2 us (36%)
  Pallas kernels  23 us (30%)
  waiting for transfers between devices  22 us (28%)
  local copies, waits for them, and re-layouts  1.9 us (2%)
  other arithmetic  0.97 us (1%)
  between operations  0.8 us (1%)
    ppermute x11, starting transfers between devices, swap(): return lax.ppermute(array, 'dp', [(d, d ^ away) for d in range(shards)])  18.2 us
    ppermute x11, waiting for transfers between devices, swap(): return lax.ppermute(array, 'dp', [(d, d ^ away) for d in range(shards)])  15.9 us
    pallas_call x2, Pallas kernels, train_gradients(): pl.pallas_call(functools.partial(train_kernel, parts=parts), grid=(count,...  13.1 us
    ppermute x12, starting transfers between devices, flip(): return lax.ppermute(array, 'factor', [(p, p ^ away) for p in range(factor)])  6.1 us
    ppermute x12, waiting for transfers between devices, flip(): return lax.ppermute(array, 'factor', [(p, p ^ away) for p in range(factor)])  6.08 us
    all_to_all x1, starting transfers between devices, on_device(): arrived = lax.all_to_all(partial, 'dp', 0, 0)  3.86 us
    pallas_call x1, Pallas kernels, query_partial(): pl.pallas_call(functools.partial(query_kernel, groups=groups, parts=parts...  3.65 us
    pallas_call x1, Pallas kernels, project_back(): pl.pallas_call(functools.partial(back_kernel, spots=spots, groups=groups,...  1.94 us
  transfers between devices with their start and end apart: 24, of which 10 were waited for; matrix products, arithmetic and copies ran while one was open for 2% of the time, Pallas kernels for 26%

profile of v4, /device:TPU:0, one launch (start us, length us, event | category | flops | bytes accessed | tf_op | source)
XLA Modules:
  0.0 76.8 jit_solution(14239821740769277222)
XLA Ops:
  0.6 3.1 %collective-permute-start.1 = (bf16[360,720]{1,0:T(8,128)(2,1)}, bf16[360,720]{1,0:T(8,128)(2,1)S(1)}, u32[]{:S(2)}, u32[]{:S(2)}) collective-permute-start(bf16[360,720]{1,0:T(8,128)(2,1)} %refs_2_), channel_id=1, source_target_pairs={{0,8},{4,12},{8,0},{12,4},{16,24},{20,28},{24,16},{28,20},{1,9},{5... | collective-permute-start | bytes 1555208 | tf_op jit(solution)/shard_map/ppermute | solution.py:414
  3.7 1.5 %collective-permute-start = (bf16[360,720]{1,0:T(8,128)(2,1)}, bf16[360,720]{1,0:T(8,128)(2,1)S(1)}, u32[]{:S(2)}, u32[]{:S(2)}) collective-permute-start(bf16[360,720]{1,0:T(8,128)(2,1)} %refs_2_), channel_id=1, source_target_pairs={{0,4},{4,0},{8,12},{12,8},{16,20},{20,16},{24,28},{28,24},{1,5},{5... | collective-permute-start | bytes 1555208 | tf_op jit(solution)/shard_map/ppermute | solution.py:414
  5.2 0.0 collective-permute-start.2
  5.2 3.6 %query_gradient.1 = (s16[8,40,768]{2,1,0:T(8,128)(2,1)}, bf16[320,160]{1,0:T(8,128)(2,1)S(1)}) custom-call(bf16[1,8,64,320]{3,2,1,0:T(8,128)(2,1)} %x_ref.3, bf16[1,8,64,320]{3,2,1,0:T(8,128)(2,1)} %c_ref.3, bf16[320,320]{1,0:T(8,128)(2,1)} %basis_ref.1), custom_call_target="tpu_custom_call" | custom-call | flops 1000 | bytes 1000 | tf_op jit(solution)/shard_map/query_gradient/pallas_call | solution.py:165
  8.9 3.9 %all-to-all-start = ((s16[8,40,768]{2,1,0:T(8,128)(2,1)}), s16[8,40,768]{2,1,0:T(8,128)(2,1)S(1)}, u32[]{:S(2)}, u32[]{:S(2)}) async-start(s16[8,40,768]{2,1,0:T(8,128)(2,1)} %get-tuple-element.71), calls=%async_computation | async-start | bytes 983040 | tf_op jit(solution)/shard_map/all_to_all | solution.py:437
  12.8 6.6 %train_gradients.2.refs_0_ = f32[8,4,40,720]{3,2,1,0:T(8,128)} custom-call(bf16[320,160]{1,0:T(8,128)(2,1)S(1)} %get-tuple-element.70.basis_ref, bf16[8,8,64,320]{3,2,1,0:T(8,128)(2,1)} %x_ref.5, bf16[8,8,64,320]{3,2,1,0:T(8,128)(2,1)} %c_ref.5), custom_call_target="tpu_custom_call" | custom-call | flops 1000 | bytes 1000 | tf_op jit(solution)/shard_map/train_gradients/pallas_call | solution.py:209
  19.3 0.0 collective-permute-done.1.refs_2_.refs_4_
  19.3 1.8 %collective-permute-done.refs_1_.refs_3_ = bf16[360,720]{1,0:T(8,128)(2,1)S(1)} collective-permute-done((bf16[360,720]{1,0:T(8,128)(2,1)}, bf16[360,720]{1,0:T(8,128)(2,1)S(1)}, u32[]{:S(2)}, u32[]{:S(2)}) %collective-permute-start) | collective-permute-done | bytes 518432 | tf_op jit(solution)/shard_map/ppermute | solution.py:414
  21.1 0.0 collective-permute-done.2.refs_5_.refs_7_
  21.1 1.0 %constant_dynamic-slice_fusion = (f32[40,720]{1,0:T(8,128)S(1)}, f32[40,720]{1,0:T(8,128)S(1)}) fusion(f32[320,720]{1,0:T(8,128)} %param.15, s32[]{:T(128)S(6)} %select_n.24, s32[]{:T(128)S(6)} %select_n.23), kind=kLoop, calls=%fused_computation.22 | loop fusion | bytes 460808 | tf_op jit(solution)/shard_map/dynamic_slice | solution.py:450
  22.1 0.1 collective-permute-start.5
  22.2 0.3 collective-permute-start.4
  22.5 0.0 copy-start.2
  22.6 2.4 %collective-permute-start.3 = (bf16[192,720]{1,0:T(8,128)(2,1)S(1)}, bf16[192,720]{1,0:T(8,128)(2,1)S(1)}, u32[]{:S(2)}, u32[]{:S(2)}) collective-permute-start(bf16[192,720]{1,0:T(8,128)(2,1)S(1)} %slice.21), channel_id=1, source_target_pairs={{0,4},{4,0},{8,12},{12,8},{16,20},{20,16},{24,28},{28,24},{1,5},{5... | collective-permute-start | bytes 829448 | tf_op jit(solution)/shard_map/ppermute | solution.py:414
  24.9 6.6 %train_gradients.3.refs_1_ = f32[8,4,40,720]{3,2,1,0:T(8,128)} custom-call(bf16[320,160]{1,0:T(8,128)(2,1)S(1)} %get-tuple-element.70.basis_ref, bf16[8,8,64,320]{3,2,1,0:T(8,128)(2,1)} %x_ref.5, bf16[8,8,64,320]{3,2,1,0:T(8,128)(2,1)} %c_ref.5), custom_call_target="tpu_custom_call" | custom-call | flops 10000000000 | bytes 1000 | tf_op jit(solution)/shard_map/train_gradients/pallas_call | solution.py:209
  31.5 0.0 collective-permute-done.5.refs_1_
  31.5 0.7 copy-done.3
  32.2 0.0 collective-permute-done.4.refs_4_.refs_6_
  32.2 0.9 %collective-permute-done.3.refs_3_.refs_5_ = bf16[192,720]{1,0:T(8,128)(2,1)S(1)} collective-permute-done((bf16[192,720]{1,0:T(8,128)(2,1)S(1)}, bf16[192,720]{1,0:T(8,128)(2,1)S(1)}, u32[]{:S(2)}, u32[]{:S(2)}) %collective-permute-start.3) | collective-permute-done | bytes 276512 | tf_op jit(solution)/shard_map/ppermute | solution.py:414
  33.1 0.0 all-to-all-done.arrived
  33.1 0.0 collective-permute-start.6
  33.1 0.5 collective-permute-start.7
  33.6 0.0 collective-permute-start.8
  33.6 0.5 collective-permute-start.9
  34.1 0.3 merge.1
  34.5 1.5 %collective-permute-start.10 = (s16[40,768]{1,0:T(8,128)(2,1)S(1)}, s16[40,768]{1,0:T(8,128)(2,1)S(1)}, u32[]{:S(2)}, u32[]{:S(2)}) collective-permute-start(s16[40,768]{1,0:T(8,128)(2,1)S(1)} %get-tuple-element.81), channel_id=1, source_target_pairs={{0,2},{1,3},{2,0},{3,1},{4,6},{5,7},{6,4},{7,5},{8,10},{9,11},{10,... | collective-permute-start | bytes 184328 | tf_op jit(solution)/shard_map/ppermute | solution.py:417
  35.9 2.8 %collective-permute-done.10.other_ref = s16[40,768]{1,0:T(8,128)(2,1)S(1)} collective-permute-done((s16[40,768]{1,0:T(8,128)(2,1)S(1)}, s16[40,768]{1,0:T(8,128)(2,1)S(1)}, u32[]{:S(2)}, u32[]{:S(2)}) %collective-permute-start.10) | collective-permute-done | bytes 61472 | tf_op jit(solution)/shard_map/ppermute | solution.py:417
  38.7 0.0 collective-permute-done.9.refs_9_.refs_11_
  38.7 0.0 collective-permute-done.8.refs_8_.refs_10_
  38.7 0.0 collective-permute-done.6.refs_6_.refs_8_
  38.8 0.0 collective-permute-done.7.refs_7_.refs_9_
  38.8 1.2 %project.1.own_ref = s16[2,40,768]{2,1,0:T(8,128)(2,1)S(1)} custom-call(f32[40,720]{1,0:T(8,128)S(1)} %get-tuple-element.84.own_ref, s16[40,768]{1,0:T(8,128)(2,1)S(1)} %collective-permute-done.10.other_ref, bf16[360,720]{1,0:T(8,128)(2,1)S(1)} %copy-done.2, bf16[360,720]{1,0:T(8,128)(2,1)S(1)} %collective-permute-done.refs_1_.refs_3_, ...), custom_call_target="tpu_custom_call" | custom-call | flops 1000 | bytes 1000 | tf_op jit(solution)/shard_map/project/pallas_call | solution.py:271
  40.0 3.3 %collective-permute-start.11 = (s16[2,40,768]{2,1,0:T(8,128)(2,1)S(1)}, s16[2,40,768]{2,1,0:T(8,128)(2,1)S(1)}, u32[]{:S(2)}, u32[]{:S(2)}) collective-permute-start(s16[2,40,768]{2,1,0:T(8,128)(2,1)S(1)} %project.1.own_ref), channel_id=1, source_target_pairs={{0,16},{4,20},{8,24},{12,28},{16,0},{20,4},{24,8},{28,12},{1,17},{... | collective-permute-start | bytes 368648 | tf_op jit(solution)/shard_map/ppermute | solution.py:414
  43.3 5.0 %collective-permute-done.11.other_ref = s16[2,40,768]{2,1,0:T(8,128)(2,1)S(1)} collective-permute-done((s16[2,40,768]{2,1,0:T(8,128)(2,1)S(1)}, s16[2,40,768]{2,1,0:T(8,128)(2,1)S(1)}, u32[]{:S(2)}, u32[]{:S(2)}) %collective-permute-start.11) | collective-permute-done | bytes 122912 | tf_op jit(solution)/shard_map/ppermute | solution.py:414
  48.3 1.9 %project_back.1 = (s16[2,40,768]{2,1,0:T(8,128)(2,1)S(1)}, s16[40,768]{1,0:T(8,128)(2,1)S(1)}, s16[40,768]{1,0:T(8,128)(2,1)S(1)}) custom-call(s16[2,40,768]{2,1,0:T(8,128)(2,1)S(1)} %project.1.own_ref, s16[2,40,768]{2,1,0:T(8,128)(2,1)S(1)} %collective-permute-done.11.other_ref, f32[40,720]{1,0:T(8,128)S(1)} %get-tuple-element.100.refs_0_, ...), custom_call_target="tpu_custom_call" | custom-call | flops 1000 | bytes 1000 | tf_op jit(solution)/shard_map/project_back/pallas_call | solution.py:323
  50.2 1.3 %collective-permute-start.12 = (s16[40,768]{1,0:T(8,128)(2,1)S(1)}, s16[40,768]{1,0:T(8,128)(2,1)S(1)}, u32[]{:S(2)}, u32[]{:S(2)}) collective-permute-start(s16[40,768]{1,0:T(8,128)(2,1)S(1)} %get-tuple-element.103), channel_id=1, source_target_pairs={{0,2},{1,3},{2,0},{3,1},{4,6},{5,7},{6,4},{7,5},{8,10},{9,11},{10,... | collective-permute-start | bytes 184328 | tf_op jit(solution)/shard_map/ppermute | solution.py:417
  51.5 1.1 %collective-permute-start.16 = (s16[2,40,768]{2,1,0:T(8,128)(2,1)S(1)}, s16[2,40,768]{2,1,0:T(8,128)(2,1)S(1)}, u32[]{:S(2)}, u32[]{:S(2)}) collective-permute-start(s16[2,40,768]{2,1,0:T(8,128)(2,1)S(1)} %get-tuple-element.111), channel_id=1, source_target_pairs={{0,4},{4,0},{8,12},{12,8},{16,20},{20,16},{24,28},{28,24},{1,5},{5... | collective-permute-start | bytes 368648 | tf_op jit(solution)/shard_map/ppermute | solution.py:414
  52.6 1.9 %collective-permute-done.12 = s16[40,768]{1,0:T(8,128)(2,1)S(1)} collective-permute-done((s16[40,768]{1,0:T(8,128)(2,1)S(1)}, s16[40,768]{1,0:T(8,128)(2,1)S(1)}, u32[]{:S(2)}, u32[]{:S(2)}) %collective-permute-start.12) | collective-permute-done | bytes 61472 | tf_op jit(solution)/shard_map/ppermute | solution.py:417
  54.5 0.2 fusion.4
  54.8 0.1 select_convert_fusion
  54.9 2.7 %collective-permute-start.15 = (s16[40,768]{1,0:T(8,128)(2,1)S(1)}, s16[40,768]{1,0:T(8,128)(2,1)S(1)}, u32[]{:S(2)}, u32[]{:S(2)}) collective-permute-start(s16[40,768]{1,0:T(8,128)(2,1)S(1)} %select_convert_fusion), channel_id=1, source_target_pairs={{0,24},{4,28},{8,16},{12,20},{16,8},{20,12},{24,0},{28,4},{1,25},{... | collective-permute-start | bytes 184328 | tf_op jit(solution)/shard_map/ppermute | solution.py:414
  57.6 0.0 collective-permute-start.14
  57.6 1.8 %collective-permute-start.13 = (s16[40,768]{1,0:T(8,128)(2,1)S(1)}, s16[40,768]{1,0:T(8,128)(2,1)S(1)}, u32[]{:S(2)}, u32[]{:S(2)}) collective-permute-start(s16[40,768]{1,0:T(8,128)(2,1)S(1)} %select_convert_fusion), channel_id=1, source_target_pairs={{0,8},{4,12},{8,0},{12,4},{16,24},{20,28},{24,16},{28,20},{1,9},{5... | collective-permute-start | bytes 184328 | tf_op jit(solution)/shard_map/ppermute | solution.py:414
  59.3 2.2 %collective-permute-done.15 = s16[40,768]{1,0:T(8,128)(2,1)S(1)} collective-permute-done((s16[40,768]{1,0:T(8,128)(2,1)S(1)}, s16[40,768]{1,0:T(8,128)(2,1)S(1)}, u32[]{:S(2)}, u32[]{:S(2)}) %collective-permute-start.15) | collective-permute-done | bytes 61472 | tf_op jit(solution)/shard_map/ppermute | solution.py:414
  61.6 1.2 %collective-permute-done.14 = s16[40,768]{1,0:T(8,128)(2,1)S(1)} collective-permute-done((s16[40,768]{1,0:T(8,128)(2,1)S(1)}, s16[40,768]{1,0:T(8,128)(2,1)S(1)}, u32[]{:S(2)}, u32[]{:S(2)}) %collective-permute-start.14) | collective-permute-done | bytes 61472 | tf_op jit(solution)/shard_map/ppermute | solution.py:414
  62.8 0.0 collective-permute-done.13
  62.8 0.0 collective-permute-done.16
  62.8 1.4 %collective-permute-start.18 = (s16[2,2,40,768]{3,2,0,1:T(8,128)(2,1)S(1)}, s16[2,2,40,768]{3,2,0,1:T(8,128)(2,1)S(1)}, u32[]{:S(2)}, u32[]{:S(2)}) collective-permute-start(s16[2,2,40,768]{3,2,0,1:T(8,128)(2,1)S(1)} %pad_add_fusion.1), channel_id=1, source_target_pairs={{0,8},{4,12},{8,0},{12,4},{16,24},{20,28},{24,16},{28,20},{1,9},{5... | collective-permute-start | bytes 737288 | tf_op jit(solution)/shard_map/ppermute | solution.py:414
  64.3 0.0 copy-start.5
  64.3 0.7 collective-permute-start.17
  65.0 0.8 %score_products.2 = f32[8,128]{1,0:T(8,128)S(1)} custom-call(s16[4,40,768]{2,1,0:T(8,128)(2,1)S(1)} %pad_add_fusion.found, f32[8,4,40,720]{3,2,1,0:T(8,128)S(1)} %copy-done, f32[8,4,40,720]{3,2,1,0:T(8,128)S(1)} %copy-done.1), custom_call_target="tpu_custom_call" | custom-call | flops 10000000000 | bytes 1000 | tf_op jit(solution)/shard_map/score_products/pallas_call | solution.py:355
  65.8 3.3 %collective-permute-done.18 = s16[2,2,40,768]{3,2,0,1:T(8,128)(2,1)S(1)} collective-permute-done((s16[2,2,40,768]{3,2,0,1:T(8,128)(2,1)S(1)}, s16[2,2,40,768]{3,2,0,1:T(8,128)(2,1)S(1)}, u32[]{:S(2)}, u32[]{:S(2)}) %collective-permute-start.18) | collective-permute-done | bytes 245792 | tf_op jit(solution)/shard_map/ppermute | solution.py:414
  69.1 1.4 %collective-permute-done.17.found = s16[4,40,768]{2,1,0:T(8,128)(2,1)S(1)} collective-permute-done((s16[4,40,768]{2,1,0:T(8,128)(2,1)S(1)}, s16[4,40,768]{2,1,0:T(8,128)(2,1)S(1)}, u32[]{:S(2)}, u32[]{:S(2)}) %collective-permute-start.17) | collective-permute-done | bytes 245792 | tf_op jit(solution)/shard_map/ppermute | solution.py:414
  70.6 0.1 collective-permute-start.22
  70.7 0.8 %score_products.3 = f32[8,128]{1,0:T(8,128)S(1)} custom-call(s16[4,40,768]{2,1,0:T(8,128)(2,1)S(1)} %collective-permute-done.17.found, f32[8,4,40,720]{3,2,1,0:T(8,128)S(1)} %copy-done, f32[8,4,40,720]{3,2,1,0:T(8,128)S(1)} %copy-done.1), custom_call_target="tpu_custom_call" | custom-call | flops 1000 | bytes 1000 | tf_op jit(solution)/shard_map/score_products/pallas_call | solution.py:355
  71.5 0.1 slice_reduce_fusion
  71.7 1.1 %collective-permute-start.21 = (f32[8]{0:T(128)S(1)}, f32[8]{0:T(128)S(1)}, u32[]{:S(2)}, u32[]{:S(2)}) collective-permute-start(f32[8]{0:T(128)S(1)} %slice_reduce_fusion), channel_id=1, source_target_pairs={{0,3},{1,2},{2,1},{3,0},{4,7},{5,6},{6,5},{7,4},{8,11},{9,10},{10,... | collective-permute-start | bytes 104 | tf_op jit(solution)/shard_map/ppermute | solution.py:417
  72.8 1.1 %collective-permute-start.20 = (f32[8]{0:T(128)S(1)}, f32[8]{0:T(128)S(1)}, u32[]{:S(2)}, u32[]{:S(2)}) collective-permute-start(f32[8]{0:T(128)S(1)} %slice_reduce_fusion), channel_id=1, source_target_pairs={{0,2},{1,3},{2,0},{3,1},{4,6},{5,7},{6,4},{7,5},{8,10},{9,11},{10,... | collective-permute-start | bytes 104 | tf_op jit(solution)/shard_map/ppermute | solution.py:417
  73.9 0.0 collective-permute-start.19
  73.9 1.2 %output_rows.1 = f32[2,4,40,720]{3,2,1,0:T(8,128)} custom-call(s16[4,40,768]{2,1,0:T(8,128)(2,1)S(1)} %get-tuple-element.132.own_ref, s16[4,40,768]{2,1,0:T(8,128)(2,1)S(1)} %collective-permute-done.22.refs_0_), custom_call_target="tpu_custom_call" | custom-call | flops 1000 | bytes 1000 | tf_op jit(solution)/shard_map/output_rows/pallas_call | solution.py:377
  75.0 0.0 collective-permute-done.21
  75.0 1.3 %collective-permute-done.20 = f32[8]{0:T(128)S(1)} collective-permute-done((f32[8]{0:T(128)S(1)}, f32[8]{0:T(128)S(1)}, u32[]{:S(2)}, u32[]{:S(2)}) %collective-permute-start.20) | collective-permute-done | bytes 64 | tf_op jit(solution)/shard_map/ppermute | solution.py:417
  76.3 0.0 collective-permute-done.19
  76.3 0.5 add_multiply_fusion
  (20 shorter events, 0.2 us)
Async XLA Ops:
  0.6 18.7 %collective-permute-start.1 = (bf16[360,720]{1,0:T(8,128)(2,1)}, bf16[360,720]{1,0:T(8,128)(2,1)S(1)}, u32[]{:S(2)}, u32[]{:S(2)}) collective-permute-start(bf16[360,720]{1,0:T(8,128)(2,1)} %refs_2_), channel_id=1, source_target_pairs={{0,8},{4,12},{8,0},{12,4},{16,24},{20,28},{24,16},{28,20},{1,9},{5... | collective-permute-start | bytes 1555208 | tf_op jit(solution)/shard_map/ppermute | solution.py:414
  3.7 17.4 %collective-permute-start = (bf16[360,720]{1,0:T(8,128)(2,1)}, bf16[360,720]{1,0:T(8,128)(2,1)S(1)}, u32[]{:S(2)}, u32[]{:S(2)}) collective-permute-start(bf16[360,720]{1,0:T(8,128)(2,1)} %refs_2_), channel_id=1, source_target_pairs={{0,4},{4,0},{8,12},{12,8},{16,20},{20,16},{24,28},{28,24},{1,5},{5... | collective-permute-start | bytes 1555208 | tf_op jit(solution)/shard_map/ppermute | solution.py:414
  5.2 15.9 %collective-permute-start.2 = (bf16[360,720]{1,0:T(8,128)(2,1)}, bf16[360,720]{1,0:T(8,128)(2,1)S(1)}, u32[]{:S(2)}, u32[]{:S(2)}) collective-permute-start(bf16[360,720]{1,0:T(8,128)(2,1)} %refs_2_), channel_id=1, source_target_pairs={{0,1},{1,0},{2,3},{3,2},{4,5},{5,4},{6,7},{7,6},{8,9},{9,8},{10,11... | collective-permute-start | bytes 1555208 | tf_op jit(solution)/shard_map/ppermute | solution.py:417
  8.9 24.2 %all-to-all-start = ((s16[8,40,768]{2,1,0:T(8,128)(2,1)}), s16[8,40,768]{2,1,0:T(8,128)(2,1)S(1)}, u32[]{:S(2)}, u32[]{:S(2)}) async-start(s16[8,40,768]{2,1,0:T(8,128)(2,1)} %get-tuple-element.71), calls=%async_computation | async-start | bytes 983040 | tf_op jit(solution)/shard_map/all_to_all | solution.py:437
  22.1 9.4 %collective-permute-start.5 = (f32[40,720]{1,0:T(8,128)S(1)}, f32[40,720]{1,0:T(8,128)S(1)}, u32[]{:S(2)}, u32[]{:S(2)}) collective-permute-start(f32[40,720]{1,0:T(8,128)S(1)} %get-tuple-element.129), channel_id=1, source_target_pairs={{0,1},{1,0},{2,3},{3,2},{4,5},{5,4},{6,7},{7,6},{8,9},{9,8},{10,11... | collective-permute-start | bytes 345608 | tf_op jit(solution)/shard_map/ppermute | solution.py:417
  22.2 9.9 %collective-permute-start.4 = (bf16[168,720]{1,0:T(8,128)(2,1)S(1)}, bf16[168,720]{1,0:T(8,128)(2,1)S(1)}, u32[]{:S(2)}, u32[]{:S(2)}) collective-permute-start(bf16[168,720]{1,0:T(8,128)(2,1)S(1)} %slice.22), channel_id=1, source_target_pairs={{0,8},{4,12},{8,0},{12,4},{16,24},{20,28},{24,16},{28,20},{1,9},{5... | collective-permute-start | bytes 725768 | tf_op jit(solution)/shard_map/ppermute | solution.py:414
  22.5 16.2 %copy-start.2 = (bf16[360,720]{1,0:T(8,128)(2,1)S(1)}, bf16[360,720]{1,0:T(8,128)(2,1)}, u32[]{:S(2)}) copy-start(bf16[360,720]{1,0:T(8,128)(2,1)} %refs_2_) | copy-start | bytes 1555204
  22.6 10.5 %collective-permute-start.3 = (bf16[192,720]{1,0:T(8,128)(2,1)S(1)}, bf16[192,720]{1,0:T(8,128)(2,1)S(1)}, u32[]{:S(2)}, u32[]{:S(2)}) collective-permute-start(bf16[192,720]{1,0:T(8,128)(2,1)S(1)} %slice.21), channel_id=1, source_target_pairs={{0,4},{4,0},{8,12},{12,8},{16,20},{20,16},{24,28},{28,24},{1,5},{5... | collective-permute-start | bytes 829448 | tf_op jit(solution)/shard_map/ppermute | solution.py:414
  31.5 0.7 copy-start.3
  32.2 16.1 %copy-start.4 = (f32[40,720]{1,0:T(8,128)S(1)}, f32[40,720]{1,0:T(8,128)}, u32[]{:S(2)}) copy-start(f32[40,720]{1,0:T(8,128)} %copy-done.3) | copy-start | bytes 345604
  33.1 5.7 %collective-permute-start.6 = (bf16[360,720]{1,0:T(8,128)(2,1)S(1)}, bf16[360,720]{1,0:T(8,128)(2,1)S(1)}, u32[]{:S(2)}, u32[]{:S(2)}) collective-permute-start(bf16[360,720]{1,0:T(8,128)(2,1)S(1)} %collective-permute-done.refs_1_.refs_3_), channel_id=1, source_target_pairs={{0,1},{1,0},{2,3},{3,2},{4,5},{5,4},{6,7},{7,6},{8,9},{9,8},{10,11... | collective-permute-start | bytes 1555208 | tf_op jit(solution)/shard_map/ppermute | solution.py:417
  33.1 5.7 %collective-permute-start.7 = (bf16[360,720]{1,0:T(8,128)(2,1)S(1)}, bf16[360,720]{1,0:T(8,128)(2,1)S(1)}, u32[]{:S(2)}, u32[]{:S(2)}) collective-permute-start(bf16[360,720]{1,0:T(8,128)(2,1)S(1)} %collective-permute-done.1.refs_2_.refs_4_), channel_id=1, source_target_pairs={{0,1},{1,0},{2,3},{3,2},{4,5},{5,4},{6,7},{7,6},{8,9},{9,8},{10,11... | collective-permute-start | bytes 1555208 | tf_op jit(solution)/shard_map/ppermute | solution.py:417
  33.6 5.1 %collective-permute-start.8 = (bf16[192,720]{1,0:T(8,128)(2,1)S(1)}, bf16[192,720]{1,0:T(8,128)(2,1)S(1)}, u32[]{:S(2)}, u32[]{:S(2)}) collective-permute-start(bf16[192,720]{1,0:T(8,128)(2,1)S(1)} %collective-permute-done.3.refs_3_.refs_5_), channel_id=1, source_target_pairs={{0,1},{1,0},{2,3},{3,2},{4,5},{5,4},{6,7},{7,6},{8,9},{9,8},{10,11... | collective-permute-start | bytes 829448 | tf_op jit(solution)/shard_map/ppermute | solution.py:417
  33.6 5.1 %collective-permute-start.9 = (bf16[168,720]{1,0:T(8,128)(2,1)S(1)}, bf16[168,720]{1,0:T(8,128)(2,1)S(1)}, u32[]{:S(2)}, u32[]{:S(2)}) collective-permute-start(bf16[168,720]{1,0:T(8,128)(2,1)S(1)} %collective-permute-done.4.refs_4_.refs_6_), channel_id=1, source_target_pairs={{0,1},{1,0},{2,3},{3,2},{4,5},{5,4},{6,7},{7,6},{8,9},{9,8},{10,11... | collective-permute-start | bytes 725768 | tf_op jit(solution)/shard_map/ppermute | solution.py:417
  34.5 4.3 %collective-permute-start.10 = (s16[40,768]{1,0:T(8,128)(2,1)S(1)}, s16[40,768]{1,0:T(8,128)(2,1)S(1)}, u32[]{:S(2)}, u32[]{:S(2)}) collective-permute-start(s16[40,768]{1,0:T(8,128)(2,1)S(1)} %get-tuple-element.81), channel_id=1, source_target_pairs={{0,2},{1,3},{2,0},{3,1},{4,6},{5,7},{6,4},{7,5},{8,10},{9,11},{10,... | collective-permute-start | bytes 184328 | tf_op jit(solution)/shard_map/ppermute | solution.py:417
  38.8 26.2 %copy-start.1 = (f32[8,4,40,720]{3,2,1,0:T(8,128)S(1)}, f32[8,4,40,720]{3,2,1,0:T(8,128)}, u32[]{:S(2)}) copy-start(f32[8,4,40,720]{3,2,1,0:T(8,128)} %train_gradients.3.refs_1_) | copy-start | bytes 11059204
  40.0 25.0 %copy-start = (f32[8,4,40,720]{3,2,1,0:T(8,128)S(1)}, f32[8,4,40,720]{3,2,1,0:T(8,128)}, u32[]{:S(2)}) copy-start(f32[8,4,40,720]{3,2,1,0:T(8,128)} %train_gradients.2.refs_0_) | copy-start | bytes 11059204
  40.0 8.3 %collective-permute-start.11 = (s16[2,40,768]{2,1,0:T(8,128)(2,1)S(1)}, s16[2,40,768]{2,1,0:T(8,128)(2,1)S(1)}, u32[]{:S(2)}, u32[]{:S(2)}) collective-permute-start(s16[2,40,768]{2,1,0:T(8,128)(2,1)S(1)} %project.1.own_ref), channel_id=1, source_target_pairs={{0,16},{4,20},{8,24},{12,28},{16,0},{20,4},{24,8},{28,12},{1,17},{... | collective-permute-start | bytes 368648 | tf_op jit(solution)/shard_map/ppermute | solution.py:414
  50.2 4.3 %collective-permute-start.12 = (s16[40,768]{1,0:T(8,128)(2,1)S(1)}, s16[40,768]{1,0:T(8,128)(2,1)S(1)}, u32[]{:S(2)}, u32[]{:S(2)}) collective-permute-start(s16[40,768]{1,0:T(8,128)(2,1)S(1)} %get-tuple-element.103), channel_id=1, source_target_pairs={{0,2},{1,3},{2,0},{3,1},{4,6},{5,7},{6,4},{7,5},{8,10},{9,11},{10,... | collective-permute-start | bytes 184328 | tf_op jit(solution)/shard_map/ppermute | solution.py:417
  51.5 11.3 %collective-permute-start.16 = (s16[2,40,768]{2,1,0:T(8,128)(2,1)S(1)}, s16[2,40,768]{2,1,0:T(8,128)(2,1)S(1)}, u32[]{:S(2)}, u32[]{:S(2)}) collective-permute-start(s16[2,40,768]{2,1,0:T(8,128)(2,1)S(1)} %get-tuple-element.111), channel_id=1, source_target_pairs={{0,4},{4,0},{8,12},{12,8},{16,20},{20,16},{24,28},{28,24},{1,5},{5... | collective-permute-start | bytes 368648 | tf_op jit(solution)/shard_map/ppermute | solution.py:414
  54.9 6.7 %collective-permute-start.15 = (s16[40,768]{1,0:T(8,128)(2,1)S(1)}, s16[40,768]{1,0:T(8,128)(2,1)S(1)}, u32[]{:S(2)}, u32[]{:S(2)}) collective-permute-start(s16[40,768]{1,0:T(8,128)(2,1)S(1)} %select_convert_fusion), channel_id=1, source_target_pairs={{0,24},{4,28},{8,16},{12,20},{16,8},{20,12},{24,0},{28,4},{1,25},{... | collective-permute-start | bytes 184328 | tf_op jit(solution)/shard_map/ppermute | solution.py:414
  57.6 5.2 %collective-permute-start.14 = (s16[40,768]{1,0:T(8,128)(2,1)S(1)}, s16[40,768]{1,0:T(8,128)(2,1)S(1)}, u32[]{:S(2)}, u32[]{:S(2)}) collective-permute-start(s16[40,768]{1,0:T(8,128)(2,1)S(1)} %select_convert_fusion), channel_id=1, source_target_pairs={{0,16},{4,20},{8,24},{12,28},{16,0},{20,4},{24,8},{28,12},{1,17},{... | collective-permute-start | bytes 184328 | tf_op jit(solution)/shard_map/ppermute | solution.py:414
  57.6 5.2 %collective-permute-start.13 = (s16[40,768]{1,0:T(8,128)(2,1)S(1)}, s16[40,768]{1,0:T(8,128)(2,1)S(1)}, u32[]{:S(2)}, u32[]{:S(2)}) collective-permute-start(s16[40,768]{1,0:T(8,128)(2,1)S(1)} %select_convert_fusion), channel_id=1, source_target_pairs={{0,8},{4,12},{8,0},{12,4},{16,24},{20,28},{24,16},{28,20},{1,9},{5... | collective-permute-start | bytes 184328 | tf_op jit(solution)/shard_map/ppermute | solution.py:414
  62.8 6.3 %collective-permute-start.18 = (s16[2,2,40,768]{3,2,0,1:T(8,128)(2,1)S(1)}, s16[2,2,40,768]{3,2,0,1:T(8,128)(2,1)S(1)}, u32[]{:S(2)}, u32[]{:S(2)}) collective-permute-start(s16[2,2,40,768]{3,2,0,1:T(8,128)(2,1)S(1)} %pad_add_fusion.1), channel_id=1, source_target_pairs={{0,8},{4,12},{8,0},{12,4},{16,24},{20,28},{24,16},{28,20},{1,9},{5... | collective-permute-start | bytes 737288 | tf_op jit(solution)/shard_map/ppermute | solution.py:414
  64.3 1.5 %copy-start.5 = (s32[8]{0:T(128)S(1)}, s32[8]{0:T(128)}, u32[]{:S(2)}) copy-start(s32[8]{0:T(128)} %param.12) | copy-start | bytes 100
  64.3 6.3 %collective-permute-start.17 = (s16[4,40,768]{2,1,0:T(8,128)(2,1)S(1)}, s16[4,40,768]{2,1,0:T(8,128)(2,1)S(1)}, u32[]{:S(2)}, u32[]{:S(2)}) collective-permute-start(s16[4,40,768]{2,1,0:T(8,128)(2,1)S(1)} %pad_add_fusion.found), channel_id=1, source_target_pairs={{0,4},{4,0},{8,12},{12,8},{16,20},{20,16},{24,28},{28,24},{1,5},{5... | collective-permute-start | bytes 737288 | tf_op jit(solution)/shard_map/ppermute | solution.py:414
  70.6 3.2 %collective-permute-start.22 = (s16[4,40,768]{2,1,0:T(8,128)(2,1)S(1)}, s16[4,40,768]{2,1,0:T(8,128)(2,1)S(1)}, u32[]{:S(2)}, u32[]{:S(2)}) collective-permute-start(s16[4,40,768]{2,1,0:T(8,128)(2,1)S(1)} %get-tuple-element.131), channel_id=1, source_target_pairs={{0,1},{1,0},{2,3},{3,2},{4,5},{5,4},{6,7},{7,6},{8,9},{9,8},{10,11... | collective-permute-start | bytes 737288 | tf_op jit(solution)/shard_map/ppermute | solution.py:417
  71.7 3.3 %collective-permute-start.21 = (f32[8]{0:T(128)S(1)}, f32[8]{0:T(128)S(1)}, u32[]{:S(2)}, u32[]{:S(2)}) collective-permute-start(f32[8]{0:T(128)S(1)} %slice_reduce_fusion), channel_id=1, source_target_pairs={{0,3},{1,2},{2,1},{3,0},{4,7},{5,6},{6,5},{7,4},{8,11},{9,10},{10,... | collective-permute-start | bytes 104 | tf_op jit(solution)/shard_map/ppermute | solution.py:417
  72.8 3.5 %collective-permute-start.20 = (f32[8]{0:T(128)S(1)}, f32[8]{0:T(128)S(1)}, u32[]{:S(2)}, u32[]{:S(2)}) collective-permute-start(f32[8]{0:T(128)S(1)} %slice_reduce_fusion), channel_id=1, source_target_pairs={{0,2},{1,3},{2,0},{3,1},{4,6},{5,7},{6,4},{7,5},{8,10},{9,11},{10,... | collective-permute-start | bytes 104 | tf_op jit(solution)/shard_map/ppermute | solution.py:417
  73.9 2.5 %collective-permute-start.19 = (f32[8]{0:T(128)S(1)}, f32[8]{0:T(128)S(1)}, u32[]{:S(2)}, u32[]{:S(2)}) collective-permute-start(f32[8]{0:T(128)S(1)} %slice_reduce_fusion), channel_id=1, source_target_pairs={{0,1},{1,0},{2,3},{3,2},{4,5},{5,4},{6,7},{7,6},{8,9},{9,8},{10,11... | collective-permute-start | bytes 104 | tf_op jit(solution)/shard_map/ppermute | solution.py:417

commit v5 on v4

--- a/solution.py
+++ b/solution.py
@@ -436,21 +436,20 @@
     )
     arrived = lax.all_to_all(partial, "dp", 0, 0)
     trained = train(0, chosen)
-    blocks, near, trained, chosen, eigenvalues = fence_blocks(
-        blocks, near, trained, chosen, eigenvalues
-    )
-
-    if groups > 3:
-        blocks.append(((3, 0, 0, cut), swap(blocks[2][1][:cut], 1)))
-        blocks.append(((3, 0, cut, rows), swap(blocks[1][1][cut:], 2)))
-    trained += train(1, chosen, 10**10)
     eigen = []
     for away in range(parts):
         start = ((part ^ away) * groups + group) * own_rows
         lines = lax.dynamic_slice_in_dim(eigenvalues, start, own_rows, axis=0)
         if high_rows > own_rows:
             lines = jnp.pad(lines, ((0, high_rows - own_rows), (0, 0)), constant_values=1.0)
-        eigen.append(flip(lines, away) if away else lines)
+        eigen.append(lines)
+    blocks, near, trained, chosen, eigen = fence_blocks(blocks, near, trained, chosen, eigen)
+
+    if groups > 3:
+        blocks.append(((3, 0, 0, cut), swap(blocks[2][1][:cut], 1)))
+        blocks.append(((3, 0, cut, rows), swap(blocks[1][1][cut:], 2)))
+    trained += train(1, chosen, 10**10)
+    eigen = [flip(lines, away) if away else lines for away, lines in enumerate(eigen)]
     blocks, near, trained, chosen, arrived, eigen = fence_blocks(
         blocks, near, trained, chosen, arrived, eigen
     )
@@ -485,22 +484,23 @@
 
     even, pair = jnp.stack(even), jnp.stack(pair)
     odd = swap(even, 1)
-    found = [pair] + [swap(pair, away) for away in range(2, groups, 2)]
     phase = (timesteps.astype(f32) / 1000.0 + 0.008) / 1.008 * (math.pi / 2)
     weight = jnp.sin(phase) * (1 / math.sqrt(channels * width))
     sums = score_products(even, trained, 0, 10**10)
-    odd, found, sums, weight = fence((odd, found, sums, weight))
+    pair, sums = fence((pair, sums))
+    found = [pair] + [swap(pair, away) for away in range(2, groups, 2)]
+    odd, sums, weight = fence((odd, sums, weight))
 
     sums = sums + score_products(odd, trained, 1, 10**3)
     found = jnp.concatenate(found)
-    terms = [sums[:, 0]]
-    terms += [flip(terms[0], away) for away in range(1, factor)]
+    terms = [sums]
+    terms += [flip(terms[0], away) for away in range(factor - 1, 0, -1)][::-1]
     rows_found = [found[:, 0]] + [flip(found[:, away], away) for away in range(1, parts)]
     query_proj = output_rows(rows_found, groups, parts, own_rows, jump).reshape(channels, jump)
     terms, query_proj = fence((terms, query_proj))
     while len(terms) > 1:
         terms = [terms[at] + terms[at + 1] for at in range(0, len(terms), 2)]
-    return (terms[0] * weight, query_proj)
+    return (terms[0][:, 0] * weight, query_proj)
 
 
 def solution(mesh):

time: 77.3 us -> 76.3 us (0.987)
  waiting for transfers between devices: 22 us -> 20.2 us
  starting transfers between devices: 28.2 us -> 29 us
    ppermute x12, waiting for transfers between devices: 6.08 us -> 5.15 us  [flip(): return lax.ppermute(array, 'factor', [(p, p ^ away) for p in range(factor)])]
    ppermute x11, waiting for transfers between devices: 15.9 us -> 15 us  [swap(): return lax.ppermute(array, 'dp', [(d, d ^ away) for d in range(shards)])]
    ppermute x12, starting transfers between devices: 6.1 us -> 6.94 us  [flip(): return lax.ppermute(array, 'factor', [(p, p ^ away) for p in range(factor)])]
  transfers between devices with their start and end apart: 24 -> 24, of which waited for: 10 -> 10; matrix products, arithmetic and copies ran while one was open for 2% -> 2% of each run, Pallas kernels for 26% -> 25%
where the time goes in v5:
time: 76.3 us; the launch traced here: 75.9 us
  starting transfers between devices  29 us (38%)
  Pallas kernels  23.1 us (30%)
  waiting for transfers between devices  20.2 us (26%)
  local copies, waits for them, and re-layouts  1.89 us (2%)
  other arithmetic  0.97 us (1%)
  between operations  0.82 us (1%)
    ppermute x11, starting transfers between devices, swap(): return lax.ppermute(array, 'dp', [(d, d ^ away) for d in range(shards)])  18.2 us
    ppermute x11, waiting for transfers between devices, swap(): return lax.ppermute(array, 'dp', [(d, d ^ away) for d in range(shards)])  15 us
    pallas_call x2, Pallas kernels, train_gradients(): pl.pallas_call(functools.partial(train_kernel, parts=parts), grid=(count,...  13.1 us
    ppermute x12, starting transfers between devices, flip(): return lax.ppermute(array, 'factor', [(p, p ^ away) for p in range(factor)])  6.94 us
    ppermute x12, waiting for transfers between devices, flip(): return lax.ppermute(array, 'factor', [(p, p ^ away) for p in range(factor)])  5.15 us
    all_to_all x1, starting transfers between devices, on_device(): arrived = lax.all_to_all(partial, 'dp', 0, 0)  3.86 us
    pallas_call x1, Pallas kernels, query_partial(): pl.pallas_call(functools.partial(query_kernel, groups=groups, parts=parts...  3.65 us
    pallas_call x1, Pallas kernels, project_back(): pl.pallas_call(functools.partial(back_kernel, spots=spots, groups=groups,...  1.95 us
  transfers between devices with their start and end apart: 24, of which 10 were waited for; matrix products, arithmetic and copies ran while one was open for 2% of the time, Pallas kernels for 25%

profile of v5, /device:TPU:0, one launch (start us, length us, event | category | flops | bytes accessed | tf_op | source)
XLA Modules:
  0.0 75.9 jit_solution(11763909565433622631)
XLA Ops:
  0.6 3.1 %collective-permute-start.1 = (bf16[360,720]{1,0:T(8,128)(2,1)}, bf16[360,720]{1,0:T(8,128)(2,1)S(1)}, u32[]{:S(2)}, u32[]{:S(2)}) collective-permute-start(bf16[360,720]{1,0:T(8,128)(2,1)} %refs_2_), channel_id=1, source_target_pairs={{0,8},{4,12},{8,0},{12,4},{16,24},{20,28},{24,16},{28,20},{1,9},{5... | collective-permute-start | bytes 1555208 | tf_op jit(solution)/shard_map/ppermute | solution.py:414
  3.7 1.5 %collective-permute-start = (bf16[360,720]{1,0:T(8,128)(2,1)}, bf16[360,720]{1,0:T(8,128)(2,1)S(1)}, u32[]{:S(2)}, u32[]{:S(2)}) collective-permute-start(bf16[360,720]{1,0:T(8,128)(2,1)} %refs_2_), channel_id=1, source_target_pairs={{0,4},{4,0},{8,12},{12,8},{16,20},{20,16},{24,28},{28,24},{1,5},{5... | collective-permute-start | bytes 1555208 | tf_op jit(solution)/shard_map/ppermute | solution.py:414
  5.2 0.0 collective-permute-start.2
  5.2 3.6 %query_gradient.1 = (s16[8,40,768]{2,1,0:T(8,128)(2,1)}, bf16[320,160]{1,0:T(8,128)(2,1)S(1)}) custom-call(bf16[1,8,64,320]{3,2,1,0:T(8,128)(2,1)} %x_ref.3, bf16[1,8,64,320]{3,2,1,0:T(8,128)(2,1)} %c_ref.3, bf16[320,320]{1,0:T(8,128)(2,1)} %basis_ref.1), custom_call_target="tpu_custom_call" | custom-call | flops 1000 | bytes 1000 | tf_op jit(solution)/shard_map/query_gradient/pallas_call | solution.py:165
  8.9 3.9 %all-to-all-start = ((s16[8,40,768]{2,1,0:T(8,128)(2,1)}), s16[8,40,768]{2,1,0:T(8,128)(2,1)S(1)}, u32[]{:S(2)}, u32[]{:S(2)}) async-start(s16[8,40,768]{2,1,0:T(8,128)(2,1)} %get-tuple-element.72), calls=%async_computation | async-start | bytes 983040 | tf_op jit(solution)/shard_map/all_to_all | solution.py:437
  12.8 6.6 %train_gradients.2.refs_0_ = f32[8,4,40,720]{3,2,1,0:T(8,128)} custom-call(bf16[320,160]{1,0:T(8,128)(2,1)S(1)} %get-tuple-element.71.basis_ref, bf16[8,8,64,320]{3,2,1,0:T(8,128)(2,1)} %x_ref.5, bf16[8,8,64,320]{3,2,1,0:T(8,128)(2,1)} %c_ref.5), custom_call_target="tpu_custom_call" | custom-call | flops 1000 | bytes 1000 | tf_op jit(solution)/shard_map/train_gradients/pallas_call | solution.py:209
  19.3 1.0 %constant_dynamic-slice_fusion = (f32[40,720]{1,0:T(8,128)S(1)}, f32[40,720]{1,0:T(8,128)S(1)}) fusion(f32[320,720]{1,0:T(8,128)} %param.15, s32[]{:T(128)S(6)} %select_n.24, s32[]{:T(128)S(6)} %select_n.23), kind=kLoop, calls=%fused_computation.22 | loop fusion | bytes 460808 | tf_op jit(solution)/shard_map/dynamic_slice | solution.py:442
  20.3 0.0 collective-permute-done.1.refs_2_.refs_4_
  20.3 0.8 %collective-permute-done.refs_1_.refs_3_ = bf16[360,720]{1,0:T(8,128)(2,1)S(1)} collective-permute-done((bf16[360,720]{1,0:T(8,128)(2,1)}, bf16[360,720]{1,0:T(8,128)(2,1)S(1)}, u32[]{:S(2)}, u32[]{:S(2)}) %collective-permute-start) | collective-permute-done | bytes 518432 | tf_op jit(solution)/shard_map/ppermute | solution.py:414
  21.1 0.0 collective-permute-done.2.refs_5_.refs_7_
  21.1 0.0 collective-permute-start.5
  21.2 1.4 %collective-permute-start.4 = (bf16[168,720]{1,0:T(8,128)(2,1)S(1)}, bf16[168,720]{1,0:T(8,128)(2,1)S(1)}, u32[]{:S(2)}, u32[]{:S(2)}) collective-permute-start(bf16[168,720]{1,0:T(8,128)(2,1)S(1)} %slice.22), channel_id=1, source_target_pairs={{0,8},{4,12},{8,0},{12,4},{16,24},{20,28},{24,16},{28,20},{1,9},{5... | collective-permute-start | bytes 725768 | tf_op jit(solution)/shard_map/ppermute | solution.py:414
  22.6 0.0 copy-start.2
  22.6 1.5 %collective-permute-start.3 = (bf16[192,720]{1,0:T(8,128)(2,1)S(1)}, bf16[192,720]{1,0:T(8,128)(2,1)S(1)}, u32[]{:S(2)}, u32[]{:S(2)}) collective-permute-start(bf16[192,720]{1,0:T(8,128)(2,1)S(1)} %slice.21), channel_id=1, source_target_pairs={{0,4},{4,0},{8,12},{12,8},{16,20},{20,16},{24,28},{28,24},{1,5},{5... | collective-permute-start | bytes 829448 | tf_op jit(solution)/shard_map/ppermute | solution.py:414
  24.1 6.6 %train_gradients.3.refs_1_ = f32[8,4,40,720]{3,2,1,0:T(8,128)} custom-call(bf16[320,160]{1,0:T(8,128)(2,1)S(1)} %get-tuple-element.71.basis_ref, bf16[8,8,64,320]{3,2,1,0:T(8,128)(2,1)} %x_ref.5, bf16[8,8,64,320]{3,2,1,0:T(8,128)(2,1)} %c_ref.5), custom_call_target="tpu_custom_call" | custom-call | flops 10000000000 | bytes 1000 | tf_op jit(solution)/shard_map/train_gradients/pallas_call | solution.py:209
  30.7 0.0 collective-permute-done.5.refs_1_
  30.7 0.7 copy-done.3
  31.3 0.0 collective-permute-done.4.refs_4_.refs_6_
  31.3 1.1 %collective-permute-done.3.refs_3_.refs_5_ = bf16[192,720]{1,0:T(8,128)(2,1)S(1)} collective-permute-done((bf16[192,720]{1,0:T(8,128)(2,1)S(1)}, bf16[192,720]{1,0:T(8,128)(2,1)S(1)}, u32[]{:S(2)}, u32[]{:S(2)}) %collective-permute-start.3) | collective-permute-done | bytes 276512 | tf_op jit(solution)/shard_map/ppermute | solution.py:414
  32.4 0.0 all-to-all-done.arrived
  32.4 0.0 collective-permute-start.6
  32.4 0.5 collective-permute-start.7
  32.9 0.0 collective-permute-start.8
  32.9 0.5 collective-permute-start.9
  33.4 0.3 merge.1
  33.8 2.1 %collective-permute-start.10 = (s16[40,768]{1,0:T(8,128)(2,1)S(1)}, s16[40,768]{1,0:T(8,128)(2,1)S(1)}, u32[]{:S(2)}, u32[]{:S(2)}) collective-permute-start(s16[40,768]{1,0:T(8,128)(2,1)S(1)} %get-tuple-element.83), channel_id=1, source_target_pairs={{0,2},{1,3},{2,0},{3,1},{4,6},{5,7},{6,4},{7,5},{8,10},{9,11},{10,... | collective-permute-start | bytes 184328 | tf_op jit(solution)/shard_map/ppermute | solution.py:417
  35.9 2.2 %collective-permute-done.10.other_ref = s16[40,768]{1,0:T(8,128)(2,1)S(1)} collective-permute-done((s16[40,768]{1,0:T(8,128)(2,1)S(1)}, s16[40,768]{1,0:T(8,128)(2,1)S(1)}, u32[]{:S(2)}, u32[]{:S(2)}) %collective-permute-start.10) | collective-permute-done | bytes 61472 | tf_op jit(solution)/shard_map/ppermute | solution.py:417
  38.1 0.0 collective-permute-done.9.refs_9_.refs_11_
  38.1 0.0 collective-permute-done.8.refs_8_.refs_10_
  38.1 0.0 collective-permute-done.6.refs_6_.refs_8_
  38.1 0.0 collective-permute-done.7.refs_7_.refs_9_
  38.2 1.2 %project.1.own_ref = s16[2,40,768]{2,1,0:T(8,128)(2,1)S(1)} custom-call(f32[40,720]{1,0:T(8,128)S(1)} %get-tuple-element.86.own_ref, s16[40,768]{1,0:T(8,128)(2,1)S(1)} %collective-permute-done.10.other_ref, bf16[360,720]{1,0:T(8,128)(2,1)S(1)} %copy-done.2, bf16[360,720]{1,0:T(8,128)(2,1)S(1)} %collective-permute-done.refs_1_.refs_3_, ...), custom_call_target="tpu_custom_call" | custom-call | flops 1000 | bytes 1000 | tf_op jit(solution)/shard_map/project/pallas_call | solution.py:271
  39.4 2.9 %collective-permute-start.11 = (s16[2,40,768]{2,1,0:T(8,128)(2,1)S(1)}, s16[2,40,768]{2,1,0:T(8,128)(2,1)S(1)}, u32[]{:S(2)}, u32[]{:S(2)}) collective-permute-start(s16[2,40,768]{2,1,0:T(8,128)(2,1)S(1)} %project.1.own_ref), channel_id=1, source_target_pairs={{0,16},{4,20},{8,24},{12,28},{16,0},{20,4},{24,8},{28,12},{1,17},{... | collective-permute-start | bytes 368648 | tf_op jit(solution)/shard_map/ppermute | solution.py:414
  42.3 5.1 %collective-permute-done.11.other_ref = s16[2,40,768]{2,1,0:T(8,128)(2,1)S(1)} collective-permute-done((s16[2,40,768]{2,1,0:T(8,128)(2,1)S(1)}, s16[2,40,768]{2,1,0:T(8,128)(2,1)S(1)}, u32[]{:S(2)}, u32[]{:S(2)}) %collective-permute-start.11) | collective-permute-done | bytes 122912 | tf_op jit(solution)/shard_map/ppermute | solution.py:414
  47.3 1.9 %project_back.1 = (s16[2,40,768]{2,1,0:T(8,128)(2,1)S(1)}, s16[40,768]{1,0:T(8,128)(2,1)S(1)}, s16[40,768]{1,0:T(8,128)(2,1)S(1)}) custom-call(s16[2,40,768]{2,1,0:T(8,128)(2,1)S(1)} %project.1.own_ref, s16[2,40,768]{2,1,0:T(8,128)(2,1)S(1)} %collective-permute-done.11.other_ref, f32[40,720]{1,0:T(8,128)S(1)} %get-tuple-element.102.refs_0_, ...), custom_call_target="tpu_custom_call" | custom-call | flops 1000 | bytes 1000 | tf_op jit(solution)/shard_map/project_back/pallas_call | solution.py:323
  49.3 1.8 %collective-permute-start.12 = (s16[40,768]{1,0:T(8,128)(2,1)S(1)}, s16[40,768]{1,0:T(8,128)(2,1)S(1)}, u32[]{:S(2)}, u32[]{:S(2)}) collective-permute-start(s16[40,768]{1,0:T(8,128)(2,1)S(1)} %get-tuple-element.105), channel_id=1, source_target_pairs={{0,2},{1,3},{2,0},{3,1},{4,6},{5,7},{6,4},{7,5},{8,10},{9,11},{10,... | collective-permute-start | bytes 184328 | tf_op jit(solution)/shard_map/ppermute | solution.py:417
  51.1 1.2 %collective-permute-start.16 = (s16[2,40,768]{2,1,0:T(8,128)(2,1)S(1)}, s16[2,40,768]{2,1,0:T(8,128)(2,1)S(1)}, u32[]{:S(2)}, u32[]{:S(2)}) collective-permute-start(s16[2,40,768]{2,1,0:T(8,128)(2,1)S(1)} %get-tuple-element.113), channel_id=1, source_target_pairs={{0,4},{4,0},{8,12},{12,8},{16,20},{20,16},{24,28},{28,24},{1,5},{5... | collective-permute-start | bytes 368648 | tf_op jit(solution)/shard_map/ppermute | solution.py:414
  52.3 1.3 %collective-permute-done.12 = s16[40,768]{1,0:T(8,128)(2,1)S(1)} collective-permute-done((s16[40,768]{1,0:T(8,128)(2,1)S(1)}, s16[40,768]{1,0:T(8,128)(2,1)S(1)}, u32[]{:S(2)}, u32[]{:S(2)}) %collective-permute-start.12) | collective-permute-done | bytes 61472 | tf_op jit(solution)/shard_map/ppermute | solution.py:417
  53.6 0.2 fusion.4
  53.8 0.1 select_convert_fusion
  53.9 2.6 %collective-permute-start.15 = (s16[40,768]{1,0:T(8,128)(2,1)S(1)}, s16[40,768]{1,0:T(8,128)(2,1)S(1)}, u32[]{:S(2)}, u32[]{:S(2)}) collective-permute-start(s16[40,768]{1,0:T(8,128)(2,1)S(1)} %select_convert_fusion), channel_id=1, source_target_pairs={{0,24},{4,28},{8,16},{12,20},{16,8},{20,12},{24,0},{28,4},{1,25},{... | collective-permute-start | bytes 184328 | tf_op jit(solution)/shard_map/ppermute | solution.py:414
  56.5 0.0 collective-permute-start.14
  56.5 1.9 %collective-permute-start.13 = (s16[40,768]{1,0:T(8,128)(2,1)S(1)}, s16[40,768]{1,0:T(8,128)(2,1)S(1)}, u32[]{:S(2)}, u32[]{:S(2)}) collective-permute-start(s16[40,768]{1,0:T(8,128)(2,1)S(1)} %select_convert_fusion), channel_id=1, source_target_pairs={{0,8},{4,12},{8,0},{12,4},{16,24},{20,28},{24,16},{28,20},{1,9},{5... | collective-permute-start | bytes 184328 | tf_op jit(solution)/shard_map/ppermute | solution.py:414
  58.4 1.9 %collective-permute-done.15 = s16[40,768]{1,0:T(8,128)(2,1)S(1)} collective-permute-done((s16[40,768]{1,0:T(8,128)(2,1)S(1)}, s16[40,768]{1,0:T(8,128)(2,1)S(1)}, u32[]{:S(2)}, u32[]{:S(2)}) %collective-permute-start.15) | collective-permute-done | bytes 61472 | tf_op jit(solution)/shard_map/ppermute | solution.py:414
  60.3 1.3 %collective-permute-done.14 = s16[40,768]{1,0:T(8,128)(2,1)S(1)} collective-permute-done((s16[40,768]{1,0:T(8,128)(2,1)S(1)}, s16[40,768]{1,0:T(8,128)(2,1)S(1)}, u32[]{:S(2)}, u32[]{:S(2)}) %collective-permute-start.14) | collective-permute-done | bytes 61472 | tf_op jit(solution)/shard_map/ppermute | solution.py:414
  61.6 0.0 collective-permute-done.13
  61.6 0.0 collective-permute-done.16
  61.7 0.0 copy-start.5
  61.7 0.8 %score_products.2 = f32[8,128]{1,0:T(8,128)S(1)} custom-call(s16[4,40,768]{2,1,0:T(8,128)(2,1)S(1)} %pad_add_fusion.found, f32[8,4,40,720]{3,2,1,0:T(8,128)S(1)} %copy-done, f32[8,4,40,720]{3,2,1,0:T(8,128)S(1)} %copy-done.1), custom_call_target="tpu_custom_call" | custom-call | flops 10000000000 | bytes 1000 | tf_op jit(solution)/shard_map/score_products/pallas_call | solution.py:355
  62.6 1.0 %collective-permute-start.21 = (s16[2,2,40,768]{3,2,0,1:T(8,128)(2,1)S(1)}, s16[2,2,40,768]{3,2,0,1:T(8,128)(2,1)S(1)}, u32[]{:S(2)}, u32[]{:S(2)}) collective-permute-start(s16[2,2,40,768]{3,2,0,1:T(8,128)(2,1)S(1)} %pad_add_fusion.1), channel_id=1, source_target_pairs={{0,8},{4,12},{8,0},{12,4},{16,24},{20,28},{24,16},{28,20},{1,9},{5... | collective-permute-start | bytes 737288 | tf_op jit(solution)/shard_map/ppermute | solution.py:414
  63.5 1.2 %collective-permute-start.17 = (s16[4,40,768]{2,1,0:T(8,128)(2,1)S(1)}, s16[4,40,768]{2,1,0:T(8,128)(2,1)S(1)}, u32[]{:S(2)}, u32[]{:S(2)}) collective-permute-start(s16[4,40,768]{2,1,0:T(8,128)(2,1)S(1)} %pad_add_fusion.found), channel_id=1, source_target_pairs={{0,4},{4,0},{8,12},{12,8},{16,20},{20,16},{24,28},{28,24},{1,5},{5... | collective-permute-start | bytes 737288 | tf_op jit(solution)/shard_map/ppermute | solution.py:414
  64.7 4.0 %collective-permute-done.21 = s16[2,2,40,768]{3,2,0,1:T(8,128)(2,1)S(1)} collective-permute-done((s16[2,2,40,768]{3,2,0,1:T(8,128)(2,1)S(1)}, s16[2,2,40,768]{3,2,0,1:T(8,128)(2,1)S(1)}, u32[]{:S(2)}, u32[]{:S(2)}) %collective-permute-start.21) | collective-permute-done | bytes 245792 | tf_op jit(solution)/shard_map/ppermute | solution.py:414
  68.8 0.1 collective-permute-start.22
  68.9 0.8 %collective-permute-done.17.found = s16[4,40,768]{2,1,0:T(8,128)(2,1)S(1)} collective-permute-done((s16[4,40,768]{2,1,0:T(8,128)(2,1)S(1)}, s16[4,40,768]{2,1,0:T(8,128)(2,1)S(1)}, u32[]{:S(2)}, u32[]{:S(2)}) %collective-permute-start.17) | collective-permute-done | bytes 245792 | tf_op jit(solution)/shard_map/ppermute | solution.py:414
  69.7 0.8 %score_products.3 = f32[8,128]{1,0:T(8,128)S(1)} custom-call(s16[4,40,768]{2,1,0:T(8,128)(2,1)S(1)} %collective-permute-done.17.found, f32[8,4,40,720]{3,2,1,0:T(8,128)S(1)} %copy-done, f32[8,4,40,720]{3,2,1,0:T(8,128)S(1)} %copy-done.1), custom_call_target="tpu_custom_call" | custom-call | flops 1000 | bytes 1000 | tf_op jit(solution)/shard_map/score_products/pallas_call | solution.py:355
  70.6 1.1 %collective-permute-start.20 = (f32[8,128]{1,0:T(8,128)S(1)}, f32[8,128]{1,0:T(8,128)S(1)}, u32[]{:S(2)}, u32[]{:S(2)}) collective-permute-start(f32[8,128]{1,0:T(8,128)S(1)} %add.53), channel_id=1, source_target_pairs={{0,3},{1,2},{2,1},{3,0},{4,7},{5,6},{6,5},{7,4},{8,11},{9,10},{10,... | collective-permute-start | bytes 12296 | tf_op jit(solution)/shard_map/ppermute | solution.py:417
  71.6 0.8 collective-permute-start.19
  72.4 0.1 collective-permute-start.18
  72.5 1.2 %output_rows.1 = f32[2,4,40,720]{3,2,1,0:T(8,128)} custom-call(s16[4,40,768]{2,1,0:T(8,128)(2,1)S(1)} %get-tuple-element.134.own_ref, s16[4,40,768]{2,1,0:T(8,128)(2,1)S(1)} %collective-permute-done.22.refs_0_), custom_call_target="tpu_custom_call" | custom-call | flops 1000 | bytes 1000 | tf_op jit(solution)/shard_map/output_rows/pallas_call | solution.py:377
  73.6 0.0 collective-permute-done.20
  73.6 1.6 %collective-permute-done.19 = f32[8,128]{1,0:T(8,128)S(1)} collective-permute-done((f32[8,128]{1,0:T(8,128)S(1)}, f32[8,128]{1,0:T(8,128)S(1)}, u32[]{:S(2)}, u32[]{:S(2)}) %collective-permute-start.19) | collective-permute-done | bytes 4128 | tf_op jit(solution)/shard_map/ppermute | solution.py:417
  75.2 0.0 collective-permute-done.18
  75.2 0.1 slice_reduce_fusion
  75.4 0.5 mul.56
  (21 shorter events, 0.2 us)
Async XLA Ops:
  0.6 19.7 %collective-permute-start.1 = (bf16[360,720]{1,0:T(8,128)(2,1)}, bf16[360,720]{1,0:T(8,128)(2,1)S(1)}, u32[]{:S(2)}, u32[]{:S(2)}) collective-permute-start(bf16[360,720]{1,0:T(8,128)(2,1)} %refs_2_), channel_id=1, source_target_pairs={{0,8},{4,12},{8,0},{12,4},{16,24},{20,28},{24,16},{28,20},{1,9},{5... | collective-permute-start | bytes 1555208 | tf_op jit(solution)/shard_map/ppermute | solution.py:414
  3.7 17.4 %collective-permute-start = (bf16[360,720]{1,0:T(8,128)(2,1)}, bf16[360,720]{1,0:T(8,128)(2,1)S(1)}, u32[]{:S(2)}, u32[]{:S(2)}) collective-permute-start(bf16[360,720]{1,0:T(8,128)(2,1)} %refs_2_), channel_id=1, source_target_pairs={{0,4},{4,0},{8,12},{12,8},{16,20},{20,16},{24,28},{28,24},{1,5},{5... | collective-permute-start | bytes 1555208 | tf_op jit(solution)/shard_map/ppermute | solution.py:414
  5.2 15.9 %collective-permute-start.2 = (bf16[360,720]{1,0:T(8,128)(2,1)}, bf16[360,720]{1,0:T(8,128)(2,1)S(1)}, u32[]{:S(2)}, u32[]{:S(2)}) collective-permute-start(bf16[360,720]{1,0:T(8,128)(2,1)} %refs_2_), channel_id=1, source_target_pairs={{0,1},{1,0},{2,3},{3,2},{4,5},{5,4},{6,7},{7,6},{8,9},{9,8},{10,11... | collective-permute-start | bytes 1555208 | tf_op jit(solution)/shard_map/ppermute | solution.py:417
  8.9 23.5 %all-to-all-start = ((s16[8,40,768]{2,1,0:T(8,128)(2,1)}), s16[8,40,768]{2,1,0:T(8,128)(2,1)S(1)}, u32[]{:S(2)}, u32[]{:S(2)}) async-start(s16[8,40,768]{2,1,0:T(8,128)(2,1)} %get-tuple-element.72), calls=%async_computation | async-start | bytes 983040 | tf_op jit(solution)/shard_map/all_to_all | solution.py:437
  21.1 9.5 %collective-permute-start.5 = (f32[40,720]{1,0:T(8,128)S(1)}, f32[40,720]{1,0:T(8,128)S(1)}, u32[]{:S(2)}, u32[]{:S(2)}) collective-permute-start(f32[40,720]{1,0:T(8,128)S(1)} %get-tuple-element.74), channel_id=1, source_target_pairs={{0,1},{1,0},{2,3},{3,2},{4,5},{5,4},{6,7},{7,6},{8,9},{9,8},{10,11... | collective-permute-start | bytes 345608 | tf_op jit(solution)/shard_map/ppermute | solution.py:417
  21.2 10.2 %collective-permute-start.4 = (bf16[168,720]{1,0:T(8,128)(2,1)S(1)}, bf16[168,720]{1,0:T(8,128)(2,1)S(1)}, u32[]{:S(2)}, u32[]{:S(2)}) collective-permute-start(bf16[168,720]{1,0:T(8,128)(2,1)S(1)} %slice.22), channel_id=1, source_target_pairs={{0,8},{4,12},{8,0},{12,4},{16,24},{20,28},{24,16},{28,20},{1,9},{5... | collective-permute-start | bytes 725768 | tf_op jit(solution)/shard_map/ppermute | solution.py:414
  22.6 15.6 %copy-start.2 = (bf16[360,720]{1,0:T(8,128)(2,1)S(1)}, bf16[360,720]{1,0:T(8,128)(2,1)}, u32[]{:S(2)}) copy-start(bf16[360,720]{1,0:T(8,128)(2,1)} %refs_2_) | copy-start | bytes 1555204
  22.6 9.8 %collective-permute-start.3 = (bf16[192,720]{1,0:T(8,128)(2,1)S(1)}, bf16[192,720]{1,0:T(8,128)(2,1)S(1)}, u32[]{:S(2)}, u32[]{:S(2)}) collective-permute-start(bf16[192,720]{1,0:T(8,128)(2,1)S(1)} %slice.21), channel_id=1, source_target_pairs={{0,4},{4,0},{8,12},{12,8},{16,20},{20,16},{24,28},{28,24},{1,5},{5... | collective-permute-start | bytes 829448 | tf_op jit(solution)/shard_map/ppermute | solution.py:414
  30.7 0.7 copy-start.3
  31.3 16.0 %copy-start.4 = (f32[40,720]{1,0:T(8,128)S(1)}, f32[40,720]{1,0:T(8,128)}, u32[]{:S(2)}) copy-start(f32[40,720]{1,0:T(8,128)} %copy-done.3) | copy-start | bytes 345604
  32.4 5.7 %collective-permute-start.6 = (bf16[360,720]{1,0:T(8,128)(2,1)S(1)}, bf16[360,720]{1,0:T(8,128)(2,1)S(1)}, u32[]{:S(2)}, u32[]{:S(2)}) collective-permute-start(bf16[360,720]{1,0:T(8,128)(2,1)S(1)} %collective-permute-done.refs_1_.refs_3_), channel_id=1, source_target_pairs={{0,1},{1,0},{2,3},{3,2},{4,5},{5,4},{6,7},{7,6},{8,9},{9,8},{10,11... | collective-permute-start | bytes 1555208 | tf_op jit(solution)/shard_map/ppermute | solution.py:417
  32.4 5.7 %collective-permute-start.7 = (bf16[360,720]{1,0:T(8,128)(2,1)S(1)}, bf16[360,720]{1,0:T(8,128)(2,1)S(1)}, u32[]{:S(2)}, u32[]{:S(2)}) collective-permute-start(bf16[360,720]{1,0:T(8,128)(2,1)S(1)} %collective-permute-done.1.refs_2_.refs_4_), channel_id=1, source_target_pairs={{0,1},{1,0},{2,3},{3,2},{4,5},{5,4},{6,7},{7,6},{8,9},{9,8},{10,11... | collective-permute-start | bytes 1555208 | tf_op jit(solution)/shard_map/ppermute | solution.py:417
  32.9 5.2 %collective-permute-start.8 = (bf16[192,720]{1,0:T(8,128)(2,1)S(1)}, bf16[192,720]{1,0:T(8,128)(2,1)S(1)}, u32[]{:S(2)}, u32[]{:S(2)}) collective-permute-start(bf16[192,720]{1,0:T(8,128)(2,1)S(1)} %collective-permute-done.3.refs_3_.refs_5_), channel_id=1, source_target_pairs={{0,1},{1,0},{2,3},{3,2},{4,5},{5,4},{6,7},{7,6},{8,9},{9,8},{10,11... | collective-permute-start | bytes 829448 | tf_op jit(solution)/shard_map/ppermute | solution.py:417
  32.9 5.2 %collective-permute-start.9 = (bf16[168,720]{1,0:T(8,128)(2,1)S(1)}, bf16[168,720]{1,0:T(8,128)(2,1)S(1)}, u32[]{:S(2)}, u32[]{:S(2)}) collective-permute-start(bf16[168,720]{1,0:T(8,128)(2,1)S(1)} %collective-permute-done.4.refs_4_.refs_6_), channel_id=1, source_target_pairs={{0,1},{1,0},{2,3},{3,2},{4,5},{5,4},{6,7},{7,6},{8,9},{9,8},{10,11... | collective-permute-start | bytes 725768 | tf_op jit(solution)/shard_map/ppermute | solution.py:417
  33.8 4.3 %collective-permute-start.10 = (s16[40,768]{1,0:T(8,128)(2,1)S(1)}, s16[40,768]{1,0:T(8,128)(2,1)S(1)}, u32[]{:S(2)}, u32[]{:S(2)}) collective-permute-start(s16[40,768]{1,0:T(8,128)(2,1)S(1)} %get-tuple-element.83), channel_id=1, source_target_pairs={{0,2},{1,3},{2,0},{3,1},{4,6},{5,7},{6,4},{7,5},{8,10},{9,11},{10,... | collective-permute-start | bytes 184328 | tf_op jit(solution)/shard_map/ppermute | solution.py:417
  38.2 23.5 %copy-start.1 = (f32[8,4,40,720]{3,2,1,0:T(8,128)S(1)}, f32[8,4,40,720]{3,2,1,0:T(8,128)}, u32[]{:S(2)}) copy-start(f32[8,4,40,720]{3,2,1,0:T(8,128)} %train_gradients.3.refs_1_) | copy-start | bytes 11059204
  39.4 22.4 %copy-start = (f32[8,4,40,720]{3,2,1,0:T(8,128)S(1)}, f32[8,4,40,720]{3,2,1,0:T(8,128)}, u32[]{:S(2)}) copy-start(f32[8,4,40,720]{3,2,1,0:T(8,128)} %train_gradients.2.refs_0_) | copy-start | bytes 11059204
  39.4 8.0 %collective-permute-start.11 = (s16[2,40,768]{2,1,0:T(8,128)(2,1)S(1)}, s16[2,40,768]{2,1,0:T(8,128)(2,1)S(1)}, u32[]{:S(2)}, u32[]{:S(2)}) collective-permute-start(s16[2,40,768]{2,1,0:T(8,128)(2,1)S(1)} %project.1.own_ref), channel_id=1, source_target_pairs={{0,16},{4,20},{8,24},{12,28},{16,0},{20,4},{24,8},{28,12},{1,17},{... | collective-permute-start | bytes 368648 | tf_op jit(solution)/shard_map/ppermute | solution.py:414
  49.3 4.3 %collective-permute-start.12 = (s16[40,768]{1,0:T(8,128)(2,1)S(1)}, s16[40,768]{1,0:T(8,128)(2,1)S(1)}, u32[]{:S(2)}, u32[]{:S(2)}) collective-permute-start(s16[40,768]{1,0:T(8,128)(2,1)S(1)} %get-tuple-element.105), channel_id=1, source_target_pairs={{0,2},{1,3},{2,0},{3,1},{4,6},{5,7},{6,4},{7,5},{8,10},{9,11},{10,... | collective-permute-start | bytes 184328 | tf_op jit(solution)/shard_map/ppermute | solution.py:417
  51.1 10.5 %collective-permute-start.16 = (s16[2,40,768]{2,1,0:T(8,128)(2,1)S(1)}, s16[2,40,768]{2,1,0:T(8,128)(2,1)S(1)}, u32[]{:S(2)}, u32[]{:S(2)}) collective-permute-start(s16[2,40,768]{2,1,0:T(8,128)(2,1)S(1)} %get-tuple-element.113), channel_id=1, source_target_pairs={{0,4},{4,0},{8,12},{12,8},{16,20},{20,16},{24,28},{28,24},{1,5},{5... | collective-permute-start | bytes 368648 | tf_op jit(solution)/shard_map/ppermute | solution.py:414
  53.9 6.4 %collective-permute-start.15 = (s16[40,768]{1,0:T(8,128)(2,1)S(1)}, s16[40,768]{1,0:T(8,128)(2,1)S(1)}, u32[]{:S(2)}, u32[]{:S(2)}) collective-permute-start(s16[40,768]{1,0:T(8,128)(2,1)S(1)} %select_convert_fusion), channel_id=1, source_target_pairs={{0,24},{4,28},{8,16},{12,20},{16,8},{20,12},{24,0},{28,4},{1,25},{... | collective-permute-start | bytes 184328 | tf_op jit(solution)/shard_map/ppermute | solution.py:414
  56.5 5.1 %collective-permute-start.14 = (s16[40,768]{1,0:T(8,128)(2,1)S(1)}, s16[40,768]{1,0:T(8,128)(2,1)S(1)}, u32[]{:S(2)}, u32[]{:S(2)}) collective-permute-start(s16[40,768]{1,0:T(8,128)(2,1)S(1)} %select_convert_fusion), channel_id=1, source_target_pairs={{0,16},{4,20},{8,24},{12,28},{16,0},{20,4},{24,8},{28,12},{1,17},{... | collective-permute-start | bytes 184328 | tf_op jit(solution)/shard_map/ppermute | solution.py:414
  56.5 5.1 %collective-permute-start.13 = (s16[40,768]{1,0:T(8,128)(2,1)S(1)}, s16[40,768]{1,0:T(8,128)(2,1)S(1)}, u32[]{:S(2)}, u32[]{:S(2)}) collective-permute-start(s16[40,768]{1,0:T(8,128)(2,1)S(1)} %select_convert_fusion), channel_id=1, source_target_pairs={{0,8},{4,12},{8,0},{12,4},{16,24},{20,28},{24,16},{28,20},{1,9},{5... | collective-permute-start | bytes 184328 | tf_op jit(solution)/shard_map/ppermute | solution.py:414
  61.7 7.2 %copy-start.5 = (s32[8]{0:T(128)S(1)}, s32[8]{0:T(128)}, u32[]{:S(2)}) copy-start(s32[8]{0:T(128)} %param.12) | copy-start | bytes 100
  62.6 6.2 %collective-permute-start.21 = (s16[2,2,40,768]{3,2,0,1:T(8,128)(2,1)S(1)}, s16[2,2,40,768]{3,2,0,1:T(8,128)(2,1)S(1)}, u32[]{:S(2)}, u32[]{:S(2)}) collective-permute-start(s16[2,2,40,768]{3,2,0,1:T(8,128)(2,1)S(1)} %pad_add_fusion.1), channel_id=1, source_target_pairs={{0,8},{4,12},{8,0},{12,4},{16,24},{20,28},{24,16},{28,20},{1,9},{5... | collective-permute-start | bytes 737288 | tf_op jit(solution)/shard_map/ppermute | solution.py:414
  63.5 6.2 %collective-permute-start.17 = (s16[4,40,768]{2,1,0:T(8,128)(2,1)S(1)}, s16[4,40,768]{2,1,0:T(8,128)(2,1)S(1)}, u32[]{:S(2)}, u32[]{:S(2)}) collective-permute-start(s16[4,40,768]{2,1,0:T(8,128)(2,1)S(1)} %pad_add_fusion.found), channel_id=1, source_target_pairs={{0,4},{4,0},{8,12},{12,8},{16,20},{20,16},{24,28},{28,24},{1,5},{5... | collective-permute-start | bytes 737288 | tf_op jit(solution)/shard_map/ppermute | solution.py:414
  68.8 3.6 %collective-permute-start.22 = (s16[4,40,768]{2,1,0:T(8,128)(2,1)S(1)}, s16[4,40,768]{2,1,0:T(8,128)(2,1)S(1)}, u32[]{:S(2)}, u32[]{:S(2)}) collective-permute-start(s16[4,40,768]{2,1,0:T(8,128)(2,1)S(1)} %get-tuple-element.133), channel_id=1, source_target_pairs={{0,1},{1,0},{2,3},{3,2},{4,5},{5,4},{6,7},{7,6},{8,9},{9,8},{10,11... | collective-permute-start | bytes 737288 | tf_op jit(solution)/shard_map/ppermute | solution.py:417
  70.6 3.1 %collective-permute-start.20 = (f32[8,128]{1,0:T(8,128)S(1)}, f32[8,128]{1,0:T(8,128)S(1)}, u32[]{:S(2)}, u32[]{:S(2)}) collective-permute-start(f32[8,128]{1,0:T(8,128)S(1)} %add.53), channel_id=1, source_target_pairs={{0,3},{1,2},{2,1},{3,0},{4,7},{5,6},{6,5},{7,4},{8,11},{9,10},{10,... | collective-permute-start | bytes 12296 | tf_op jit(solution)/shard_map/ppermute | solution.py:417
  71.6 3.6 %collective-permute-start.19 = (f32[8,128]{1,0:T(8,128)S(1)}, f32[8,128]{1,0:T(8,128)S(1)}, u32[]{:S(2)}, u32[]{:S(2)}) collective-permute-start(f32[8,128]{1,0:T(8,128)S(1)} %add.53), channel_id=1, source_target_pairs={{0,2},{1,3},{2,0},{3,1},{4,6},{5,7},{6,4},{7,5},{8,10},{9,11},{10,... | collective-permute-start | bytes 12296 | tf_op jit(solution)/shard_map/ppermute | solution.py:417
  72.4 2.9 %collective-permute-start.18 = (f32[8,128]{1,0:T(8,128)S(1)}, f32[8,128]{1,0:T(8,128)S(1)}, u32[]{:S(2)}, u32[]{:S(2)}) collective-permute-start(f32[8,128]{1,0:T(8,128)S(1)} %add.53), channel_id=1, source_target_pairs={{0,1},{1,0},{2,3},{3,2},{4,5},{5,4},{6,7},{7,6},{8,9},{9,8},{10,11... | collective-permute-start | bytes 12296 | tf_op jit(solution)/shard_map/ppermute | solution.py:417
